TPU v7x, 128 devices: a whole 4x4x4 slice. The times are simulated.
128 devices in a mesh: seq: 32 (over y_hi, x, z), tp: 4 (over y_lo, core).
Axes of the slice: x: 4, y: 4 (y_hi: 2, y_lo: 2; y = y_hi * 2 + y_lo), z: 4, core: 2. Of those that a mesh axis runs over, the one named last changes fastest.
Arguments:
- hidden_in: bfloat16 [8192, 4096], P('seq', 'tp'), may hold values from -6 to 6
- queries: bfloat16 [8192, 2048], P('seq', 'tp'), may hold values from -6 to 6
- keys: bfloat16 [8192, 2048], P('seq', 'tp'), may hold values from -6 to 6
- values: bfloat16 [8192, 2048], P('seq', 'tp'), may hold values from -6 to 6
- out_weight: bfloat16 [2048, 4096], P('tp'), may hold values from -0.125 to 0.125
- context_weight: bfloat16 [4096, 1024], P('tp'), may hold values from -0.1875 to 0.1875
- codes: int32 [8192, 4], P(('seq', 'tp')), may hold values from 0 to 1023
- table: bfloat16 [4, 1024, 1024], replicated, may hold values from -6 to 6
- depth_weights: bfloat16 [4, 1024, 1024], replicated, may hold values from -0.5 to 0.5
Outputs:
- losses: float32 [8192], P(('seq', 'tp'))
- grad_hidden: bfloat16 [8192, 4096], P('seq', 'tp')
All inputs are finite; a program needn't handle non-finite values.
Results may differ from a plain program's by a relative error of at most 0.034.
Values may be sent and summed in bfloat16 or wider, within the bound.
No kernel may reach another device: no remote copies, remote signals or barrier semaphores. Data moves between devices by JAX's collectives and lax.ppermute only.
A program may use at most 192 MiB of HBM per device.

v0:
```python
import functools
import itertools

import jax
import jax.numpy as jnp
from jax import lax
from jax.experimental import pallas as pl
from jax.experimental.pallas import tpu as pltpu
from jax.sharding import Mesh, PartitionSpec as P

HD = 128
DHEADS = 16
F32 = jnp.float32
BF16 = jnp.bfloat16
AXES = ("h", "x", "z", "l", "c")
SIZES = (2, 4, 4, 2, 2)
LOG2E = 1.4426950408889634
NEG = -1e30
VM = pl.BlockSpec(memory_space=pltpu.VMEM)
SM = pl.BlockSpec(memory_space=pltpu.SMEM)
ANY = pl.BlockSpec(memory_space=pl.ANY)


def flat(coords):
    number = 0
    for coord, size in zip(coords, SIZES):
        number = number * size + coord
    return number


def move(array, target):
    pairs = []
    for coords in itertools.product(*map(range, SIZES)):
        pairs.append((flat(coords), flat(target(*coords))))
    return lax.ppermute(array, AXES, pairs)


def other_core(h, x, z, l, c):
    return h, x, z, l, 1 - c


def x_up(h, x, z, l, c):
    return h, (x + 1) % 4, z, l, c


def z_by(n):
    return lambda h, x, z, l, c: (h, x, (z + n) % 4, l, c)


def x_down(h, x, z, l, c):
    return h, (x + 3) % 4, z, l, c


def l_swap(h, x, z, l, c):
    return h, x, z, 1 - l, c


def lc_swap(h, x, z, l, c):
    return h, x, z, 1 - l, 1 - c


def call(body, out_shape, in_specs, *args, after=(), scratch=(), limit=16, flops=0, nbytes=0, aliases=None, out_specs=None):
    if out_specs is None:
        out_specs = jax.tree.map(lambda _: VM, out_shape)
    reads = len(args)

    def run(*refs):
        body(*refs[:reads], *refs[reads + len(after) :])

    args = args + tuple(after)
    in_specs = in_specs + [ANY] * len(after)
    return pl.pallas_call(
        run,
        out_shape=out_shape,
        in_specs=in_specs,
        out_specs=out_specs,
        scratch_shapes=list(scratch),
        input_output_aliases=aliases or {},
        compiler_params=pltpu.CompilerParams(vmem_limit_bytes=limit * 1024 * 1024),
        cost_estimate=pl.CostEstimate(flops=flops, bytes_accessed=nbytes, transcendentals=0),
    )(*args)


def shape(*dims, dtype=BF16):
    return jax.ShapeDtypeStruct(dims, dtype)


def dot_nn(a, b):
    return lax.dot_general(a, b, (((1,), (0,)), ((), ())), preferred_element_type=F32)


def dot_nt(a, b):
    return lax.dot_general(a, b, (((1,), (1,)), ((), ())), preferred_element_type=F32)


def dot_tn(a, b):
    return lax.dot_general(a, b, (((0,), (0,)), ((), ())), preferred_element_type=F32)


def split_rows_body(ids, q_hbm, k_hbm, v_hbm, w_hbm, keep_ref, send_ref, cols_ref, local, sems):
    c = ids[4]
    copies = [pltpu.make_async_copy(ref, local.at[n], sems.at[n]) for n, ref in enumerate((q_hbm, k_hbm, v_hbm))]
    cols = pl.ds(pl.multiple_of(ids[2] * 256, 256), 256)
    copies.append(pltpu.make_async_copy(w_hbm.at[:, cols], cols_ref, sems.at[3]))
    for copy in copies:
        copy.start()
    for part in range(3):
        copies[part].wait()
        for half in range(2):
            mine = pl.ds(pl.multiple_of(half * 128 + c * 64, 64), 64)
            theirs = pl.ds(pl.multiple_of(half * 128 + (1 - c) * 64, 64), 64)
            for head in range(4):
                cols = slice(head * 128, head * 128 + 128)
                to = slice(part * 128, part * 128 + 128)
                keep_ref[c * 4 + head, half * 64 : half * 64 + 64, to] = local[part, mine, cols]
                send_ref[head, half * 64 : half * 64 + 64, to] = local[part, theirs, cols]
    copies[3].wait()


def attend(state, q, keys, vals, start, mask=None):
    acc_ref, m_ref, l_ref = state
    cols = slice(start, start + 512)
    s = dot_nt(keys, q) * (LOG2E / HD**0.5)
    if mask is not None:
        s = jnp.where(mask, s, NEG)
    old = m_ref[:, cols]
    new = jnp.maximum(old, jnp.max(s, 0, keepdims=True))
    p = jnp.exp2(s - new)
    alpha = jnp.exp2(old - new)
    m_ref[:, cols] = new
    l_ref[:, cols] = l_ref[:, cols] * alpha + jnp.sum(p, 0, keepdims=True)
    acc_ref[:, cols] = acc_ref[:, cols] * alpha + dot_tn(vals, p.astype(BF16))


def rows_of(ref, first, col):
    return ref[first : first + 4, :, col : col + 128].reshape(512, 128)


def take_rows_body(r_ref, lo_ref, hi_ref, q_ref):
    q_ref[...] = r_ref[:, :, 0:128]
    lo_ref[...] = r_ref[0:4, :, 128:384]
    hi_ref[...] = r_ref[4:8, :, 128:384]


def own_block_body(ids, q_ref, q_o_ref, lo_ref, hi_ref, acc_ref, m_ref, l_ref):
    state = (acc_ref, m_ref, l_ref)
    c = ids[4]
    m_ref[...] = jnp.full_like(m_ref, 0.1 * NEG)
    l_ref[...] = jnp.zeros_like(l_ref)
    acc_ref[...] = jnp.zeros_like(acc_ref)
    key_row = lax.broadcasted_iota(jnp.int32, (512, 512), 0)
    q_row = lax.broadcasted_iota(jnp.int32, (512, 512), 1)
    place = lambda row, core: (row // 64) * 128 + core * 64 + row % 64
    key_place = place(key_row, c)
    for section, (ref, core) in enumerate(((q_ref, c), (q_o_ref, 1 - c))):
        mask = key_place <= place(q_row, core)
        for h, kv in enumerate((lo_ref, hi_ref)):
            q = rows_of(ref, h * 4, 0)
            attend(state, q, rows_of(kv, 0, 0), rows_of(kv, 0, 128), h * 1024 + section * 512, mask)
        attend(state, q, rows_of(lo_ref, 0, 0), rows_of(lo_ref, 0, 128), 1024 + section * 512)


def block_steps(state, qs, low, high, earlier):
    for section, ref in enumerate(qs):
        attend(state, rows_of(ref, 4, 0), rows_of(low, 0, 0), rows_of(low, 0, 128), 1024 + section * 512)

    @pl.when(earlier)
    def _():
        for section, ref in enumerate(qs):
            attend(state, rows_of(ref, 0, 0), rows_of(low, 0, 0), rows_of(low, 0, 128), section * 512)
            attend(state, rows_of(ref, 4, 0), rows_of(high, 0, 0), rows_of(high, 0, 128), 1024 + section * 512)


def near_blocks_body(
    ids, q_ref, q_o_ref, up_lo, up_hi, down_lo, down_hi, acc_in, m_in, l_in, acc_ref, m_ref, l_ref
):
    acc_ref[...] = acc_in[...]
    m_ref[...] = m_in[...]
    l_ref[...] = l_in[...]
    state = (acc_ref, m_ref, l_ref)
    x = ids[1]
    block_steps(state, (q_ref, q_o_ref), up_lo, up_hi, x > 0)
    block_steps(state, (q_ref, q_o_ref), down_lo, down_hi, x == 3)


def far_block_body(ids, q_ref, q_o_ref, lo, hi, acc_in, m_in, l_in, own_ref, send_ref, own_stat, send_stat, acc_ref, m_ref, l_ref):
    acc_ref[...] = acc_in[...]
    m_ref[...] = m_in[...]
    l_ref[...] = l_in[...]
    state = (acc_ref, m_ref, l_ref)
    block_steps(state, (q_ref, q_o_ref), lo, hi, ids[1] >= 2)
    for section, (ref, stat) in enumerate(((own_ref, own_stat), (send_ref, send_stat))):
        for h in range(2):
            cols = slice(h * 1024 + section * 512, h * 1024 + section * 512 + 512)
            to = slice(h * 512, h * 512 + 512)
            total = l_ref[:, cols]
            ref[:, to] = (acc_ref[:, cols] / jnp.maximum(total, 0.5)).astype(ref.dtype)
            stat[0:1, to] = m_ref[:, cols]
            stat[1:2, to] = total


def join_cores_body(own_ref, recv_ref, own_stat, recv_stat, out_ref):
    m1, l1 = own_stat[0:1, :], own_stat[1:2, :]
    m2, l2 = recv_stat[0:1, :], recv_stat[1:2, :]
    top = jnp.maximum(m1, m2)
    w1 = l1 * jnp.exp2(m1 - top)
    w2 = l2 * jnp.exp2(m2 - top)
    share = 1.0 / (w1 + w2)
    joined = own_ref[...] * (w1 * share) + recv_ref[...].astype(F32) * (w2 * share)
    out_ref[...] = joined.T.astype(BF16).reshape(8, 128, 128)


def merged_weight_body(ids, ow_ref, b00, b01, b10, b11, out_ref):
    l, c = ids[3], ids[4]
    total = None
    for dl, dc, ref in ((0, 0, b00), (0, 1, b01), (1, 0, b10), (1, 1, b11)):
        t = jnp.where(dl == 1, 1 - l, l) * 2 + jnp.where(dc == 1, 1 - c, c)
        part = dot_nn(ow_ref[:, pl.ds(pl.multiple_of(t * 1024, 1024), 1024)], ref[...])
        total = part if total is None else total + part
    out_ref[...] = total.astype(BF16)


def hidden_part_body(ids, hid_ref, cw_ref, own_ref, send_ref, out):
    c = ids[4]
    out[...] = dot_nn(hid_ref[...], cw_ref[...])
    for half in range(2):
        rows = slice(half * 64, half * 64 + 64)
        own_ref[rows, :] = out[pl.ds(pl.multiple_of(half * 128 + c * 64, 64), 64), :]
        send_ref[rows, :] = out[pl.ds(pl.multiple_of(half * 128 + (1 - c) * 64, 64), 64), :].astype(BF16)


def embed_body(codes_ref, table_ref, out_ref):
    vocab = lax.broadcasted_iota(jnp.int32, (64, 1024), 1)
    for n in range(3):
        hit = (vocab == codes_ref[:, n : n + 1]).astype(BF16)
        out_ref[n] = dot_nn(hit, table_ref[n]).astype(BF16)


def relay_body(lo_in, hi_in, w_in, lo_ref, hi_ref, w_ref):
    lo_ref[...] = lo_in[...]
    hi_ref[...] = hi_in[...]
    w_ref[...] = w_in[...]


def pack_body(*refs):
    for n in range(4):
        refs[4][n] = refs[n][...]


def project_body(ids, att_ref, w_ref, wo_ref, h_own_ref, h_recv_ref, own_ref, send_ref, out):
    z, l, c = ids[2], ids[3], ids[4]
    a_own = att_ref[pl.ds(c * 4, 4)]
    a_oth = att_ref[pl.ds((1 - c) * 4, 4)]
    a_own = jnp.concatenate([a_own[i] for i in range(4)], 1)
    a_oth = jnp.concatenate([a_oth[i] for i in range(4)], 1)
    for dz in range(4):
        col = pl.multiple_of(((z + 4 - dz) % 4) * 256, 256)
        out[:, pl.ds(col, 256)] = dot_nn(a_own, w_ref[dz]) + dot_nn(a_oth, wo_ref[dz])
    out[...] += h_own_ref[...] + h_recv_ref[...].astype(F32)
    own_ref[...] = out[pl.ds(pl.multiple_of(l * 64, 64), 64), :]
    send_ref[...] = out[pl.ds(pl.multiple_of((1 - l) * 64, 64), 64), :].astype(BF16)


def rms(stream):
    return lax.rsqrt(jnp.mean(stream * stream, -1, keepdims=True) + 1e-05)


def split_dot(a, b):
    high = a.astype(BF16)
    low = (a - high.astype(F32)).astype(BF16)
    return dot_nn(high, b) + dot_nn(low, b)


def depth_body(
    own_ref, recv_ref, embed_ref, codes_ref, wt_hbm, tab_hbm, loss_ref, dctx_ref, wt, tab, sems,
):
    copies = [pltpu.make_async_copy(wt_hbm.at[i], wt.at[i], sems.at[i]) for i in range(4)]
    copies += [pltpu.make_async_copy(tab_hbm.at[i], tab.at[i], sems.at[4 + i]) for i in range(4)]
    copies[0].start()
    copies[1].start()
    copies[2].start()
    n = 64
    context = own_ref[...] + recv_ref[...].astype(F32)
    stream = jnp.concatenate([context] + [context + embed_ref[i].astype(F32) for i in range(3)], 0)
    r1 = rms(stream)
    normed = (stream * r1).astype(BF16)
    qkv = []
    for i in range(3):
        copies[i].wait()
        copies[3 + i].start()
        qkv.append(dot_nn(normed, wt[i]))
    q, k, v = qkv
    at = lambda a, i: a[i * n : (i + 1) * n]
    pairs = [(i, j) for i in range(4) for j in range(i + 1)]
    lane = lax.broadcasted_iota(jnp.int32, (1024, 128), 0) // 64
    head = lax.broadcasted_iota(jnp.int32, (1024, 128), 1)
    gather_heads = (lane == head).astype(BF16)
    head_t = lax.broadcasted_iota(jnp.int32, (128, 1024), 0)
    lane_t = lax.broadcasted_iota(jnp.int32, (128, 1024), 1) // 64
    spread_heads = (lane_t == head_t).astype(BF16)
    prod = jnp.concatenate([at(q, i) * at(k, j) for i, j in pairs], 0)
    scores = split_dot(prod, gather_heads) * 0.125
    score = {pair: at(scores, number) for number, pair in enumerate(pairs)}
    weight = {}
    for i in range(4):
        top = functools.reduce(jnp.maximum, [score[i, j] for j in range(i + 1)])
        es = [jnp.exp(score[i, j] - top) for j in range(i + 1)]
        total = functools.reduce(jnp.add, es)
        for j in range(i + 1):
            weight[i, j] = es[j] / total
    spread = dot_nn(jnp.concatenate([weight[p] for p in pairs], 0).astype(BF16), spread_heads)
    wide = {pair: at(spread, number) for number, pair in enumerate(pairs)}
    mixed = jnp.concatenate(
        [functools.reduce(jnp.add, [wide[i, j] * at(v, j) for j in range(i + 1)]) for i in range(4)], 0
    ).astype(BF16)
    copies[3].wait()
    copies[6].start()
    update = dot_nn(mixed, wt[3])
    out = stream + update
    r2 = rms(out)
    final = (out * r2).astype(BF16)
    loss = jnp.zeros((n, 1), F32)
    dfinal = []
    scale = 3.0 / 1024**0.5
    vocab = lax.broadcasted_iota(jnp.int32, (n, 1024), 1)
    for i in range(4):
        copies[4 + i].wait()
        if i == 0:
            copies[7].start()
        logits = dot_nt(at(final, i), tab[i]) * scale
        top = jnp.max(logits, -1, keepdims=True)
        e = jnp.exp(logits - top)
        total = jnp.sum(e, -1, keepdims=True)
        hit = vocab == codes_ref[:, i : i + 1]
        picked = jnp.sum(jnp.where(hit, logits, 0.0), -1, keepdims=True)
        loss = loss + top + jnp.log(total) - picked
        dlogits = (e / total - hit.astype(F32)).astype(BF16)
        dfinal.append(dot_nn(dlogits, tab[i]) * scale)
    loss_ref[...] = jnp.broadcast_to(loss, (n, 128))
    dfinal = jnp.concatenate(dfinal, 0)
    dout = r2 * (dfinal - out * (r2 * r2) * jnp.mean(dfinal * out, -1, keepdims=True))
    dmixed = dot_nt(dout.astype(BF16), wt[3])
    dprod = jnp.concatenate([at(dmixed, i) * at(v, j) for i, j in pairs], 0)
    dweights = split_dot(dprod, gather_heads)
    dweight = {pair: at(dweights, number) for number, pair in enumerate(pairs)}
    dscore = []
    for i in range(4):
        mean = functools.reduce(jnp.add, [weight[i, j] * dweight[i, j] for j in range(i + 1)])
        for j in range(i + 1):
            dscore.append(weight[i, j] * (dweight[i, j] - mean) * 0.125)
    spread = dot_nn(jnp.concatenate(dscore, 0).astype(BF16), spread_heads)
    dwide = {pair: at(spread, number) for number, pair in enumerate(pairs)}
    add = lambda terms: functools.reduce(jnp.add, terms)
    dq = jnp.concatenate([add([dwide[i, j] * at(k, j) for j in range(i + 1)]) for i in range(4)], 0)
    dk = jnp.concatenate([add([dwide[i, j] * at(q, i) for i in range(j, 4)]) for j in range(4)], 0)
    dv = jnp.concatenate([add([wide[i, j] * at(dmixed, i) for i in range(j, 4)]) for j in range(4)], 0)
    dnormed = dot_nt(dq.astype(BF16), wt[0]) + dot_nt(dk.astype(BF16), wt[1]) + dot_nt(dv.astype(BF16), wt[2])
    dstream = dout + r1 * (dnormed - stream * (r1 * r1) * jnp.mean(dnormed * stream, -1, keepdims=True))
    dctx_ref[...] = add([at(dstream, i) for i in range(4)]).astype(BF16)


def grad_body(ids, d0, d1, d2, d3, cw_ref, out_ref, rows):
    l, c = ids[3], ids[4]
    for dl, dc, ref in ((0, 0, d0), (0, 1, d1), (1, 0, d2), (1, 1, d3)):
        t = jnp.where(dl == 1, 1 - l, l) * 2 + jnp.where(dc == 1, 1 - c, c)
        rows[pl.ds(pl.multiple_of(t * 64, 64), 64), :] = ref[...]
    out_ref[...] = dot_nt(rows[...], cw_ref[...]).astype(BF16)


def per_device(hidden_in, queries, keys, values, out_weight, context_weight, codes, table, depth_weights):
    coords = [lax.axis_index(name) for name in AXES]
    h, x, z, l, c = coords
    ids = jnp.stack(coords).astype(jnp.int32)

    keep, send, cw_cols = call(
        split_rows_body, (shape(8, 128, 384), shape(4, 128, 384), shape(1024, 256)), [SM] + [ANY] * 4,
        ids, queries, keys, values, context_weight,
        scratch=[pltpu.VMEM((3, 256, 512), BF16), pltpu.SemaphoreType.DMA((4,))], limit=60, nbytes=3 << 20,
    )
    full = lax.dynamic_update_slice(keep, move(send, other_core), ((1 - c) * 4, 0, 0))
    mine = lax.all_to_all(full, ("h", "z"), 0, 0, tiled=True)

    cw_l = move(cw_cols, l_swap)
    cw_c = move(cw_cols, other_core)
    cw_lc = move(cw_l, other_core)
    h_own, h_send = call(
        hidden_part_body, (shape(128, 1024, dtype=F32), shape(128, 1024)), [SM] + [VM] * 2,
        ids, hidden_in, context_weight, scratch=[pltpu.VMEM((256, 1024), F32)], flops=1 << 29, nbytes=3 << 20,
    )
    merged = call(
        merged_weight_body, shape(512, 256), [SM] + [VM] * 5, ids, out_weight, cw_cols, cw_c, cw_l, cw_lc,
        flops=1 << 30, nbytes=6 << 20,
    )
    half = shape(4, 128, 256)
    low, high, q = call(
        take_rows_body, (half, half, shape(8, 128, 128)), [VM], mine, after=(h_own, merged), nbytes=1 << 20
    )
    up_lo, down_hi = move(low, x_up), move(high, x_down)
    q_o = move(q, other_core)
    up_hi, down_lo = move(high, x_up), move(low, x_down)
    stats = (shape(128, 2048, dtype=F32), shape(1, 2048, dtype=F32), shape(1, 2048, dtype=F32))
    carry = call(own_block_body, stats, [SM] + [VM] * 4, ids, q, q_o, low, high, flops=4 << 30, nbytes=2 << 20)
    relay_lo, relay_hi, merged = call(
        relay_body, (half, half, shape(512, 256)), [VM] * 3, up_lo, down_hi, merged, after=carry[1:2], nbytes=1 << 20
    )
    far_lo, far_hi = move(relay_lo, x_up), move(relay_hi, x_down)
    carry = call(
        near_blocks_body, stats, [SM] + [VM] * 9, ids, q, q_o, up_lo, up_hi, down_lo, down_hi, *carry,
        aliases={7: 0, 8: 1, 9: 2}, flops=4 << 30, nbytes=4 << 20,
    )
    pieces = [merged] + [move(merged, z_by(n)) for n in (1, 2, 3)]
    h_recv = move(h_send, other_core)
    own, send, own_stat, send_stat = call(
        far_block_body,
        (shape(128, 1024, dtype=F32), shape(128, 1024), shape(8, 1024, dtype=F32), shape(8, 1024, dtype=F32)),
        [SM] + [VM] * 7, ids, q, q_o, far_lo, far_hi, *carry,
        scratch=[pltpu.VMEM(s.shape, s.dtype) for s in stats], flops=3 << 30, nbytes=3 << 20,
    )
    attended = call(
        join_cores_body, shape(8, 128, 128), [VM] * 4,
        own, move(send, other_core), own_stat, move(send_stat, other_core), nbytes=1 << 20,
    )
    merged = call(pack_body, shape(4, 512, 256), [VM] * 4, *pieces, after=(own_stat,), nbytes=2 << 20)
    merged_o = move(merged, other_core)
    embedded = call(
        embed_body, shape(3, 64, 1024), [VM] * 2, codes, table, after=(own_stat,), flops=3 << 27, nbytes=8 << 20,
    )
    attended = lax.all_to_all(attended, ("h", "z"), 0, 0, tiled=True)

    own, send = call(
        project_body, (shape(64, 1024, dtype=F32), shape(64, 1024)), [SM] + [VM] * 5,
        ids, attended, merged, merged_o, h_own, h_recv, after=(embedded,),
        scratch=[pltpu.VMEM((128, 1024), F32)], flops=1 << 28, nbytes=3 << 20,
    )
    recv = move(send, l_swap)
    losses, dcontext = call(
        depth_body, (shape(64, 128, dtype=F32), shape(64, 1024)), [VM] * 4 + [ANY] * 2,
        own, recv, embedded, codes, depth_weights, table,
        scratch=[pltpu.VMEM((4, 1024, 1024), BF16), pltpu.VMEM((4, 1024, 1024), BF16), pltpu.SemaphoreType.DMA((8,))],
        limit=58, flops=12 << 30, nbytes=17 << 20,
    )
    grad = call(
        grad_body, shape(256, 1024), [SM] + [VM] * 5, ids,
        dcontext, move(dcontext, other_core), move(dcontext, l_swap), move(dcontext, lc_swap), context_weight,
        scratch=[pltpu.VMEM((256, 1024), BF16)], flops=1 << 29, nbytes=3 << 20,
    )
    return losses[:, 0], grad


def solution(mesh):
    fine = Mesh(mesh.devices.reshape(SIZES), AXES)
    seq, tp = AXES[:3], AXES[3:]
    return jax.shard_map(
        per_device,
        mesh=fine,
        in_specs=(
            P(seq, tp), P(seq, tp), P(seq, tp), P(seq, tp), P(tp, None), P(tp, None), P(seq + tp, None), P(), P(),
        ),
        out_specs=(P(seq + tp), P(seq, tp)),
        check_vma=False,
    )
```

profile of v0, /device:TPU:7, one launch (start us, length us, event | category | flops | bytes accessed | tf_op | source)
XLA Modules:
  0.0 124.8 jit_solution(14616103592862966051)
XLA Ops:
  0.6 0.7 stack.23.refs_0_
  1.3 3.3 %shard_map.104 = (bf16[8,128,384]{2,1,0:T(8,128)(2,1)}, bf16[4,128,384]{2,1,0:T(8,128)(2,1)}, bf16[1024,256]{1,0:T(8,128)(2,1)}) custom-call(s32[5]{0:T(128)} %stack.23.refs_0_, bf16[256,512]{1,0:T(8,128)(2,1)} %refs_1_.4, bf16[256,512]{1,0:T(8,128)(2,1)} %refs_2_.2, bf16[256,512]{1,0:T(8,128)(2,1)} %refs_3_.2, bf16[1024,1024]{1,0:T(8,128)(2,1)} %refs_5_.3), custom_call_target="tpu_custom_call" | custom-call | bytes 3145728 | tf_op jit(solution)/shard_map/pallas_call | solution.py:72
  4.6 0.8 collective-permute-start
  5.4 1.3 %collective-permute-start.2 = (bf16[1024,256]{1,0:T(8,128)(2,1)}, bf16[1024,256]{1,0:T(8,128)(2,1)S(1)}, u32[]{:S(2)}, u32[]{:S(2)}) collective-permute-start(bf16[1024,256]{1,0:T(8,128)(2,1)} %get-tuple-element.30.refs_2_), channel_id=1, source_target_pairs={{0,2},{1,3},{2,0},{3,1},{4,6},{5,7},{6,4},{7,5},{8,10},{9,11},{10,... | collective-permute-start | bytes 1572872 | tf_op jit(solution)/shard_map/ppermute | solution.py:35
  6.9 0.8 constant_dynamic-update-slice_fusion
  7.7 7.7 %all-to-all-start = ((bf16[8,128,384]{2,1,0:T(8,128)(2,1)}), bf16[8,128,384]{2,1,0:T(8,128)(2,1)S(1)}, u32[]{:S(2)}, u32[]{:S(2)}) async-start(bf16[8,128,384]{2,1,0:T(8,128)(2,1)} %constant_dynamic-update-slice_fusion), calls=%async_computation | async-start | bytes 1572864 | tf_op jit(solution)/shard_map/all_to_all | solution.py:381
  15.4 0.7 collective-permute-start.1
  16.0 3.0 %collective-permute-done.2.refs_4_ = bf16[1024,256]{1,0:T(8,128)(2,1)S(1)} collective-permute-done((bf16[1024,256]{1,0:T(8,128)(2,1)}, bf16[1024,256]{1,0:T(8,128)(2,1)S(1)}, u32[]{:S(2)}, u32[]{:S(2)}) %collective-permute-start.2) | collective-permute-done | bytes 524320 | tf_op jit(solution)/shard_map/ppermute | solution.py:35
  19.1 1.3 %collective-permute-start.3 = (bf16[1024,256]{1,0:T(8,128)(2,1)S(1)}, bf16[1024,256]{1,0:T(8,128)(2,1)S(1)}, u32[]{:S(2)}, u32[]{:S(2)}) collective-permute-start(bf16[1024,256]{1,0:T(8,128)(2,1)S(1)} %collective-permute-done.2.refs_4_), channel_id=1, source_target_pairs={{0,1},{1,0},{2,3},{3,2},{4,5},{5,4},{6,7},{7,6},{8,9},{9,8},{10,11... | collective-permute-start | bytes 1572872 | tf_op jit(solution)/shard_map/ppermute | solution.py:35
  20.4 1.6 %copy-done = bf16[1024,1024]{1,0:T(8,128)(2,1)S(1)} copy-done((bf16[1024,1024]{1,0:T(8,128)(2,1)S(1)}, bf16[1024,1024]{1,0:T(8,128)(2,1)}, u32[]{:S(2)}) %copy-start) | copy-done | bytes 2097176
  22.0 1.0 copy-done.5
  23.0 0.7 copy-done.9
  23.7 2.0 %shard_map.105 = (f32[128,1024]{1,0:T(8,128)S(1)}, bf16[128,1024]{1,0:T(8,128)(2,1)}) custom-call(s32[5]{0:T(128)S(1)} %copy-done.9, bf16[256,1024]{1,0:T(8,128)(2,1)S(1)} %copy-done.5, bf16[1024,1024]{1,0:T(8,128)(2,1)S(1)} %copy-done), custom_call_target="tpu_custom_call" | custom-call | flops 536870912 | bytes 3145728 | tf_op jit(solution)/shard_map/pallas_call | solution.py:72
  25.7 2.2 %copy-done.3 = bf16[512,4096]{1,0:T(8,128)(2,1)S(1)} copy-done((bf16[512,4096]{1,0:T(8,128)(2,1)S(1)}, bf16[512,4096]{1,0:T(8,128)(2,1)}, u32[]{:S(2)}) %copy-start.3) | copy-done | bytes 4194328
  27.9 1.0 copy-done.6
  29.0 1.8 %shard_map.106.refs_2_ = bf16[512,256]{1,0:T(8,128)(2,1)S(1)} custom-call(s32[5]{0:T(128)S(1)} %copy-done.9, bf16[512,4096]{1,0:T(8,128)(2,1)S(1)} %copy-done.3, bf16[1024,256]{1,0:T(8,128)(2,1)S(1)} %copy-done.6, bf16[1024,256]{1,0:T(8,128)(2,1)S(1)} %collective-permute-done.1.refs_3_, bf16[1024,256]{1,0:T(8,128)(2,1)S(1)} %collective-permute-done.2.refs_4_, ...), custom_call_target="tpu_custom_call" | custom-call | flops 1073741824 | bytes 6291456 | tf_op jit(solution)/shard_map/pallas_call | solution.py:72
  30.8 0.5 all-to-all-done.refs_0_
  31.4 1.4 %collective-permute-start.4 = (bf16[8,128,128]{2,1,0:T(8,128)(2,1)S(1)}, bf16[8,128,128]{2,1,0:T(8,128)(2,1)S(1)}, u32[]{:S(2)}, u32[]{:S(2)}) collective-permute-start(bf16[8,128,128]{2,1,0:T(8,128)(2,1)S(1)} %get-tuple-element.31.refs_1_), channel_id=1, source_target_pairs={{0,1},{1,0},{2,3},{3,2},{4,5},{5,4},{6,7},{7,6},{8,9},{9,8},{10,11... | collective-permute-start | bytes 786440 | tf_op jit(solution)/shard_map/ppermute | solution.py:35
  33.0 1.3 %collective-permute-start.10 = (bf16[4,128,256]{2,1,0:T(8,128)(2,1)S(1)}, bf16[4,128,256]{2,1,0:T(8,128)(2,1)S(1)}, u32[]{:S(2)}, u32[]{:S(2)}) collective-permute-start(bf16[4,128,256]{2,1,0:T(8,128)(2,1)S(1)} %get-tuple-element.32.refs_3_), channel_id=1, source_target_pairs={{0,48},{1,49},{2,50},{3,51},{4,52},{5,53},{6,54},{7,55},{8,56},{9,... | collective-permute-start | bytes 786440 | tf_op jit(solution)/shard_map/ppermute | solution.py:35
  34.3 0.5 collective-permute-start.6
  34.8 2.1 %collective-permute-start.9 = (bf16[4,128,256]{2,1,0:T(8,128)(2,1)S(1)}, bf16[4,128,256]{2,1,0:T(8,128)(2,1)S(1)}, u32[]{:S(2)}, u32[]{:S(2)}) collective-permute-start(bf16[4,128,256]{2,1,0:T(8,128)(2,1)S(1)} %get-tuple-element.33.refs_4_), channel_id=1, source_target_pairs={{0,16},{1,17},{2,18},{3,19},{4,20},{5,21},{6,22},{7,23},{8,24},{9,... | collective-permute-start | bytes 786440 | tf_op jit(solution)/shard_map/ppermute | solution.py:35
  37.0 3.8 %shard_map.108 = (f32[128,2048]{1,0:T(8,128)S(1)}, f32[1,2048]{1,0:T(1,128)S(1)}, f32[1,2048]{1,0:T(1,128)S(1)}) custom-call(s32[5]{0:T(128)S(1)} %copy-done.10, bf16[8,128,128]{2,1,0:T(8,128)(2,1)S(1)} %get-tuple-element.31.refs_1_, bf16[8,128,128]{2,1,0:T(8,128)(2,1)S(1)} %collective-permute-done.4.refs_2_, ...), custom_call_target="tpu_custom_call" | custom-call | flops 4294967296 | bytes 2097152 | tf_op jit(solution)/shard_map/pallas_call | solution.py:72
  40.8 6.6 %collective-permute-done.6.refs_1_.refs_6_ = bf16[4,128,256]{2,1,0:T(8,128)(2,1)S(1)} collective-permute-done((bf16[4,128,256]{2,1,0:T(8,128)(2,1)S(1)}, bf16[4,128,256]{2,1,0:T(8,128)(2,1)S(1)}, u32[]{:S(2)}, u32[]{:S(2)}) %collective-permute-start.6) | collective-permute-done | bytes 262176 | tf_op jit(solution)/shard_map/ppermute | solution.py:35
  47.5 2.7 %collective-permute-start.14 = (bf16[512,256]{1,0:T(8,128)(2,1)S(1)}, bf16[512,256]{1,0:T(8,128)(2,1)S(1)}, u32[]{:S(2)}, u32[]{:S(2)}) collective-permute-start(bf16[512,256]{1,0:T(8,128)(2,1)S(1)} %get-tuple-element.46.refs_0_), channel_id=1, source_target_pairs={{0,8},{1,9},{2,10},{3,11},{4,12},{5,13},{6,14},{7,15},{8,0},{9,1},... | collective-permute-start | bytes 786440 | tf_op jit(solution)/shard_map/ppermute | solution.py:35
  50.3 0.7 collective-permute-start.15
  51.0 1.5 %collective-permute-start.8 = (bf16[4,128,256]{2,1,0:T(8,128)(2,1)S(1)}, bf16[4,128,256]{2,1,0:T(8,128)(2,1)S(1)}, u32[]{:S(2)}, u32[]{:S(2)}) collective-permute-start(bf16[4,128,256]{2,1,0:T(8,128)(2,1)S(1)} %get-tuple-element.36), channel_id=1, source_target_pairs={{0,48},{1,49},{2,50},{3,51},{4,52},{5,53},{6,54},{7,55},{8,56},{9,... | collective-permute-start | bytes 786440 | tf_op jit(solution)/shard_map/ppermute | solution.py:35
  52.5 7.8 %shard_map.110 = (f32[128,2048]{1,0:T(8,128)S(1)}, f32[1,2048]{1,0:T(1,128)S(1)}, f32[1,2048]{1,0:T(1,128)S(1)}) custom-call(s32[5]{0:T(128)S(1)} %copy-done.10, bf16[8,128,128]{2,1,0:T(8,128)(2,1)S(1)} %get-tuple-element.31.refs_1_, ...), custom_call_target="tpu_custom_call", output_to_operand_aliasing={{0}: (7, {}), {1}: (8, {}), {2}: (9, {})} | custom-call | flops 4294967296 | bytes 4194304 | tf_op jit(solution)/shard_map/pallas_call | solution.py:72
  60.3 4.2 %shard_map.111 = (f32[128,1024]{1,0:T(8,128)S(1)}, bf16[128,1024]{1,0:T(8,128)(2,1)S(1)}, f32[8,1024]{1,0:T(8,128)S(1)}, f32[8,1024]{1,0:T(8,128)S(1)}) custom-call(s32[5]{0:T(128)S(1)} %copy-done.10, bf16[8,128,128]{2,1,0:T(8,128)(2,1)S(1)} %get-tuple-element.31.refs_1_, bf16[8,128,128]{2,1,0:T(8,128)(2,1)S(1)} %collective-permute-done.4.refs_2_, ...), custom_call_target="tpu_custom_call" | custom-call | flops 3221225472 | bytes 3145728 | tf_op jit(solution)/shard_map/pallas_call | solution.py:72
  64.6 3.1 %collective-permute-start.16 = (bf16[4,512,256]{2,1,0:T(8,128)(2,1)S(1)}, bf16[4,512,256]{2,1,0:T(8,128)(2,1)S(1)}, u32[]{:S(2)}, u32[]{:S(2)}) collective-permute-start(bf16[4,512,256]{2,1,0:T(8,128)(2,1)S(1)} %shard_map.113.refs_2_), channel_id=1, source_target_pairs={{0,1},{1,0},{2,3},{3,2},{4,5},{5,4},{6,7},{7,6},{8,9},{9,8},{10,11... | collective-permute-start | bytes 3145736 | tf_op jit(solution)/shard_map/ppermute | solution.py:35
  67.8 0.4 collective-permute-start.12
  68.3 2.5 %collective-permute-done.12.refs_3_ = f32[8,1024]{1,0:T(8,128)S(1)} collective-permute-done((f32[8,1024]{1,0:T(8,128)S(1)}, f32[8,1024]{1,0:T(8,128)S(1)}, u32[]{:S(2)}, u32[]{:S(2)}) %collective-permute-start.12) | collective-permute-done | bytes 32800 | tf_op jit(solution)/shard_map/ppermute | solution.py:35
  70.8 0.9 shard_map.112
  71.6 4.6 %all-to-all-start.1 = ((bf16[8,128,128]{2,1,0:T(8,128)(2,1)}), bf16[8,128,128]{2,1,0:T(8,128)(2,1)S(1)}, u32[]{:S(2)}, u32[]{:S(2)}) async-start(bf16[8,128,128]{2,1,0:T(8,128)(2,1)} %shard_map.112), calls=%async_computation.1 | async-start | bytes 524288 | tf_op jit(solution)/shard_map/all_to_all | solution.py:428
  76.4 3.4 %copy-done.2 = bf16[4,1024,1024]{2,1,0:T(8,128)(2,1)S(1)} copy-done((bf16[4,1024,1024]{2,1,0:T(8,128)(2,1)S(1)}, bf16[4,1024,1024]{2,1,0:T(8,128)(2,1)}, u32[]{:S(2)}) %copy-start.2) | copy-done | bytes 8388632
  79.8 1.3 %shard_map.114.refs_6_.refs_2_ = bf16[3,64,1024]{2,1,0:T(8,128)(2,1)S(1)} custom-call(s32[64,4]{1,0:T(8,128)S(1)} %copy.16.refs_0_.refs_3_, bf16[4,1024,1024]{2,1,0:T(8,128)(2,1)S(1)} %copy-done.2, f32[8,1024]{1,0:T(8,128)S(1)} %get-tuple-element.44.refs_2_.refs_4_), custom_call_target="tpu_custom_call" | custom-call | flops 402653184 | bytes 8388608 | tf_op jit(solution)/shard_map/pallas_call | solution.py:72
  81.1 2.8 %all-to-all-done.1.refs_1_ = bf16[8,128,128]{2,1,0:T(8,128)(2,1)S(1)} async-done(((bf16[8,128,128]{2,1,0:T(8,128)(2,1)}), bf16[8,128,128]{2,1,0:T(8,128)(2,1)S(1)}, u32[]{:S(2)}, u32[]{:S(2)}) %all-to-all-start.1) | async-done | bytes 262176 | tf_op jit(solution)/shard_map/all_to_all | solution.py:428
  83.9 1.5 %shard_map.115 = (f32[64,1024]{1,0:T(8,128)S(1)}, bf16[64,1024]{1,0:T(8,128)(2,1)S(1)}) custom-call(s32[5]{0:T(128)S(1)} %copy-done.10, bf16[8,128,128]{2,1,0:T(8,128)(2,1)S(1)} %all-to-all-done.1.refs_1_, bf16[4,512,256]{2,1,0:T(8,128)(2,1)S(1)} %shard_map.113.refs_2_, bf16[4,512,256]{2,1,0:T(8,128)(2,1)S(1)} %collective-permute-done.16.refs_3_, ...), custom_call_target="tpu_custom_call" | custom-call | flops 268435456 | bytes 3145728 | tf_op jit(solution)/shard_map/pallas_call | solution.py:72
  85.4 0.7 copy-done.11
  86.5 3.4 %collective-permute-done.18.refs_1_ = bf16[64,1024]{1,0:T(8,128)(2,1)S(1)} collective-permute-done((bf16[64,1024]{1,0:T(8,128)(2,1)S(1)}, bf16[64,1024]{1,0:T(8,128)(2,1)S(1)}, u32[]{:S(2)}, u32[]{:S(2)}) %collective-permute-start.18) | collective-permute-done | bytes 131104 | tf_op jit(solution)/shard_map/ppermute | solution.py:35
  90.0 0.6 copy-done.13
  90.6 19.6 %shard_map.116 = (f32[64,128]{1,0:T(8,128)}, bf16[64,1024]{1,0:T(8,128)(2,1)}) custom-call(f32[64,1024]{1,0:T(8,128)} %copy-done.11, bf16[64,1024]{1,0:T(8,128)(2,1)} %copy-done.13, bf16[3,64,1024]{2,1,0:T(8,128)(2,1)} %copy-done.4, s32[64,4]{1,0:T(8,128)} %copy-done.7, bf16[4,1024,1024]{2,1,0:T(8,128)(2,1)} %refs_4_.3, bf16[4,1024,1024]{2,1,0:T(8,128)(2,1)} %refs_5_.2), custom_call_target="tpu_custom_call" | custom-call | flops 12884901888 | bytes 17825792 | tf_op jit(solution)/shard_map/pallas_call | solution.py:72
  110.2 3.3 %collective-permute-start.19 = (bf16[64,1024]{1,0:T(8,128)(2,1)}, bf16[64,1024]{1,0:T(8,128)(2,1)S(1)}, u32[]{:S(2)}, u32[]{:S(2)}) collective-permute-start(bf16[64,1024]{1,0:T(8,128)(2,1)} %get-tuple-element.51.refs_1_), channel_id=1, source_target_pairs={{0,1},{1,0},{2,3},{3,2},{4,5},{5,4},{6,7},{7,6},{8,9},{9,8},{10,11... | collective-permute-start | bytes 393224 | tf_op jit(solution)/shard_map/ppermute | solution.py:35
  113.9 1.3 %collective-permute-start.21 = (bf16[64,1024]{1,0:T(8,128)(2,1)}, bf16[64,1024]{1,0:T(8,128)(2,1)S(1)}, u32[]{:S(2)}, u32[]{:S(2)}) collective-permute-start(bf16[64,1024]{1,0:T(8,128)(2,1)} %get-tuple-element.51.refs_1_), channel_id=1, source_target_pairs={{0,3},{1,2},{2,1},{3,0},{4,7},{5,6},{6,5},{7,4},{8,11},{9,10},{10,... | collective-permute-start | bytes 393224 | tf_op jit(solution)/shard_map/ppermute | solution.py:35
  115.3 1.4 %slice_reduce_fusion = f32[64]{0:T(128)} fusion(f32[64,128]{1,0:T(8,128)} %get-tuple-element.50), kind=kLoop, calls=%fused_computation | loop fusion | bytes 512 | tf_op jit(solution)/shard_map/slice | solution.py:447
  116.6 2.2 %collective-permute-done.20.refs_3_ = bf16[64,1024]{1,0:T(8,128)(2,1)S(1)} collective-permute-done((bf16[64,1024]{1,0:T(8,128)(2,1)}, bf16[64,1024]{1,0:T(8,128)(2,1)S(1)}, u32[]{:S(2)}, u32[]{:S(2)}) %collective-permute-start.20) | collective-permute-done | bytes 131104 | tf_op jit(solution)/shard_map/ppermute | solution.py:35
  118.8 3.0 %collective-permute-done.21.refs_4_ = bf16[64,1024]{1,0:T(8,128)(2,1)S(1)} collective-permute-done((bf16[64,1024]{1,0:T(8,128)(2,1)}, bf16[64,1024]{1,0:T(8,128)(2,1)S(1)}, u32[]{:S(2)}, u32[]{:S(2)}) %collective-permute-start.21) | collective-permute-done | bytes 131104 | tf_op jit(solution)/shard_map/ppermute | solution.py:35
  121.8 0.9 copy-done.8
  122.7 2.1 %shard_map.117 = bf16[256,1024]{1,0:T(8,128)(2,1)} custom-call(s32[5]{0:T(128)S(1)} %copy-done.10, bf16[64,1024]{1,0:T(8,128)(2,1)S(1)} %copy-done.8, bf16[64,1024]{1,0:T(8,128)(2,1)S(1)} %collective-permute-done.19.refs_2_, bf16[64,1024]{1,0:T(8,128)(2,1)S(1)} %collective-permute-done.20.refs_3_, bf16[64,1024]{1,0:T(8,128)(2,1)S(1)} %collective-permute-done.21.refs_4_, ...), custom_call_target="tpu_custom_call" | custom-call | flops 536870912 | bytes 3145728 | tf_op jit(solution)/shard_map/pallas_call | solution.py:72
  (46 shorter events, 1.9 us)
Async XLA Ops:
  1.3 35.7 %copy-start.10 = (s32[5]{0:T(128)S(1)}, s32[5]{0:T(128)}, u32[]{:S(2)}) copy-start(s32[5]{0:T(128)} %stack.23.refs_0_) | copy-start | bytes 64
  4.6 2.3 %collective-permute-start = (bf16[4,128,384]{2,1,0:T(8,128)(2,1)}, bf16[4,128,384]{2,1,0:T(8,128)(2,1)S(1)}, u32[]{:S(2)}, u32[]{:S(2)}) collective-permute-start(bf16[4,128,384]{2,1,0:T(8,128)(2,1)} %get-tuple-element.28), channel_id=1, source_target_pairs={{0,1},{1,0},{2,3},{3,2},{4,5},{5,4},{6,7},{7,6},{8,9},{9,8},{10,11... | collective-permute-start | bytes 1179656 | tf_op jit(solution)/shard_map/ppermute | solution.py:35
  5.4 13.7 %collective-permute-start.2 = (bf16[1024,256]{1,0:T(8,128)(2,1)}, bf16[1024,256]{1,0:T(8,128)(2,1)S(1)}, u32[]{:S(2)}, u32[]{:S(2)}) collective-permute-start(bf16[1024,256]{1,0:T(8,128)(2,1)} %get-tuple-element.30.refs_2_), channel_id=1, source_target_pairs={{0,2},{1,3},{2,0},{3,1},{4,6},{5,7},{6,4},{7,5},{8,10},{9,11},{10,... | collective-permute-start | bytes 1572872 | tf_op jit(solution)/shard_map/ppermute | solution.py:35
  7.7 23.6 %all-to-all-start = ((bf16[8,128,384]{2,1,0:T(8,128)(2,1)}), bf16[8,128,384]{2,1,0:T(8,128)(2,1)S(1)}, u32[]{:S(2)}, u32[]{:S(2)}) async-start(bf16[8,128,384]{2,1,0:T(8,128)(2,1)} %constant_dynamic-update-slice_fusion), calls=%async_computation | async-start | bytes 1572864 | tf_op jit(solution)/shard_map/all_to_all | solution.py:381
  15.4 10.4 %collective-permute-start.1 = (bf16[1024,256]{1,0:T(8,128)(2,1)}, bf16[1024,256]{1,0:T(8,128)(2,1)S(1)}, u32[]{:S(2)}, u32[]{:S(2)}) collective-permute-start(bf16[1024,256]{1,0:T(8,128)(2,1)} %get-tuple-element.30.refs_2_), channel_id=1, source_target_pairs={{0,1},{1,0},{2,3},{3,2},{4,5},{5,4},{6,7},{7,6},{8,9},{9,8},{10,11... | collective-permute-start | bytes 1572872 | tf_op jit(solution)/shard_map/ppermute | solution.py:35
  19.1 6.7 %collective-permute-start.3 = (bf16[1024,256]{1,0:T(8,128)(2,1)S(1)}, bf16[1024,256]{1,0:T(8,128)(2,1)S(1)}, u32[]{:S(2)}, u32[]{:S(2)}) collective-permute-start(bf16[1024,256]{1,0:T(8,128)(2,1)S(1)} %collective-permute-done.2.refs_4_), channel_id=1, source_target_pairs={{0,1},{1,0},{2,3},{3,2},{4,5},{5,4},{6,7},{7,6},{8,9},{9,8},{10,11... | collective-permute-start | bytes 1572872 | tf_op jit(solution)/shard_map/ppermute | solution.py:35
  20.4 1.6 %copy-start = (bf16[1024,1024]{1,0:T(8,128)(2,1)S(1)}, bf16[1024,1024]{1,0:T(8,128)(2,1)}, u32[]{:S(2)}) copy-start(bf16[1024,1024]{1,0:T(8,128)(2,1)} %refs_5_.3) | copy-start | bytes 6291460
  22.0 1.0 copy-start.5
  23.0 0.7 copy-start.9
  25.7 2.2 %copy-start.3 = (bf16[512,4096]{1,0:T(8,128)(2,1)S(1)}, bf16[512,4096]{1,0:T(8,128)(2,1)}, u32[]{:S(2)}) copy-start(bf16[512,4096]{1,0:T(8,128)(2,1)} %refs_1_.6) | copy-start | bytes 12582916
  27.9 1.0 copy-start.6
  31.4 5.6 %collective-permute-start.4 = (bf16[8,128,128]{2,1,0:T(8,128)(2,1)S(1)}, bf16[8,128,128]{2,1,0:T(8,128)(2,1)S(1)}, u32[]{:S(2)}, u32[]{:S(2)}) collective-permute-start(bf16[8,128,128]{2,1,0:T(8,128)(2,1)S(1)} %get-tuple-element.31.refs_1_), channel_id=1, source_target_pairs={{0,1},{1,0},{2,3},{3,2},{4,5},{5,4},{6,7},{7,6},{8,9},{9,8},{10,11... | collective-permute-start | bytes 786440 | tf_op jit(solution)/shard_map/ppermute | solution.py:35
  32.8 8.0 %collective-permute-start.5 = (bf16[4,128,256]{2,1,0:T(8,128)(2,1)S(1)}, bf16[4,128,256]{2,1,0:T(8,128)(2,1)S(1)}, u32[]{:S(2)}, u32[]{:S(2)}) collective-permute-start(bf16[4,128,256]{2,1,0:T(8,128)(2,1)S(1)} %get-tuple-element.32.refs_3_), channel_id=1, source_target_pairs={{0,16},{1,17},{2,18},{3,19},{4,20},{5,21},{6,22},{7,23},{8,24},{9,... | collective-permute-start | bytes 786440 | tf_op jit(solution)/shard_map/ppermute | solution.py:35
  33.0 18.0 %collective-permute-start.10 = (bf16[4,128,256]{2,1,0:T(8,128)(2,1)S(1)}, bf16[4,128,256]{2,1,0:T(8,128)(2,1)S(1)}, u32[]{:S(2)}, u32[]{:S(2)}) collective-permute-start(bf16[4,128,256]{2,1,0:T(8,128)(2,1)S(1)} %get-tuple-element.32.refs_3_), channel_id=1, source_target_pairs={{0,48},{1,49},{2,50},{3,51},{4,52},{5,53},{6,54},{7,55},{8,56},{9,... | collective-permute-start | bytes 786440 | tf_op jit(solution)/shard_map/ppermute | solution.py:35
  34.3 13.1 %collective-permute-start.6 = (bf16[4,128,256]{2,1,0:T(8,128)(2,1)S(1)}, bf16[4,128,256]{2,1,0:T(8,128)(2,1)S(1)}, u32[]{:S(2)}, u32[]{:S(2)}) collective-permute-start(bf16[4,128,256]{2,1,0:T(8,128)(2,1)S(1)} %get-tuple-element.33.refs_4_), channel_id=1, source_target_pairs={{0,48},{1,49},{2,50},{3,51},{4,52},{5,53},{6,54},{7,55},{8,56},{9,... | collective-permute-start | bytes 786440 | tf_op jit(solution)/shard_map/ppermute | solution.py:35
  34.8 16.2 %collective-permute-start.9 = (bf16[4,128,256]{2,1,0:T(8,128)(2,1)S(1)}, bf16[4,128,256]{2,1,0:T(8,128)(2,1)S(1)}, u32[]{:S(2)}, u32[]{:S(2)}) collective-permute-start(bf16[4,128,256]{2,1,0:T(8,128)(2,1)S(1)} %get-tuple-element.33.refs_4_), channel_id=1, source_target_pairs={{0,16},{1,17},{2,18},{3,19},{4,20},{5,21},{6,22},{7,23},{8,24},{9,... | collective-permute-start | bytes 786440 | tf_op jit(solution)/shard_map/ppermute | solution.py:35
  47.4 17.0 %collective-permute-start.13 = (bf16[512,256]{1,0:T(8,128)(2,1)S(1)}, bf16[512,256]{1,0:T(8,128)(2,1)S(1)}, u32[]{:S(2)}, u32[]{:S(2)}) collective-permute-start(bf16[512,256]{1,0:T(8,128)(2,1)S(1)} %get-tuple-element.46.refs_0_), channel_id=1, source_target_pairs={{0,4},{1,5},{2,6},{3,7},{4,8},{5,9},{6,10},{7,11},{8,12},{9,13},{1... | collective-permute-start | bytes 786440 | tf_op jit(solution)/shard_map/ppermute | solution.py:35
  47.5 17.0 %collective-permute-start.14 = (bf16[512,256]{1,0:T(8,128)(2,1)S(1)}, bf16[512,256]{1,0:T(8,128)(2,1)S(1)}, u32[]{:S(2)}, u32[]{:S(2)}) collective-permute-start(bf16[512,256]{1,0:T(8,128)(2,1)S(1)} %get-tuple-element.46.refs_0_), channel_id=1, source_target_pairs={{0,8},{1,9},{2,10},{3,11},{4,12},{5,13},{6,14},{7,15},{8,0},{9,1},... | collective-permute-start | bytes 786440 | tf_op jit(solution)/shard_map/ppermute | solution.py:35
  50.3 14.3 %collective-permute-start.15 = (bf16[512,256]{1,0:T(8,128)(2,1)S(1)}, bf16[512,256]{1,0:T(8,128)(2,1)S(1)}, u32[]{:S(2)}, u32[]{:S(2)}) collective-permute-start(bf16[512,256]{1,0:T(8,128)(2,1)S(1)} %get-tuple-element.46.refs_0_), channel_id=1, source_target_pairs={{0,12},{1,13},{2,14},{3,15},{4,0},{5,1},{6,2},{7,3},{8,4},{9,5},{1... | collective-permute-start | bytes 786440 | tf_op jit(solution)/shard_map/ppermute | solution.py:35
  51.0 9.3 %collective-permute-start.7 = (bf16[4,128,256]{2,1,0:T(8,128)(2,1)S(1)}, bf16[4,128,256]{2,1,0:T(8,128)(2,1)S(1)}, u32[]{:S(2)}, u32[]{:S(2)}) collective-permute-start(bf16[4,128,256]{2,1,0:T(8,128)(2,1)S(1)} %get-tuple-element.35), channel_id=1, source_target_pairs={{0,16},{1,17},{2,18},{3,19},{4,20},{5,21},{6,22},{7,23},{8,24},{9,... | collective-permute-start | bytes 786440 | tf_op jit(solution)/shard_map/ppermute | solution.py:35
  51.0 9.3 %collective-permute-start.8 = (bf16[4,128,256]{2,1,0:T(8,128)(2,1)S(1)}, bf16[4,128,256]{2,1,0:T(8,128)(2,1)S(1)}, u32[]{:S(2)}, u32[]{:S(2)}) collective-permute-start(bf16[4,128,256]{2,1,0:T(8,128)(2,1)S(1)} %get-tuple-element.36), channel_id=1, source_target_pairs={{0,48},{1,49},{2,50},{3,51},{4,52},{5,53},{6,54},{7,55},{8,56},{9,... | collective-permute-start | bytes 786440 | tf_op jit(solution)/shard_map/ppermute | solution.py:35
  60.3 16.0 %copy-start.12 = (s32[64,4]{0,1:T(4,128)S(1)}, s32[64,4]{0,1:T(4,128)}, u32[]{:S(2)}) copy-start(s32[64,4]{0,1:T(4,128)} %param.15) | copy-start | bytes 3076
  64.6 19.3 %collective-permute-start.16 = (bf16[4,512,256]{2,1,0:T(8,128)(2,1)S(1)}, bf16[4,512,256]{2,1,0:T(8,128)(2,1)S(1)}, u32[]{:S(2)}, u32[]{:S(2)}) collective-permute-start(bf16[4,512,256]{2,1,0:T(8,128)(2,1)S(1)} %shard_map.113.refs_2_), channel_id=1, source_target_pairs={{0,1},{1,0},{2,3},{3,2},{4,5},{5,4},{6,7},{7,6},{8,9},{9,8},{10,11... | collective-permute-start | bytes 3145736 | tf_op jit(solution)/shard_map/ppermute | solution.py:35
  67.7 3.1 %collective-permute-start.11 = (bf16[128,1024]{1,0:T(8,128)(2,1)S(1)}, bf16[128,1024]{1,0:T(8,128)(2,1)S(1)}, u32[]{:S(2)}, u32[]{:S(2)}) collective-permute-start(bf16[128,1024]{1,0:T(8,128)(2,1)S(1)} %get-tuple-element.43), channel_id=1, source_target_pairs={{0,1},{1,0},{2,3},{3,2},{4,5},{5,4},{6,7},{7,6},{8,9},{9,8},{10,11... | collective-permute-start | bytes 786440 | tf_op jit(solution)/shard_map/ppermute | solution.py:35
  67.8 3.0 %collective-permute-start.12 = (f32[8,1024]{1,0:T(8,128)S(1)}, f32[8,1024]{1,0:T(8,128)S(1)}, u32[]{:S(2)}, u32[]{:S(2)}) collective-permute-start(f32[8,1024]{1,0:T(8,128)S(1)} %get-tuple-element.45), channel_id=1, source_target_pairs={{0,1},{1,0},{2,3},{3,2},{4,5},{5,4},{6,7},{7,6},{8,9},{9,8},{10,11... | collective-permute-start | bytes 98312 | tf_op jit(solution)/shard_map/ppermute | solution.py:35
  68.2 12.9 %collective-permute-start.17 = (bf16[128,1024]{1,0:T(8,128)(2,1)}, bf16[128,1024]{1,0:T(8,128)(2,1)}, u32[]{:S(2)}, u32[]{:S(2)}) collective-permute-start(bf16[128,1024]{1,0:T(8,128)(2,1)} %get-tuple-element.47), channel_id=1, source_target_pairs={{0,1},{1,0},{2,3},{3,2},{4,5},{5,4},{6,7},{7,6},{8,9},{9,8},{10,11... | collective-permute-start | bytes 786440 | tf_op jit(solution)/shard_map/ppermute | solution.py:35
  71.6 12.2 %all-to-all-start.1 = ((bf16[8,128,128]{2,1,0:T(8,128)(2,1)}), bf16[8,128,128]{2,1,0:T(8,128)(2,1)S(1)}, u32[]{:S(2)}, u32[]{:S(2)}) async-start(bf16[8,128,128]{2,1,0:T(8,128)(2,1)} %shard_map.112), calls=%async_computation.1 | async-start | bytes 524288 | tf_op jit(solution)/shard_map/all_to_all | solution.py:428
  76.4 3.4 %copy-start.2 = (bf16[4,1024,1024]{2,1,0:T(8,128)(2,1)S(1)}, bf16[4,1024,1024]{2,1,0:T(8,128)(2,1)}, u32[]{:S(2)}) copy-start(bf16[4,1024,1024]{2,1,0:T(8,128)(2,1)} %refs_5_.2) | copy-start | bytes 25165828
  79.8 10.2 %copy-start.7 = (s32[64,4]{1,0:T(8,128)}, s32[64,4]{1,0:T(8,128)S(1)}, u32[]{:S(2)}) copy-start(s32[64,4]{1,0:T(8,128)S(1)} %copy.16.refs_0_.refs_3_) | copy-start | bytes 3076
  81.0 8.9 %copy-start.4 = (bf16[3,64,1024]{2,1,0:T(8,128)(2,1)}, bf16[3,64,1024]{2,1,0:T(8,128)(2,1)S(1)}, u32[]{:S(2)}) copy-start(bf16[3,64,1024]{2,1,0:T(8,128)(2,1)S(1)} %shard_map.114.refs_6_.refs_2_) | copy-start | bytes 1179652
  85.4 0.7 copy-start.11
  86.1 3.8 %collective-permute-start.18 = (bf16[64,1024]{1,0:T(8,128)(2,1)S(1)}, bf16[64,1024]{1,0:T(8,128)(2,1)S(1)}, u32[]{:S(2)}, u32[]{:S(2)}) collective-permute-start(bf16[64,1024]{1,0:T(8,128)(2,1)S(1)} %get-tuple-element.49), channel_id=1, source_target_pairs={{0,2},{1,3},{2,0},{3,1},{4,6},{5,7},{6,4},{7,5},{8,10},{9,11},{10,... | collective-permute-start | bytes 393224 | tf_op jit(solution)/shard_map/ppermute | solution.py:35
  89.9 0.6 copy-start.13
  90.6 31.2 %copy-start.1 = (bf16[1024,1024]{1,0:T(8,128)(2,1)S(1)}, bf16[1024,1024]{1,0:T(8,128)(2,1)}, u32[]{:S(2)}) copy-start(bf16[1024,1024]{1,0:T(8,128)(2,1)} %refs_5_.3) | copy-start | bytes 6291460
  110.2 6.4 %collective-permute-start.19 = (bf16[64,1024]{1,0:T(8,128)(2,1)}, bf16[64,1024]{1,0:T(8,128)(2,1)S(1)}, u32[]{:S(2)}, u32[]{:S(2)}) collective-permute-start(bf16[64,1024]{1,0:T(8,128)(2,1)} %get-tuple-element.51.refs_1_), channel_id=1, source_target_pairs={{0,1},{1,0},{2,3},{3,2},{4,5},{5,4},{6,7},{7,6},{8,9},{9,8},{10,11... | collective-permute-start | bytes 393224 | tf_op jit(solution)/shard_map/ppermute | solution.py:35
  113.5 5.3 %collective-permute-start.20 = (bf16[64,1024]{1,0:T(8,128)(2,1)}, bf16[64,1024]{1,0:T(8,128)(2,1)S(1)}, u32[]{:S(2)}, u32[]{:S(2)}) collective-permute-start(bf16[64,1024]{1,0:T(8,128)(2,1)} %get-tuple-element.51.refs_1_), channel_id=1, source_target_pairs={{0,2},{1,3},{2,0},{3,1},{4,6},{5,7},{6,4},{7,5},{8,10},{9,11},{10,... | collective-permute-start | bytes 393224 | tf_op jit(solution)/shard_map/ppermute | solution.py:35
  113.9 7.8 %collective-permute-start.21 = (bf16[64,1024]{1,0:T(8,128)(2,1)}, bf16[64,1024]{1,0:T(8,128)(2,1)S(1)}, u32[]{:S(2)}, u32[]{:S(2)}) collective-permute-start(bf16[64,1024]{1,0:T(8,128)(2,1)} %get-tuple-element.51.refs_1_), channel_id=1, source_target_pairs={{0,3},{1,2},{2,1},{3,0},{4,7},{5,6},{6,5},{7,4},{8,11},{9,10},{10,... | collective-permute-start | bytes 393224 | tf_op jit(solution)/shard_map/ppermute | solution.py:35
  121.8 0.9 copy-start.8
where the time goes:
time: 125 us
  Pallas kernels  48.5 us (39%)
  starting transfers between devices  36.1 us (29%)
  waiting for transfers between devices  24.2 us (19%)
  local copies, waits for them, and re-layouts  15.1 us (12%)
    pallas_call x14, Pallas kernels, call(): pl.pallas_call(run, out_shape=out_shape, in_specs=in_specs, out_specs=out...  48.5 us
    ppermute x22, starting transfers between devices, move(): return lax.ppermute(array, AXES, pairs)  23.8 us
    ppermute x22, waiting for transfers between devices, move(): return lax.ppermute(array, AXES, pairs)  20.9 us
    unnamed x29, local copies, waits for them, and re-layouts  12.3 us
    all_to_all x1, starting transfers between devices, per_device(): mine = lax.all_to_all(full, ('h', 'z'), 0, 0, tiled=True)  7.66 us
    all_to_all x1, starting transfers between devices, per_device(): attended = lax.all_to_all(attended, ('h', 'z'), 0, 0, tiled=True)  4.64 us
    all_to_all x1, waiting for transfers between devices, per_device(): attended = lax.all_to_all(attended, ('h', 'z'), 0, 0, tiled=True)  2.81 us
  transfers between devices with their start and end apart: 24, of which 9 were waited for; matrix products, arithmetic and copies ran while one was open for 2% of the time, Pallas kernels for 17%

commit v1 on v0

--- a/solution.py
+++ b/solution.py
@@ -17,7 +17,6 @@
 LOG2E = 1.4426950408889634
 NEG = -1e30
 VM = pl.BlockSpec(memory_space=pltpu.VMEM)
-SM = pl.BlockSpec(memory_space=pltpu.SMEM)
 ANY = pl.BlockSpec(memory_space=pl.ANY)
 
 
@@ -53,10 +52,6 @@
 
 def l_swap(h, x, z, l, c):
     return h, x, z, 1 - l, c
-
-
-def lc_swap(h, x, z, l, c):
-    return h, x, z, 1 - l, 1 - c
 
 
 def call(body, out_shape, in_specs, *args, after=(), scratch=(), limit=16, flops=0, nbytes=0, aliases=None, out_specs=None):
@@ -97,10 +92,10 @@
     return lax.dot_general(a, b, (((0,), (0,)), ((), ())), preferred_element_type=F32)
 
 
-def split_rows_body(ids, q_hbm, k_hbm, v_hbm, w_hbm, keep_ref, send_ref, cols_ref, local, sems):
-    c = ids[4]
+def split_rows_body(q_hbm, k_hbm, v_hbm, w_hbm, keep_ref, send_ref, cols_ref, local, sems):
+    c = lax.axis_index("c")
     copies = [pltpu.make_async_copy(ref, local.at[n], sems.at[n]) for n, ref in enumerate((q_hbm, k_hbm, v_hbm))]
-    cols = pl.ds(pl.multiple_of(ids[2] * 256, 256), 256)
+    cols = pl.ds(pl.multiple_of(lax.axis_index("z") * 256, 256), 256)
     copies.append(pltpu.make_async_copy(w_hbm.at[:, cols], cols_ref, sems.at[3]))
     for copy in copies:
         copy.start()
@@ -142,9 +137,10 @@
     hi_ref[...] = r_ref[4:8, :, 128:384]
 
 
-def own_block_body(ids, q_ref, q_o_ref, lo_ref, hi_ref, acc_ref, m_ref, l_ref):
+def own_block_body(q_ref, q_o_ref, lo_ref, hi_ref, w_in, acc_ref, m_ref, l_ref, w_ref):
+    w_ref[...] = w_in[...]
     state = (acc_ref, m_ref, l_ref)
-    c = ids[4]
+    c = lax.axis_index("c")
     m_ref[...] = jnp.full_like(m_ref, 0.1 * NEG)
     l_ref[...] = jnp.zeros_like(l_ref)
     acc_ref[...] = jnp.zeros_like(acc_ref)
@@ -160,35 +156,53 @@
         attend(state, q, rows_of(lo_ref, 0, 0), rows_of(lo_ref, 0, 128), 1024 + section * 512)
 
 
-def block_steps(state, qs, low, high, earlier):
+def low_step(state, qs, kv, earlier):
     for section, ref in enumerate(qs):
-        attend(state, rows_of(ref, 4, 0), rows_of(low, 0, 0), rows_of(low, 0, 128), 1024 + section * 512)
+        attend(state, rows_of(ref, 4, 0), rows_of(kv, 0, 0), rows_of(kv, 0, 128), 1024 + section * 512)
 
     @pl.when(earlier)
     def _():
         for section, ref in enumerate(qs):
-            attend(state, rows_of(ref, 0, 0), rows_of(low, 0, 0), rows_of(low, 0, 128), section * 512)
-            attend(state, rows_of(ref, 4, 0), rows_of(high, 0, 0), rows_of(high, 0, 128), 1024 + section * 512)
-
-
-def near_blocks_body(
-    ids, q_ref, q_o_ref, up_lo, up_hi, down_lo, down_hi, acc_in, m_in, l_in, acc_ref, m_ref, l_ref
+            attend(state, rows_of(ref, 0, 0), rows_of(kv, 0, 0), rows_of(kv, 0, 128), section * 512)
+
+
+def high_step(state, qs, kv, earlier):
+    @pl.when(earlier)
+    def _():
+        for section, ref in enumerate(qs):
+            attend(state, rows_of(ref, 4, 0), rows_of(kv, 0, 0), rows_of(kv, 0, 128), 1024 + section * 512)
+
+
+def carry_over(ins, outs):
+    for source, target in zip(ins, outs):
+        target[...] = source[...]
+    return outs
+
+
+def first_blocks_body(
+    q_ref, q_o_ref, up_lo, down_hi, low, high, acc_in, m_in, l_in, acc_ref, m_ref, l_ref, lo_ref, hi_ref
 ):
-    acc_ref[...] = acc_in[...]
-    m_ref[...] = m_in[...]
-    l_ref[...] = l_in[...]
-    state = (acc_ref, m_ref, l_ref)
-    x = ids[1]
-    block_steps(state, (q_ref, q_o_ref), up_lo, up_hi, x > 0)
-    block_steps(state, (q_ref, q_o_ref), down_lo, down_hi, x == 3)
-
-
-def far_block_body(ids, q_ref, q_o_ref, lo, hi, acc_in, m_in, l_in, own_ref, send_ref, own_stat, send_stat, acc_ref, m_ref, l_ref):
-    acc_ref[...] = acc_in[...]
-    m_ref[...] = m_in[...]
-    l_ref[...] = l_in[...]
-    state = (acc_ref, m_ref, l_ref)
-    block_steps(state, (q_ref, q_o_ref), lo, hi, ids[1] >= 2)
+    carry_over((low, high), (lo_ref, hi_ref))
+    state = carry_over((acc_in, m_in, l_in), (acc_ref, m_ref, l_ref))
+    x = lax.axis_index("x")
+    low_step(state, (q_ref, q_o_ref), up_lo, x > 0)
+    high_step(state, (q_ref, q_o_ref), down_hi, x == 3)
+
+
+def far_blocks_body(q_ref, q_o_ref, lo, hi, acc_in, m_in, l_in, acc_ref, m_ref, l_ref):
+    state = carry_over((acc_in, m_in, l_in), (acc_ref, m_ref, l_ref))
+    earlier = lax.axis_index("x") >= 2
+    low_step(state, (q_ref, q_o_ref), lo, earlier)
+    high_step(state, (q_ref, q_o_ref), hi, earlier)
+
+
+def last_blocks_body(
+    q_ref, q_o_ref, up_hi, down_lo, acc_in, m_in, l_in, own_ref, send_ref, own_stat, send_stat, acc_ref, m_ref, l_ref
+):
+    state = carry_over((acc_in, m_in, l_in), (acc_ref, m_ref, l_ref))
+    x = lax.axis_index("x")
+    high_step(state, (q_ref, q_o_ref), up_hi, x > 0)
+    low_step(state, (q_ref, q_o_ref), down_lo, x == 3)
     for section, (ref, stat) in enumerate(((own_ref, own_stat), (send_ref, send_stat))):
         for h in range(2):
             cols = slice(h * 1024 + section * 512, h * 1024 + section * 512 + 512)
@@ -210,8 +224,8 @@
     out_ref[...] = joined.T.astype(BF16).reshape(8, 128, 128)
 
 
-def merged_weight_body(ids, ow_ref, b00, b01, b10, b11, out_ref):
-    l, c = ids[3], ids[4]
+def merged_weight_body(ow_ref, b00, b01, b10, b11, out_ref):
+    l, c = lax.axis_index("l"), lax.axis_index("c")
     total = None
     for dl, dc, ref in ((0, 0, b00), (0, 1, b01), (1, 0, b10), (1, 1, b11)):
         t = jnp.where(dl == 1, 1 - l, l) * 2 + jnp.where(dc == 1, 1 - c, c)
@@ -220,8 +234,8 @@
     out_ref[...] = total.astype(BF16)
 
 
-def hidden_part_body(ids, hid_ref, cw_ref, own_ref, send_ref, out):
-    c = ids[4]
+def hidden_part_body(hid_ref, cw_ref, own_ref, send_ref, out):
+    c = lax.axis_index("c")
     out[...] = dot_nn(hid_ref[...], cw_ref[...])
     for half in range(2):
         rows = slice(half * 64, half * 64 + 64)
@@ -236,10 +250,8 @@
         out_ref[n] = dot_nn(hit, table_ref[n]).astype(BF16)
 
 
-def relay_body(lo_in, hi_in, w_in, lo_ref, hi_ref, w_ref):
-    lo_ref[...] = lo_in[...]
-    hi_ref[...] = hi_in[...]
-    w_ref[...] = w_in[...]
+def relay_body(lo_in, hi_in, lo_ref, hi_ref):
+    carry_over((lo_in, hi_in), (lo_ref, hi_ref))
 
 
 def pack_body(*refs):
@@ -247,8 +259,8 @@
         refs[4][n] = refs[n][...]
 
 
-def project_body(ids, att_ref, w_ref, wo_ref, h_own_ref, h_recv_ref, own_ref, send_ref, out):
-    z, l, c = ids[2], ids[3], ids[4]
+def project_body(att_ref, w_ref, wo_ref, h_own_ref, h_recv_ref, own_ref, send_ref, out):
+    z, l, c = lax.axis_index("z"), lax.axis_index("l"), lax.axis_index("c")
     a_own = att_ref[pl.ds(c * 4, 4)]
     a_oth = att_ref[pl.ds((1 - c) * 4, 4)]
     a_own = jnp.concatenate([a_own[i] for i in range(4)], 1)
@@ -265,20 +277,13 @@
     return lax.rsqrt(jnp.mean(stream * stream, -1, keepdims=True) + 1e-05)
 
 
-def split_dot(a, b):
-    high = a.astype(BF16)
-    low = (a - high.astype(F32)).astype(BF16)
-    return dot_nn(high, b) + dot_nn(low, b)
-
-
 def depth_body(
     own_ref, recv_ref, embed_ref, codes_ref, wt_hbm, tab_hbm, loss_ref, dctx_ref, wt, tab, sems,
 ):
     copies = [pltpu.make_async_copy(wt_hbm.at[i], wt.at[i], sems.at[i]) for i in range(4)]
     copies += [pltpu.make_async_copy(tab_hbm.at[i], tab.at[i], sems.at[4 + i]) for i in range(4)]
-    copies[0].start()
-    copies[1].start()
-    copies[2].start()
+    for copy in copies:
+        copy.start()
     n = 64
     context = own_ref[...] + recv_ref[...].astype(F32)
     stream = jnp.concatenate([context] + [context + embed_ref[i].astype(F32) for i in range(3)], 0)
@@ -287,7 +292,6 @@
     qkv = []
     for i in range(3):
         copies[i].wait()
-        copies[3 + i].start()
         qkv.append(dot_nn(normed, wt[i]))
     q, k, v = qkv
     at = lambda a, i: a[i * n : (i + 1) * n]
@@ -299,7 +303,7 @@
     lane_t = lax.broadcasted_iota(jnp.int32, (128, 1024), 1) // 64
     spread_heads = (lane_t == head_t).astype(BF16)
     prod = jnp.concatenate([at(q, i) * at(k, j) for i, j in pairs], 0)
-    scores = split_dot(prod, gather_heads) * 0.125
+    scores = dot_nn(prod.astype(BF16), gather_heads) * 0.125
     score = {pair: at(scores, number) for number, pair in enumerate(pairs)}
     weight = {}
     for i in range(4):
@@ -314,7 +318,6 @@
         [functools.reduce(jnp.add, [wide[i, j] * at(v, j) for j in range(i + 1)]) for i in range(4)], 0
     ).astype(BF16)
     copies[3].wait()
-    copies[6].start()
     update = dot_nn(mixed, wt[3])
     out = stream + update
     r2 = rms(out)
@@ -325,8 +328,6 @@
     vocab = lax.broadcasted_iota(jnp.int32, (n, 1024), 1)
     for i in range(4):
         copies[4 + i].wait()
-        if i == 0:
-            copies[7].start()
         logits = dot_nt(at(final, i), tab[i]) * scale
         top = jnp.max(logits, -1, keepdims=True)
         e = jnp.exp(logits - top)
@@ -336,12 +337,12 @@
         loss = loss + top + jnp.log(total) - picked
         dlogits = (e / total - hit.astype(F32)).astype(BF16)
         dfinal.append(dot_nn(dlogits, tab[i]) * scale)
-    loss_ref[...] = jnp.broadcast_to(loss, (n, 128))
+    loss_ref[...] = jnp.broadcast_to(loss, (n, 128)).T[0:1, :]
     dfinal = jnp.concatenate(dfinal, 0)
     dout = r2 * (dfinal - out * (r2 * r2) * jnp.mean(dfinal * out, -1, keepdims=True))
     dmixed = dot_nt(dout.astype(BF16), wt[3])
     dprod = jnp.concatenate([at(dmixed, i) * at(v, j) for i, j in pairs], 0)
-    dweights = split_dot(dprod, gather_heads)
+    dweights = dot_nn(dprod.astype(BF16), gather_heads)
     dweight = {pair: at(dweights, number) for number, pair in enumerate(pairs)}
     dscore = []
     for i in range(4):
@@ -359,22 +360,27 @@
     dctx_ref[...] = add([at(dstream, i) for i in range(4)]).astype(BF16)
 
 
-def grad_body(ids, d0, d1, d2, d3, cw_ref, out_ref, rows):
-    l, c = ids[3], ids[4]
-    for dl, dc, ref in ((0, 0, d0), (0, 1, d1), (1, 0, d2), (1, 1, d3)):
-        t = jnp.where(dl == 1, 1 - l, l) * 2 + jnp.where(dc == 1, 1 - c, c)
-        rows[pl.ds(pl.multiple_of(t * 64, 64), 64), :] = ref[...]
+def grad_chip_body(own_ref, other_ref, cw_ref, out_ref, rows):
+    c = lax.axis_index("c")
+    rows[pl.ds(pl.multiple_of(c * 64, 64), 64), :] = own_ref[...]
+    rows[pl.ds(pl.multiple_of((1 - c) * 64, 64), 64), :] = other_ref[...]
     out_ref[...] = dot_nt(rows[...], cw_ref[...]).astype(BF16)
 
 
+def grad_body(chip_ref, l_ref, lc_ref, cw_ref, out_ref, rows):
+    l, c = lax.axis_index("l"), lax.axis_index("c")
+    rows[pl.ds(pl.multiple_of(c * 64, 64), 64), :] = l_ref[...]
+    rows[pl.ds(pl.multiple_of((1 - c) * 64, 64), 64), :] = lc_ref[...]
+    out_ref[pl.ds(pl.multiple_of(l * 128, 128), 128), :] = chip_ref[...]
+    out_ref[pl.ds(pl.multiple_of((1 - l) * 128, 128), 128), :] = dot_nt(rows[...], cw_ref[...]).astype(BF16)
+
+
 def per_device(hidden_in, queries, keys, values, out_weight, context_weight, codes, table, depth_weights):
-    coords = [lax.axis_index(name) for name in AXES]
-    h, x, z, l, c = coords
-    ids = jnp.stack(coords).astype(jnp.int32)
+    c = lax.axis_index("c")
 
     keep, send, cw_cols = call(
-        split_rows_body, (shape(8, 128, 384), shape(4, 128, 384), shape(1024, 256)), [SM] + [ANY] * 4,
-        ids, queries, keys, values, context_weight,
+        split_rows_body, (shape(8, 128, 384), shape(4, 128, 384), shape(1024, 256)), [ANY] * 4,
+        queries, keys, values, context_weight,
         scratch=[pltpu.VMEM((3, 256, 512), BF16), pltpu.SemaphoreType.DMA((4,))], limit=60, nbytes=3 << 20,
     )
     full = lax.dynamic_update_slice(keep, move(send, other_core), ((1 - c) * 4, 0, 0))
@@ -384,11 +390,11 @@
     cw_c = move(cw_cols, other_core)
     cw_lc = move(cw_l, other_core)
     h_own, h_send = call(
-        hidden_part_body, (shape(128, 1024, dtype=F32), shape(128, 1024)), [SM] + [VM] * 2,
-        ids, hidden_in, context_weight, scratch=[pltpu.VMEM((256, 1024), F32)], flops=1 << 29, nbytes=3 << 20,
+        hidden_part_body, (shape(128, 1024, dtype=F32), shape(128, 1024)), [VM] * 2,
+        hidden_in, context_weight, scratch=[pltpu.VMEM((256, 1024), F32)], flops=1 << 29, nbytes=3 << 20,
     )
     merged = call(
-        merged_weight_body, shape(512, 256), [SM] + [VM] * 5, ids, out_weight, cw_cols, cw_c, cw_l, cw_lc,
+        merged_weight_body, shape(512, 256), [VM] * 5, out_weight, cw_cols, cw_c, cw_l, cw_lc,
         flops=1 << 30, nbytes=6 << 20,
     )
     half = shape(4, 128, 256)
@@ -397,23 +403,28 @@
     )
     up_lo, down_hi = move(low, x_up), move(high, x_down)
     q_o = move(q, other_core)
+    stats = (shape(128, 2048, dtype=F32), shape(1, 2048, dtype=F32), shape(1, 2048, dtype=F32))
+    *carry, merged = call(
+        own_block_body, stats + (shape(512, 256),), [VM] * 5, q, q_o, low, high, merged, flops=4 << 30, nbytes=2 << 20
+    )
+    pieces = [merged] + [move(merged, z_by(n)) for n in (1, 2, 3)]
+    relay_lo, relay_hi = call(relay_body, (half, half), [VM] * 2, up_lo, down_hi, after=carry[1:2], nbytes=1 << 20)
+    far_lo, far_hi = move(relay_lo, x_up), move(relay_hi, x_down)
+    *carry, low, high = call(
+        first_blocks_body, stats + (half, half), [VM] * 9, q, q_o, up_lo, down_hi, low, high, *carry, after=(relay_lo,),
+        aliases={6: 0, 7: 1, 8: 2}, flops=3 << 30, nbytes=4 << 20,
+    )
     up_hi, down_lo = move(high, x_up), move(low, x_down)
-    stats = (shape(128, 2048, dtype=F32), shape(1, 2048, dtype=F32), shape(1, 2048, dtype=F32))
-    carry = call(own_block_body, stats, [SM] + [VM] * 4, ids, q, q_o, low, high, flops=4 << 30, nbytes=2 << 20)
-    relay_lo, relay_hi, merged = call(
-        relay_body, (half, half, shape(512, 256)), [VM] * 3, up_lo, down_hi, merged, after=carry[1:2], nbytes=1 << 20
-    )
-    far_lo, far_hi = move(relay_lo, x_up), move(relay_hi, x_down)
     carry = call(
-        near_blocks_body, stats, [SM] + [VM] * 9, ids, q, q_o, up_lo, up_hi, down_lo, down_hi, *carry,
-        aliases={7: 0, 8: 1, 9: 2}, flops=4 << 30, nbytes=4 << 20,
-    )
-    pieces = [merged] + [move(merged, z_by(n)) for n in (1, 2, 3)]
+        far_blocks_body, stats, [VM] * 7, q, q_o, far_lo, far_hi, *carry,
+        aliases={4: 0, 5: 1, 6: 2}, flops=3 << 30, nbytes=3 << 20,
+    )
     h_recv = move(h_send, other_core)
+    embedded = call(embed_body, shape(3, 64, 1024), [VM] * 2, codes, table, after=carry[1:2], flops=3 << 27, nbytes=8 << 20)
     own, send, own_stat, send_stat = call(
-        far_block_body,
+        last_blocks_body,
         (shape(128, 1024, dtype=F32), shape(128, 1024), shape(8, 1024, dtype=F32), shape(8, 1024, dtype=F32)),
-        [SM] + [VM] * 7, ids, q, q_o, far_lo, far_hi, *carry,
+        [VM] * 7, q, q_o, up_hi, down_lo, *carry, after=(embedded, h_recv, *pieces[1:]),
         scratch=[pltpu.VMEM(s.shape, s.dtype) for s in stats], flops=3 << 30, nbytes=3 << 20,
     )
     attended = call(
@@ -422,29 +433,31 @@
     )
     merged = call(pack_body, shape(4, 512, 256), [VM] * 4, *pieces, after=(own_stat,), nbytes=2 << 20)
     merged_o = move(merged, other_core)
-    embedded = call(
-        embed_body, shape(3, 64, 1024), [VM] * 2, codes, table, after=(own_stat,), flops=3 << 27, nbytes=8 << 20,
-    )
     attended = lax.all_to_all(attended, ("h", "z"), 0, 0, tiled=True)
 
     own, send = call(
-        project_body, (shape(64, 1024, dtype=F32), shape(64, 1024)), [SM] + [VM] * 5,
-        ids, attended, merged, merged_o, h_own, h_recv, after=(embedded,),
+        project_body, (shape(64, 1024, dtype=F32), shape(64, 1024)), [VM] * 5,
+        attended, merged, merged_o, h_own, h_recv,
         scratch=[pltpu.VMEM((128, 1024), F32)], flops=1 << 28, nbytes=3 << 20,
     )
     recv = move(send, l_swap)
     losses, dcontext = call(
-        depth_body, (shape(64, 128, dtype=F32), shape(64, 1024)), [VM] * 4 + [ANY] * 2,
+        depth_body, (shape(1, 64, dtype=F32), shape(64, 1024)), [VM] * 4 + [ANY] * 2,
         own, recv, embedded, codes, depth_weights, table,
         scratch=[pltpu.VMEM((4, 1024, 1024), BF16), pltpu.VMEM((4, 1024, 1024), BF16), pltpu.SemaphoreType.DMA((8,))],
-        limit=58, flops=12 << 30, nbytes=17 << 20,
+        limit=60, flops=12 << 30, nbytes=17 << 20,
+    )
+    d_l = move(dcontext, l_swap)
+    rows = [pltpu.VMEM((128, 1024), BF16)]
+    grad_chip = call(
+        grad_chip_body, shape(128, 1024), [VM] * 3, dcontext, move(dcontext, other_core), context_weight,
+        scratch=rows, flops=1 << 28, nbytes=3 << 20,
     )
     grad = call(
-        grad_body, shape(256, 1024), [SM] + [VM] * 5, ids,
-        dcontext, move(dcontext, other_core), move(dcontext, l_swap), move(dcontext, lc_swap), context_weight,
-        scratch=[pltpu.VMEM((256, 1024), BF16)], flops=1 << 29, nbytes=3 << 20,
-    )
-    return losses[:, 0], grad
+        grad_body, shape(256, 1024), [VM] * 4, grad_chip, d_l, move(d_l, other_core), context_weight,
+        scratch=rows, flops=1 << 28, nbytes=3 << 20,
+    )
+    return losses.reshape(64), grad
 
 
 def solution(mesh):

time: 125 us -> 112 us (0.90)
  waiting for transfers between devices: 24.2 us -> 12.7 us
  blocking collectives: 0 us -> 10.8 us
  Pallas kernels: 48.5 us -> 41.2 us
  local copies, waits for them, and re-layouts: 15.1 us -> 9.02 us
    ppermute x22, waiting for transfers between devices: 20.9 us -> 9.82 us  [move(): return lax.ppermute(array, AXES, pairs)]
    all_to_all x0 -> x1, blocking collectives: none -> 10.8 us  [per_device(): attended = lax.all_to_all(attended, ('h', 'z'), 0, 0, tiled=True)]
    pallas_call x14 -> x16, Pallas kernels: 48.5 us -> 41.2 us  [call(): pl.pallas_call(run, out_shape=out_shape, in_specs=in_specs, out_specs=out...]
    ppermute x22, starting transfers between devices: 23.8 us -> 29.6 us  [move(): return lax.ppermute(array, AXES, pairs)]
    all_to_all x1 -> x0, starting transfers between devices: 4.64 us -> none  [per_device(): attended = lax.all_to_all(attended, ('h', 'z'), 0, 0, tiled=True)]
    unnamed x29 -> x27, local copies, waits for them, and re-layouts: 12.3 us -> 8.24 us
    all_to_all x1 -> x0, waiting for transfers between devices: 2.81 us -> none  [per_device(): attended = lax.all_to_all(attended, ('h', 'z'), 0, 0, tiled=True)]
    all_to_all x1, waiting for transfers between devices: 0.53 us -> 2.89 us  [per_device(): mine = lax.all_to_all(full, ('h', 'z'), 0, 0, tiled=True)]
  transfers between devices with their start and end apart: 24 -> 23, of which waited for: 9 -> 8; matrix products, arithmetic and copies ran while one was open for 2% -> 1% of each run, Pallas kernels for 17% -> 13%
where the time goes in v1:
time: 112 us
  Pallas kernels  41.2 us (37%)
  starting transfers between devices  37.3 us (33%)
  waiting for transfers between devices  12.7 us (11%)
  blocking collectives  10.8 us (10%)
  local copies, waits for them, and re-layouts  9.02 us (8%)
    pallas_call x16, Pallas kernels, call(): pl.pallas_call(run, out_shape=out_shape, in_specs=in_specs, out_specs=out...  41.2 us
    ppermute x22, starting transfers between devices, move(): return lax.ppermute(array, AXES, pairs)  29.6 us
    all_to_all x1, blocking collectives, per_device(): attended = lax.all_to_all(attended, ('h', 'z'), 0, 0, tiled=True)  10.8 us
    ppermute x22, waiting for transfers between devices, move(): return lax.ppermute(array, AXES, pairs)  9.82 us
    unnamed x27, local copies, waits for them, and re-layouts  8.24 us
    all_to_all x1, starting transfers between devices, per_device(): mine = lax.all_to_all(full, ('h', 'z'), 0, 0, tiled=True)  7.66 us
    all_to_all x1, waiting for transfers between devices, per_device(): mine = lax.all_to_all(full, ('h', 'z'), 0, 0, tiled=True)  2.89 us
  transfers between devices with their start and end apart: 23, of which 8 were waited for; matrix products, arithmetic and copies ran while one was open for 1% of the time, Pallas kernels for 13%

profile of v1, /device:TPU:7, one launch (start us, length us, event | category | flops | bytes accessed | tf_op | source)
XLA Modules:
  0.0 111.9 jit_solution(17752296206258714734)
XLA Ops:
  0.6 2.5 %shard_map.104 = (bf16[8,128,384]{2,1,0:T(8,128)(2,1)}, bf16[4,128,384]{2,1,0:T(8,128)(2,1)}, bf16[1024,256]{1,0:T(8,128)(2,1)}) custom-call(bf16[256,512]{1,0:T(8,128)(2,1)} %refs_0_.4, bf16[256,512]{1,0:T(8,128)(2,1)} %refs_1_.3, bf16[256,512]{1,0:T(8,128)(2,1)} %refs_2_.2, bf16[1024,1024]{1,0:T(8,128)(2,1)} %refs_3_.4), custom_call_target="tpu_custom_call" | custom-call | bytes 3145728 | tf_op jit(solution)/shard_map/pallas_call | solution.py:67
  3.1 0.8 collective-permute-start
  3.9 1.3 %collective-permute-start.2 = (bf16[1024,256]{1,0:T(8,128)(2,1)}, bf16[1024,256]{1,0:T(8,128)(2,1)S(1)}, u32[]{:S(2)}, u32[]{:S(2)}) collective-permute-start(bf16[1024,256]{1,0:T(8,128)(2,1)} %get-tuple-element.35.refs_1_), channel_id=1, source_target_pairs={{0,2},{1,3},{2,0},{3,1},{4,6},{5,7},{6,4},{7,5},{8,10},{9,11},{10,... | collective-permute-start | bytes 1572872 | tf_op jit(solution)/shard_map/ppermute | solution.py:34
  5.2 0.2 collective-permute-done
  5.5 0.8 constant_dynamic-update-slice_fusion
  6.2 7.7 %all-to-all-start = ((bf16[8,128,384]{2,1,0:T(8,128)(2,1)}), bf16[8,128,384]{2,1,0:T(8,128)(2,1)S(1)}, u32[]{:S(2)}, u32[]{:S(2)}) async-start(bf16[8,128,384]{2,1,0:T(8,128)(2,1)} %constant_dynamic-update-slice_fusion), calls=%async_computation | async-start | bytes 1572864 | tf_op jit(solution)/shard_map/all_to_all | solution.py:387
  13.9 0.7 collective-permute-start.1
  14.6 3.0 %collective-permute-done.2.refs_3_ = bf16[1024,256]{1,0:T(8,128)(2,1)S(1)} collective-permute-done((bf16[1024,256]{1,0:T(8,128)(2,1)}, bf16[1024,256]{1,0:T(8,128)(2,1)S(1)}, u32[]{:S(2)}, u32[]{:S(2)}) %collective-permute-start.2) | collective-permute-done | bytes 524320 | tf_op jit(solution)/shard_map/ppermute | solution.py:34
  17.6 1.3 %collective-permute-start.3 = (bf16[1024,256]{1,0:T(8,128)(2,1)S(1)}, bf16[1024,256]{1,0:T(8,128)(2,1)S(1)}, u32[]{:S(2)}, u32[]{:S(2)}) collective-permute-start(bf16[1024,256]{1,0:T(8,128)(2,1)S(1)} %collective-permute-done.2.refs_3_), channel_id=1, source_target_pairs={{0,1},{1,0},{2,3},{3,2},{4,5},{5,4},{6,7},{7,6},{8,9},{9,8},{10,11... | collective-permute-start | bytes 1572872 | tf_op jit(solution)/shard_map/ppermute | solution.py:34
  18.9 1.6 %copy-done = bf16[1024,1024]{1,0:T(8,128)(2,1)S(1)} copy-done((bf16[1024,1024]{1,0:T(8,128)(2,1)S(1)}, bf16[1024,1024]{1,0:T(8,128)(2,1)}, u32[]{:S(2)}) %copy-start) | copy-done | bytes 2097176
  20.5 1.0 copy-done.3
  21.6 0.9 shard_map.105
  22.5 2.2 %copy-done.2 = bf16[512,4096]{1,0:T(8,128)(2,1)S(1)} copy-done((bf16[512,4096]{1,0:T(8,128)(2,1)S(1)}, bf16[512,4096]{1,0:T(8,128)(2,1)}, u32[]{:S(2)}) %copy-start.2) | copy-done | bytes 4194328
  24.7 1.0 copy-done.4
  25.7 1.2 %shard_map.106.refs_2_.refs_4_ = bf16[512,256]{1,0:T(8,128)(2,1)S(1)} custom-call(bf16[512,4096]{1,0:T(8,128)(2,1)S(1)} %copy-done.2, bf16[1024,256]{1,0:T(8,128)(2,1)S(1)} %copy-done.4, bf16[1024,256]{1,0:T(8,128)(2,1)S(1)} %collective-permute-done.1.refs_2_, bf16[1024,256]{1,0:T(8,128)(2,1)S(1)} %collective-permute-done.2.refs_3_, ...), custom_call_target="tpu_custom_call" | custom-call | flops 1073741824 | bytes 6291456 | tf_op jit(solution)/shard_map/pallas_call | solution.py:67
  27.0 2.9 %all-to-all-done.refs_0_ = bf16[8,128,384]{2,1,0:T(8,128)(2,1)S(1)} async-done(((bf16[8,128,384]{2,1,0:T(8,128)(2,1)}), bf16[8,128,384]{2,1,0:T(8,128)(2,1)S(1)}, u32[]{:S(2)}, u32[]{:S(2)}) %all-to-all-start) | async-done | bytes 786464 | tf_op jit(solution)/shard_map/all_to_all | solution.py:387
  29.9 1.4 %collective-permute-start.4 = (bf16[8,128,128]{2,1,0:T(8,128)(2,1)S(1)}, bf16[8,128,128]{2,1,0:T(8,128)(2,1)S(1)}, u32[]{:S(2)}, u32[]{:S(2)}) collective-permute-start(bf16[8,128,128]{2,1,0:T(8,128)(2,1)S(1)} %get-tuple-element.36.refs_0_), channel_id=1, source_target_pairs={{0,1},{1,0},{2,3},{3,2},{4,5},{5,4},{6,7},{7,6},{8,9},{9,8},{10,11... | collective-permute-start | bytes 786440 | tf_op jit(solution)/shard_map/ppermute | solution.py:34
  31.5 0.3 collective-permute-start.5
  31.8 1.3 %collective-permute-start.6 = (bf16[4,128,256]{2,1,0:T(8,128)(2,1)S(1)}, bf16[4,128,256]{2,1,0:T(8,128)(2,1)S(1)}, u32[]{:S(2)}, u32[]{:S(2)}) collective-permute-start(bf16[4,128,256]{2,1,0:T(8,128)(2,1)S(1)} %get-tuple-element.38.refs_3_.refs_5_), channel_id=1, source_target_pairs={{0,48},{1,49},{2,50},{3,51},{4,52},{5,53},{6,54},{7,55},{8,56},{9,... | collective-permute-start | bytes 786440 | tf_op jit(solution)/shard_map/ppermute | solution.py:34
  33.1 3.3 %shard_map.108 = (f32[128,2048]{1,0:T(8,128)S(1)}, f32[1,2048]{1,0:T(1,128)S(1)}, f32[1,2048]{1,0:T(1,128)S(1)}, bf16[512,256]{1,0:T(8,128)(2,1)S(1)}) custom-call(bf16[8,128,128]{2,1,0:T(8,128)(2,1)S(1)} %get-tuple-element.36.refs_0_, bf16[8,128,128]{2,1,0:T(8,128)(2,1)S(1)} %collective-permute-done.4.refs_1_, ...), custom_call_target="tpu_custom_call" | custom-call | flops 4294967296 | bytes 2097152 | tf_op jit(solution)/shard_map/pallas_call | solution.py:67
  36.5 3.1 %collective-permute-start.13 = (bf16[512,256]{1,0:T(8,128)(2,1)S(1)}, bf16[512,256]{1,0:T(8,128)(2,1)S(1)}, u32[]{:S(2)}, u32[]{:S(2)}) collective-permute-start(bf16[512,256]{1,0:T(8,128)(2,1)S(1)} %get-tuple-element.53.refs_0_), channel_id=1, source_target_pairs={{0,8},{1,9},{2,10},{3,11},{4,12},{5,13},{6,14},{7,15},{8,0},{9,1},... | collective-permute-start | bytes 786440 | tf_op jit(solution)/shard_map/ppermute | solution.py:34
  39.5 0.6 collective-permute-done.6.refs_1_.refs_3_
  40.2 0.1 collective-permute-start.10
  40.3 2.6 %collective-permute-start.9 = (bf16[4,128,256]{2,1,0:T(8,128)(2,1)S(1)}, bf16[4,128,256]{2,1,0:T(8,128)(2,1)S(1)}, u32[]{:S(2)}, u32[]{:S(2)}) collective-permute-start(bf16[4,128,256]{2,1,0:T(8,128)(2,1)S(1)} %get-tuple-element.42.refs_9_), channel_id=1, source_target_pairs={{0,16},{1,17},{2,18},{3,19},{4,20},{5,21},{6,22},{7,23},{8,24},{9,... | collective-permute-start | bytes 786440 | tf_op jit(solution)/shard_map/ppermute | solution.py:34
  43.0 3.7 %shard_map.110 = (f32[128,2048]{1,0:T(8,128)S(1)}, f32[1,2048]{1,0:T(1,128)S(1)}, f32[1,2048]{1,0:T(1,128)S(1)}, bf16[4,128,256]{2,1,0:T(8,128)(2,1)S(1)}, bf16[4,128,256]{2,1,0:T(8,128)(2,1)S(1)}) custom-call(bf16[8,128,128]{2,1,0:T(8,128)(2,1)S(1)} %get-tuple-element.36.refs_0_, ...), custom_call_target="tpu_custom_call", output_to_operand_aliasing={{0}: (6, {}), {1}: (7, {}), {2}: (8, {})} | custom-call | flops 3221225472 | bytes 4194304 | tf_op jit(solution)/shard_map/pallas_call | solution.py:67
  46.7 2.2 %collective-permute-start.14 = (bf16[512,256]{1,0:T(8,128)(2,1)S(1)}, bf16[512,256]{1,0:T(8,128)(2,1)S(1)}, u32[]{:S(2)}, u32[]{:S(2)}) collective-permute-start(bf16[512,256]{1,0:T(8,128)(2,1)S(1)} %get-tuple-element.53.refs_0_), channel_id=1, source_target_pairs={{0,12},{1,13},{2,14},{3,15},{4,0},{5,1},{6,2},{7,3},{8,4},{9,5},{1... | collective-permute-start | bytes 786440 | tf_op jit(solution)/shard_map/ppermute | solution.py:34
  48.9 1.4 %collective-permute-start.8 = (bf16[4,128,256]{2,1,0:T(8,128)(2,1)S(1)}, bf16[4,128,256]{2,1,0:T(8,128)(2,1)S(1)}, u32[]{:S(2)}, u32[]{:S(2)}) collective-permute-start(bf16[4,128,256]{2,1,0:T(8,128)(2,1)S(1)} %get-tuple-element.44), channel_id=1, source_target_pairs={{0,48},{1,49},{2,50},{3,51},{4,52},{5,53},{6,54},{7,55},{8,56},{9,... | collective-permute-start | bytes 786440 | tf_op jit(solution)/shard_map/ppermute | solution.py:34
  50.3 3.5 %shard_map.111 = (f32[128,2048]{1,0:T(8,128)S(1)}, f32[1,2048]{1,0:T(1,128)S(1)}, f32[1,2048]{1,0:T(1,128)S(1)}) custom-call(bf16[8,128,128]{2,1,0:T(8,128)(2,1)S(1)} %get-tuple-element.36.refs_0_, bf16[8,128,128]{2,1,0:T(8,128)(2,1)S(1)} %collective-permute-done.4.refs_1_, ...), custom_call_target="tpu_custom_call", output_to_operand_aliasing={{0}: (4, {}), {1}: (5, {}), {2}: (6, {})} | custom-call | flops 3221225472 | bytes 3145728 | tf_op jit(solution)/shard_map/pallas_call | solution.py:67
  53.9 1.3 %shard_map.112.refs_7_.refs_2_ = bf16[3,64,1024]{2,1,0:T(8,128)(2,1)S(1)} custom-call(s32[64,4]{1,0:T(8,128)S(1)} %copy.17.refs_0_.refs_3_, bf16[4,1024,1024]{2,1,0:T(8,128)(2,1)S(1)} %bitcast.2, f32[1,2048]{1,0:T(1,128)S(1)} %get-tuple-element.50.refs_2_.refs_5_), custom_call_target="tpu_custom_call" | custom-call | flops 402653184 | bytes 8388608 | tf_op jit(solution)/shard_map/pallas_call | solution.py:67
  55.2 0.2 collective-permute-done.8.refs_3_
  55.4 3.8 %shard_map.113 = (f32[128,1024]{1,0:T(8,128)S(1)}, bf16[128,1024]{1,0:T(8,128)(2,1)S(1)}, f32[8,1024]{1,0:T(8,128)S(1)}, f32[8,1024]{1,0:T(8,128)S(1)}) custom-call(bf16[8,128,128]{2,1,0:T(8,128)(2,1)S(1)} %get-tuple-element.36.refs_0_, bf16[8,128,128]{2,1,0:T(8,128)(2,1)S(1)} %collective-permute-done.4.refs_1_, ...), custom_call_target="tpu_custom_call" | custom-call | flops 3221225472 | bytes 3145728 | tf_op jit(solution)/shard_map/pallas_call | solution.py:67
  59.3 3.6 %collective-permute-start.17 = (bf16[4,512,256]{2,1,0:T(8,128)(2,1)S(1)}, bf16[4,512,256]{2,1,0:T(8,128)(2,1)S(1)}, u32[]{:S(2)}, u32[]{:S(2)}) collective-permute-start(bf16[4,512,256]{2,1,0:T(8,128)(2,1)S(1)} %shard_map.115.refs_1_), channel_id=1, source_target_pairs={{0,1},{1,0},{2,3},{3,2},{4,5},{5,4},{6,7},{7,6},{8,9},{9,8},{10,11... | collective-permute-start | bytes 3145736 | tf_op jit(solution)/shard_map/ppermute | solution.py:34
  63.0 0.4 collective-permute-start.16
  63.4 2.2 %collective-permute-done.16.refs_3_ = f32[8,1024]{1,0:T(8,128)S(1)} collective-permute-done((f32[8,1024]{1,0:T(8,128)S(1)}, f32[8,1024]{1,0:T(8,128)S(1)}, u32[]{:S(2)}, u32[]{:S(2)}) %collective-permute-start.16) | collective-permute-done | bytes 32800 | tf_op jit(solution)/shard_map/ppermute | solution.py:34
  65.6 0.2 shard_map.114
  65.8 10.8 %all_to_all.10.refs_0_ = bf16[8,128,128]{2,1,0:T(8,128)(2,1)S(1)} all-to-all(bf16[8,128,128]{2,1,0:T(8,128)(2,1)S(1)} %shard_map.114), channel_id=1, replica_groups=mesh['h'=2,'x'=4,'z'=4,'l'=2,'c'=2] {'h','z'}, dimensions={0} | all-to-all | bytes 524288 | tf_op jit(solution)/shard_map/all_to_all | solution.py:436
  76.6 0.6 shard_map.116
  77.2 0.7 copy-done.8
  77.9 0.4 collective-permute-start.18
  78.3 3.4 %collective-permute-done.18.refs_1_ = bf16[64,1024]{1,0:T(8,128)(2,1)S(1)} collective-permute-done((bf16[64,1024]{1,0:T(8,128)(2,1)S(1)}, bf16[64,1024]{1,0:T(8,128)(2,1)S(1)}, u32[]{:S(2)}, u32[]{:S(2)}) %collective-permute-start.18) | collective-permute-done | bytes 131104 | tf_op jit(solution)/shard_map/ppermute | solution.py:34
  81.7 0.6 copy-done.10
  82.4 17.7 %shard_map.117 = (f32[1,64]{1,0:T(1,128)}, bf16[64,1024]{1,0:T(8,128)(2,1)}) custom-call(f32[64,1024]{1,0:T(8,128)} %copy-done.8, bf16[64,1024]{1,0:T(8,128)(2,1)} %copy-done.10, bf16[3,64,1024]{2,1,0:T(8,128)(2,1)} %copy-done.5, s32[64,4]{1,0:T(8,128)} %copy-done.6, bf16[4,1024,1024]{2,1,0:T(8,128)(2,1)} %refs_4_.1, bf16[4,1024,1024]{2,1,0:T(8,128)(2,1)} %refs_5_.1), custom_call_target="tpu_custom_call" | custom-call | flops 12884901888 | bytes 17825792 | tf_op jit(solution)/shard_map/pallas_call | solution.py:67
  100.0 0.5 collective-permute-start.20
  100.5 3.5 %collective-permute-start.19 = (bf16[64,1024]{1,0:T(8,128)(2,1)}, bf16[64,1024]{1,0:T(8,128)(2,1)S(1)}, u32[]{:S(2)}, u32[]{:S(2)}) collective-permute-start(bf16[64,1024]{1,0:T(8,128)(2,1)} %get-tuple-element.61.refs_0_), channel_id=1, source_target_pairs={{0,1},{1,0},{2,3},{3,2},{4,5},{5,4},{6,7},{7,6},{8,9},{9,8},{10,11... | collective-permute-start | bytes 393224 | tf_op jit(solution)/shard_map/ppermute | solution.py:34
  104.2 4.4 %collective-permute-start.21 = (bf16[64,1024]{1,0:T(8,128)(2,1)S(1)}, bf16[64,1024]{1,0:T(8,128)(2,1)S(1)}, u32[]{:S(2)}, u32[]{:S(2)}) collective-permute-start(bf16[64,1024]{1,0:T(8,128)(2,1)S(1)} %collective-permute-done.20.refs_1_), channel_id=1, source_target_pairs={{0,1},{1,0},{2,3},{3,2},{4,5},{5,4},{6,7},{7,6},{8,9},{9,8},{10,11... | collective-permute-start | bytes 393224 | tf_op jit(solution)/shard_map/ppermute | solution.py:34
  108.6 0.9 copy-done.7
  109.5 0.8 shard_map.118.refs_0_
  110.3 1.6 %shard_map.119 = bf16[256,1024]{1,0:T(8,128)(2,1)} custom-call(bf16[128,1024]{1,0:T(8,128)(2,1)S(1)} %shard_map.118.refs_0_, bf16[64,1024]{1,0:T(8,128)(2,1)S(1)} %collective-permute-done.20.refs_1_, bf16[64,1024]{1,0:T(8,128)(2,1)S(1)} %collective-permute-done.21.refs_2_, bf16[1024,1024]{1,0:T(8,128)(2,1)S(1)} %copy-done.1), custom_call_target="tpu_custom_call" | custom-call | flops 268435456 | bytes 3145728 | tf_op jit(solution)/shard_map/pallas_call | solution.py:67
  (44 shorter events, 0.7 us)
Async XLA Ops:
  0.6 30.8 %copy-start.9 = (s32[64,4]{0,1:T(4,128)S(1)}, s32[64,4]{0,1:T(4,128)}, u32[]{:S(2)}) copy-start(s32[64,4]{0,1:T(4,128)} %param.15) | copy-start | bytes 3076
  3.1 2.3 %collective-permute-start = (bf16[4,128,384]{2,1,0:T(8,128)(2,1)}, bf16[4,128,384]{2,1,0:T(8,128)(2,1)S(1)}, u32[]{:S(2)}, u32[]{:S(2)}) collective-permute-start(bf16[4,128,384]{2,1,0:T(8,128)(2,1)} %get-tuple-element.33), channel_id=1, source_target_pairs={{0,1},{1,0},{2,3},{3,2},{4,5},{5,4},{6,7},{7,6},{8,9},{9,8},{10,11... | collective-permute-start | bytes 1179656 | tf_op jit(solution)/shard_map/ppermute | solution.py:34
  3.9 13.7 %collective-permute-start.2 = (bf16[1024,256]{1,0:T(8,128)(2,1)}, bf16[1024,256]{1,0:T(8,128)(2,1)S(1)}, u32[]{:S(2)}, u32[]{:S(2)}) collective-permute-start(bf16[1024,256]{1,0:T(8,128)(2,1)} %get-tuple-element.35.refs_1_), channel_id=1, source_target_pairs={{0,2},{1,3},{2,0},{3,1},{4,6},{5,7},{6,4},{7,5},{8,10},{9,11},{10,... | collective-permute-start | bytes 1572872 | tf_op jit(solution)/shard_map/ppermute | solution.py:34
  6.2 23.6 %all-to-all-start = ((bf16[8,128,384]{2,1,0:T(8,128)(2,1)}), bf16[8,128,384]{2,1,0:T(8,128)(2,1)S(1)}, u32[]{:S(2)}, u32[]{:S(2)}) async-start(bf16[8,128,384]{2,1,0:T(8,128)(2,1)} %constant_dynamic-update-slice_fusion), calls=%async_computation | async-start | bytes 1572864 | tf_op jit(solution)/shard_map/all_to_all | solution.py:387
  13.9 8.5 %collective-permute-start.1 = (bf16[1024,256]{1,0:T(8,128)(2,1)}, bf16[1024,256]{1,0:T(8,128)(2,1)S(1)}, u32[]{:S(2)}, u32[]{:S(2)}) collective-permute-start(bf16[1024,256]{1,0:T(8,128)(2,1)} %get-tuple-element.35.refs_1_), channel_id=1, source_target_pairs={{0,1},{1,0},{2,3},{3,2},{4,5},{5,4},{6,7},{7,6},{8,9},{9,8},{10,11... | collective-permute-start | bytes 1572872 | tf_op jit(solution)/shard_map/ppermute | solution.py:34
  17.6 4.9 %collective-permute-start.3 = (bf16[1024,256]{1,0:T(8,128)(2,1)S(1)}, bf16[1024,256]{1,0:T(8,128)(2,1)S(1)}, u32[]{:S(2)}, u32[]{:S(2)}) collective-permute-start(bf16[1024,256]{1,0:T(8,128)(2,1)S(1)} %collective-permute-done.2.refs_3_), channel_id=1, source_target_pairs={{0,1},{1,0},{2,3},{3,2},{4,5},{5,4},{6,7},{7,6},{8,9},{9,8},{10,11... | collective-permute-start | bytes 1572872 | tf_op jit(solution)/shard_map/ppermute | solution.py:34
  18.9 1.6 %copy-start = (bf16[1024,1024]{1,0:T(8,128)(2,1)S(1)}, bf16[1024,1024]{1,0:T(8,128)(2,1)}, u32[]{:S(2)}) copy-start(bf16[1024,1024]{1,0:T(8,128)(2,1)} %refs_3_.4) | copy-start | bytes 6291460
  20.5 1.0 copy-start.3
  22.5 2.2 %copy-start.2 = (bf16[512,4096]{1,0:T(8,128)(2,1)S(1)}, bf16[512,4096]{1,0:T(8,128)(2,1)}, u32[]{:S(2)}) copy-start(bf16[512,4096]{1,0:T(8,128)(2,1)} %refs_0_.6) | copy-start | bytes 12582916
  24.7 1.0 copy-start.4
  29.9 3.2 %collective-permute-start.4 = (bf16[8,128,128]{2,1,0:T(8,128)(2,1)S(1)}, bf16[8,128,128]{2,1,0:T(8,128)(2,1)S(1)}, u32[]{:S(2)}, u32[]{:S(2)}) collective-permute-start(bf16[8,128,128]{2,1,0:T(8,128)(2,1)S(1)} %get-tuple-element.36.refs_0_), channel_id=1, source_target_pairs={{0,1},{1,0},{2,3},{3,2},{4,5},{5,4},{6,7},{7,6},{8,9},{9,8},{10,11... | collective-permute-start | bytes 786440 | tf_op jit(solution)/shard_map/ppermute | solution.py:34
  31.3 15.3 %collective-permute-start.11 = (bf16[128,1024]{1,0:T(8,128)(2,1)S(1)}, bf16[128,1024]{1,0:T(8,128)(2,1)S(1)}, u32[]{:S(2)}, u32[]{:S(2)}) collective-permute-start(bf16[128,1024]{1,0:T(8,128)(2,1)S(1)} %get-tuple-element.52), channel_id=1, source_target_pairs={{0,1},{1,0},{2,3},{3,2},{4,5},{5,4},{6,7},{7,6},{8,9},{9,8},{10,11... | collective-permute-start | bytes 786440 | tf_op jit(solution)/shard_map/ppermute | solution.py:34
  31.5 22.4 %copy-start.6 = (s32[64,4]{1,0:T(8,128)}, s32[64,4]{1,0:T(8,128)S(1)}, u32[]{:S(2)}) copy-start(s32[64,4]{1,0:T(8,128)S(1)} %copy.17.refs_0_.refs_3_) | copy-start | bytes 3076
  31.5 8.0 %collective-permute-start.5 = (bf16[4,128,256]{2,1,0:T(8,128)(2,1)S(1)}, bf16[4,128,256]{2,1,0:T(8,128)(2,1)S(1)}, u32[]{:S(2)}, u32[]{:S(2)}) collective-permute-start(bf16[4,128,256]{2,1,0:T(8,128)(2,1)S(1)} %get-tuple-element.37.refs_2_.refs_4_), channel_id=1, source_target_pairs={{0,16},{1,17},{2,18},{3,19},{4,20},{5,21},{6,22},{7,23},{8,24},{9,... | collective-permute-start | bytes 786440 | tf_op jit(solution)/shard_map/ppermute | solution.py:34
  31.8 8.4 %collective-permute-start.6 = (bf16[4,128,256]{2,1,0:T(8,128)(2,1)S(1)}, bf16[4,128,256]{2,1,0:T(8,128)(2,1)S(1)}, u32[]{:S(2)}, u32[]{:S(2)}) collective-permute-start(bf16[4,128,256]{2,1,0:T(8,128)(2,1)S(1)} %get-tuple-element.38.refs_3_.refs_5_), channel_id=1, source_target_pairs={{0,48},{1,49},{2,50},{3,51},{4,52},{5,53},{6,54},{7,55},{8,56},{9,... | collective-permute-start | bytes 786440 | tf_op jit(solution)/shard_map/ppermute | solution.py:34
  36.4 19.0 %collective-permute-start.12 = (bf16[512,256]{1,0:T(8,128)(2,1)S(1)}, bf16[512,256]{1,0:T(8,128)(2,1)S(1)}, u32[]{:S(2)}, u32[]{:S(2)}) collective-permute-start(bf16[512,256]{1,0:T(8,128)(2,1)S(1)} %get-tuple-element.53.refs_0_), channel_id=1, source_target_pairs={{0,4},{1,5},{2,6},{3,7},{4,8},{5,9},{6,10},{7,11},{8,12},{9,13},{1... | collective-permute-start | bytes 786440 | tf_op jit(solution)/shard_map/ppermute | solution.py:34
  36.5 18.9 %collective-permute-start.13 = (bf16[512,256]{1,0:T(8,128)(2,1)S(1)}, bf16[512,256]{1,0:T(8,128)(2,1)S(1)}, u32[]{:S(2)}, u32[]{:S(2)}) collective-permute-start(bf16[512,256]{1,0:T(8,128)(2,1)S(1)} %get-tuple-element.53.refs_0_), channel_id=1, source_target_pairs={{0,8},{1,9},{2,10},{3,11},{4,12},{5,13},{6,14},{7,15},{8,0},{9,1},... | collective-permute-start | bytes 786440 | tf_op jit(solution)/shard_map/ppermute | solution.py:34
  40.2 8.7 %collective-permute-start.10 = (bf16[4,128,256]{2,1,0:T(8,128)(2,1)S(1)}, bf16[4,128,256]{2,1,0:T(8,128)(2,1)S(1)}, u32[]{:S(2)}, u32[]{:S(2)}) collective-permute-start(bf16[4,128,256]{2,1,0:T(8,128)(2,1)S(1)} %get-tuple-element.45), channel_id=1, source_target_pairs={{0,48},{1,49},{2,50},{3,51},{4,52},{5,53},{6,54},{7,55},{8,56},{9,... | collective-permute-start | bytes 786440 | tf_op jit(solution)/shard_map/ppermute | solution.py:34
  40.3 8.5 %collective-permute-start.9 = (bf16[4,128,256]{2,1,0:T(8,128)(2,1)S(1)}, bf16[4,128,256]{2,1,0:T(8,128)(2,1)S(1)}, u32[]{:S(2)}, u32[]{:S(2)}) collective-permute-start(bf16[4,128,256]{2,1,0:T(8,128)(2,1)S(1)} %get-tuple-element.42.refs_9_), channel_id=1, source_target_pairs={{0,16},{1,17},{2,18},{3,19},{4,20},{5,21},{6,22},{7,23},{8,24},{9,... | collective-permute-start | bytes 786440 | tf_op jit(solution)/shard_map/ppermute | solution.py:34
  42.9 11.0 %slice-start = ((s8[8388608]{0:T(1024)(128)(4,1)}), s8[4194304]{0:T(1024)(128)(4,1)S(1)}, s32[]{:S(2)}) async-start(s8[8388608]{0:T(1024)(128)(4,1)} %bitcast.1), calls=%async_computation.2 | async-start | bytes 8388608
  46.7 8.7 %collective-permute-start.14 = (bf16[512,256]{1,0:T(8,128)(2,1)S(1)}, bf16[512,256]{1,0:T(8,128)(2,1)S(1)}, u32[]{:S(2)}, u32[]{:S(2)}) collective-permute-start(bf16[512,256]{1,0:T(8,128)(2,1)S(1)} %get-tuple-element.53.refs_0_), channel_id=1, source_target_pairs={{0,12},{1,13},{2,14},{3,15},{4,0},{5,1},{6,2},{7,3},{8,4},{9,5},{1... | collective-permute-start | bytes 786440 | tf_op jit(solution)/shard_map/ppermute | solution.py:34
  48.9 6.3 %collective-permute-start.7 = (bf16[4,128,256]{2,1,0:T(8,128)(2,1)S(1)}, bf16[4,128,256]{2,1,0:T(8,128)(2,1)S(1)}, u32[]{:S(2)}, u32[]{:S(2)}) collective-permute-start(bf16[4,128,256]{2,1,0:T(8,128)(2,1)S(1)} %get-tuple-element.43), channel_id=1, source_target_pairs={{0,16},{1,17},{2,18},{3,19},{4,20},{5,21},{6,22},{7,23},{8,24},{9,... | collective-permute-start | bytes 786440 | tf_op jit(solution)/shard_map/ppermute | solution.py:34
  48.9 5.0 %slice-start.1 = ((s8[8388608]{0:T(1024)(128)(4,1)}), s8[4194304]{0:T(1024)(128)(4,1)S(1)}, s32[]{:S(2)}) async-start(s8[8388608]{0:T(1024)(128)(4,1)} %bitcast.1), calls=%async_computation.3 | async-start | bytes 8388608
  48.9 6.5 %collective-permute-start.8 = (bf16[4,128,256]{2,1,0:T(8,128)(2,1)S(1)}, bf16[4,128,256]{2,1,0:T(8,128)(2,1)S(1)}, u32[]{:S(2)}, u32[]{:S(2)}) collective-permute-start(bf16[4,128,256]{2,1,0:T(8,128)(2,1)S(1)} %get-tuple-element.44), channel_id=1, source_target_pairs={{0,48},{1,49},{2,50},{3,51},{4,52},{5,53},{6,54},{7,55},{8,56},{9,... | collective-permute-start | bytes 786440 | tf_op jit(solution)/shard_map/ppermute | solution.py:34
  55.2 22.0 %copy-start.5 = (bf16[3,64,1024]{2,1,0:T(8,128)(2,1)}, bf16[3,64,1024]{2,1,0:T(8,128)(2,1)S(1)}, u32[]{:S(2)}) copy-start(bf16[3,64,1024]{2,1,0:T(8,128)(2,1)S(1)} %shard_map.112.refs_7_.refs_2_) | copy-start | bytes 1179652
  59.3 17.3 %collective-permute-start.17 = (bf16[4,512,256]{2,1,0:T(8,128)(2,1)S(1)}, bf16[4,512,256]{2,1,0:T(8,128)(2,1)S(1)}, u32[]{:S(2)}, u32[]{:S(2)}) collective-permute-start(bf16[4,512,256]{2,1,0:T(8,128)(2,1)S(1)} %shard_map.115.refs_1_), channel_id=1, source_target_pairs={{0,1},{1,0},{2,3},{3,2},{4,5},{5,4},{6,7},{7,6},{8,9},{9,8},{10,11... | collective-permute-start | bytes 3145736 | tf_op jit(solution)/shard_map/ppermute | solution.py:34
  62.9 2.7 %collective-permute-start.15 = (bf16[128,1024]{1,0:T(8,128)(2,1)S(1)}, bf16[128,1024]{1,0:T(8,128)(2,1)S(1)}, u32[]{:S(2)}, u32[]{:S(2)}) collective-permute-start(bf16[128,1024]{1,0:T(8,128)(2,1)S(1)} %get-tuple-element.55), channel_id=1, source_target_pairs={{0,1},{1,0},{2,3},{3,2},{4,5},{5,4},{6,7},{7,6},{8,9},{9,8},{10,11... | collective-permute-start | bytes 786440 | tf_op jit(solution)/shard_map/ppermute | solution.py:34
  63.0 2.6 %collective-permute-start.16 = (f32[8,1024]{1,0:T(8,128)S(1)}, f32[8,1024]{1,0:T(8,128)S(1)}, u32[]{:S(2)}, u32[]{:S(2)}) collective-permute-start(f32[8,1024]{1,0:T(8,128)S(1)} %get-tuple-element.57), channel_id=1, source_target_pairs={{0,1},{1,0},{2,3},{3,2},{4,5},{5,4},{6,7},{7,6},{8,9},{9,8},{10,11... | collective-permute-start | bytes 98312 | tf_op jit(solution)/shard_map/ppermute | solution.py:34
  77.2 0.7 copy-start.8
  77.9 3.8 %collective-permute-start.18 = (bf16[64,1024]{1,0:T(8,128)(2,1)S(1)}, bf16[64,1024]{1,0:T(8,128)(2,1)S(1)}, u32[]{:S(2)}, u32[]{:S(2)}) collective-permute-start(bf16[64,1024]{1,0:T(8,128)(2,1)S(1)} %get-tuple-element.59), channel_id=1, source_target_pairs={{0,2},{1,3},{2,0},{3,1},{4,6},{5,7},{6,4},{7,5},{8,10},{9,11},{10,... | collective-permute-start | bytes 393224 | tf_op jit(solution)/shard_map/ppermute | solution.py:34
  81.7 0.7 copy-start.10
  82.3 26.2 %copy-start.1 = (bf16[1024,1024]{1,0:T(8,128)(2,1)S(1)}, bf16[1024,1024]{1,0:T(8,128)(2,1)}, u32[]{:S(2)}) copy-start(bf16[1024,1024]{1,0:T(8,128)(2,1)} %refs_3_.4) | copy-start | bytes 6291460
  100.0 4.1 %collective-permute-start.20 = (bf16[64,1024]{1,0:T(8,128)(2,1)}, bf16[64,1024]{1,0:T(8,128)(2,1)S(1)}, u32[]{:S(2)}, u32[]{:S(2)}) collective-permute-start(bf16[64,1024]{1,0:T(8,128)(2,1)} %get-tuple-element.61.refs_0_), channel_id=1, source_target_pairs={{0,2},{1,3},{2,0},{3,1},{4,6},{5,7},{6,4},{7,5},{8,10},{9,11},{10,... | collective-permute-start | bytes 393224 | tf_op jit(solution)/shard_map/ppermute | solution.py:34
  100.5 8.0 %collective-permute-start.19 = (bf16[64,1024]{1,0:T(8,128)(2,1)}, bf16[64,1024]{1,0:T(8,128)(2,1)S(1)}, u32[]{:S(2)}, u32[]{:S(2)}) collective-permute-start(bf16[64,1024]{1,0:T(8,128)(2,1)} %get-tuple-element.61.refs_0_), channel_id=1, source_target_pairs={{0,1},{1,0},{2,3},{3,2},{4,5},{5,4},{6,7},{7,6},{8,9},{9,8},{10,11... | collective-permute-start | bytes 393224 | tf_op jit(solution)/shard_map/ppermute | solution.py:34
  104.2 6.1 %collective-permute-start.21 = (bf16[64,1024]{1,0:T(8,128)(2,1)S(1)}, bf16[64,1024]{1,0:T(8,128)(2,1)S(1)}, u32[]{:S(2)}, u32[]{:S(2)}) collective-permute-start(bf16[64,1024]{1,0:T(8,128)(2,1)S(1)} %collective-permute-done.20.refs_1_), channel_id=1, source_target_pairs={{0,1},{1,0},{2,3},{3,2},{4,5},{5,4},{6,7},{7,6},{8,9},{9,8},{10,11... | collective-permute-start | bytes 393224 | tf_op jit(solution)/shard_map/ppermute | solution.py:34
  108.5 0.9 copy-start.7

commit v2 on v1

--- a/solution.py
+++ b/solution.py
@@ -112,32 +112,45 @@
     copies[3].wait()
 
 
-def attend(state, q, keys, vals, start, mask=None):
+def attend(state, q, keys, vals_t, start, mask=None):
     acc_ref, m_ref, l_ref = state
-    cols = slice(start, start + 512)
-    s = dot_nt(keys, q) * (LOG2E / HD**0.5)
-    if mask is not None:
-        s = jnp.where(mask, s, NEG)
-    old = m_ref[:, cols]
-    new = jnp.maximum(old, jnp.max(s, 0, keepdims=True))
-    p = jnp.exp2(s - new)
-    alpha = jnp.exp2(old - new)
-    m_ref[:, cols] = new
-    l_ref[:, cols] = l_ref[:, cols] * alpha + jnp.sum(p, 0, keepdims=True)
-    acc_ref[:, cols] = acc_ref[:, cols] * alpha + dot_tn(vals, p.astype(BF16))
-
-
-def rows_of(ref, first, col):
-    return ref[first : first + 4, :, col : col + 128].reshape(512, 128)
+    for first in range(0, 512, 128):
+        cols = slice(start + first, start + first + 128)
+        s = dot_nt(keys, q[first : first + 128]) * (LOG2E / HD**0.5)
+        if mask is not None:
+            s = jnp.where(mask[:, first : first + 128], s, NEG)
+        old = m_ref[:, cols]
+        new = jnp.maximum(old, jnp.max(s, 0, keepdims=True))
+        p = jnp.exp2(s - new)
+        alpha = jnp.exp2(old - new)
+        m_ref[:, cols] = new
+        l_ref[:, cols] = l_ref[:, cols] * alpha + jnp.sum(p, 0, keepdims=True)
+        acc_ref[:, cols] = acc_ref[:, cols] * alpha + dot_nn(vals_t, p.astype(BF16))
+
+
+def rows_of(ref, first):
+    return ref[first : first + 4, :, 0:128].reshape(512, 128)
+
+
+def values_of(ref, first):
+    return jnp.concatenate([ref[first + n, :, 128:256] for n in range(4)], 1)
 
 
 def take_rows_body(r_ref, lo_ref, hi_ref, q_ref):
     q_ref[...] = r_ref[:, :, 0:128]
-    lo_ref[...] = r_ref[0:4, :, 128:384]
-    hi_ref[...] = r_ref[4:8, :, 128:384]
-
-
-def own_block_body(q_ref, q_o_ref, lo_ref, hi_ref, w_in, acc_ref, m_ref, l_ref, w_ref):
+    for n in range(8):
+        ref = lo_ref if n < 4 else hi_ref
+        ref[n % 4, :, 0:128] = r_ref[n, :, 128:256]
+        ref[n % 4, :, 128:256] = r_ref[n, :, 256:384].T
+
+
+def carry_over(ins, outs):
+    for source, target in zip(ins, outs):
+        target[...] = source[...]
+    return outs
+
+
+def own_block_body(q_ref, q_o_ref, lo_in, hi_in, w_in, acc_ref, m_ref, l_ref, w_ref):
     w_ref[...] = w_in[...]
     state = (acc_ref, m_ref, l_ref)
     c = lax.axis_index("c")
@@ -150,33 +163,26 @@
     key_place = place(key_row, c)
     for section, (ref, core) in enumerate(((q_ref, c), (q_o_ref, 1 - c))):
         mask = key_place <= place(q_row, core)
-        for h, kv in enumerate((lo_ref, hi_ref)):
-            q = rows_of(ref, h * 4, 0)
-            attend(state, q, rows_of(kv, 0, 0), rows_of(kv, 0, 128), h * 1024 + section * 512, mask)
-        attend(state, q, rows_of(lo_ref, 0, 0), rows_of(lo_ref, 0, 128), 1024 + section * 512)
+        for h, kv in enumerate((lo_in, hi_in)):
+            attend(state, rows_of(ref, h * 4), rows_of(kv, 0), values_of(kv, 0), h * 1024 + section * 512, mask)
+        attend(state, rows_of(ref, 4), rows_of(lo_in, 0), values_of(lo_in, 0), 1024 + section * 512)
 
 
 def low_step(state, qs, kv, earlier):
     for section, ref in enumerate(qs):
-        attend(state, rows_of(ref, 4, 0), rows_of(kv, 0, 0), rows_of(kv, 0, 128), 1024 + section * 512)
+        attend(state, rows_of(ref, 4), rows_of(kv, 0), values_of(kv, 0), 1024 + section * 512)
 
     @pl.when(earlier)
     def _():
         for section, ref in enumerate(qs):
-            attend(state, rows_of(ref, 0, 0), rows_of(kv, 0, 0), rows_of(kv, 0, 128), section * 512)
+            attend(state, rows_of(ref, 0), rows_of(kv, 0), values_of(kv, 0), section * 512)
 
 
 def high_step(state, qs, kv, earlier):
     @pl.when(earlier)
     def _():
         for section, ref in enumerate(qs):
-            attend(state, rows_of(ref, 4, 0), rows_of(kv, 0, 0), rows_of(kv, 0, 128), 1024 + section * 512)
-
-
-def carry_over(ins, outs):
-    for source, target in zip(ins, outs):
-        target[...] = source[...]
-    return outs
+            attend(state, rows_of(ref, 4), rows_of(kv, 0), values_of(kv, 0), 1024 + section * 512)
 
 
 def first_blocks_body(
@@ -197,30 +203,43 @@
 
 
 def last_blocks_body(
-    q_ref, q_o_ref, up_hi, down_lo, acc_in, m_in, l_in, own_ref, send_ref, own_stat, send_stat, acc_ref, m_ref, l_ref
+    q_ref, q_o_ref, up_hi, down_lo, acc_in, m_in, l_in, own_ref, send_ref, own_stat, acc_ref, m_ref, l_ref
 ):
     state = carry_over((acc_in, m_in, l_in), (acc_ref, m_ref, l_ref))
     x = lax.axis_index("x")
     high_step(state, (q_ref, q_o_ref), up_hi, x > 0)
     low_step(state, (q_ref, q_o_ref), down_lo, x == 3)
-    for section, (ref, stat) in enumerate(((own_ref, own_stat), (send_ref, send_stat))):
+    send_ref[...] = jnp.zeros_like(send_ref)
+    for section in range(2):
         for h in range(2):
             cols = slice(h * 1024 + section * 512, h * 1024 + section * 512 + 512)
             to = slice(h * 512, h * 512 + 512)
+            top = m_ref[:, cols]
             total = l_ref[:, cols]
-            ref[:, to] = (acc_ref[:, cols] / jnp.maximum(total, 0.5)).astype(ref.dtype)
-            stat[0:1, to] = m_ref[:, cols]
-            stat[1:2, to] = total
-
-
-def join_cores_body(own_ref, recv_ref, own_stat, recv_stat, out_ref):
+            part = acc_ref[:, cols] / jnp.maximum(total, 0.5)
+            if section == 0:
+                own_ref[:, to] = part
+                own_stat[0:1, to] = top
+                own_stat[1:2, to] = total
+            else:
+                send_ref[0:128, to] = part.astype(BF16)
+                for n, value in enumerate((top, total)):
+                    for term in range(3):
+                        piece = value.astype(BF16)
+                        send_ref[128 + n * 16 + term : 129 + n * 16 + term, to] = piece
+                        value = value - piece.astype(F32)
+
+
+def join_cores_body(own_ref, recv_ref, own_stat, out_ref):
     m1, l1 = own_stat[0:1, :], own_stat[1:2, :]
-    m2, l2 = recv_stat[0:1, :], recv_stat[1:2, :]
+    stat = recv_ref[128:160, :].astype(F32)
+    m2 = stat[0:1] + stat[1:2] + stat[2:3]
+    l2 = stat[16:17] + stat[17:18] + stat[18:19]
     top = jnp.maximum(m1, m2)
     w1 = l1 * jnp.exp2(m1 - top)
     w2 = l2 * jnp.exp2(m2 - top)
     share = 1.0 / (w1 + w2)
-    joined = own_ref[...] * (w1 * share) + recv_ref[...].astype(F32) * (w2 * share)
+    joined = own_ref[...] * (w1 * share) + recv_ref[0:128, :].astype(F32) * (w2 * share)
     out_ref[...] = joined.T.astype(BF16).reshape(8, 128, 128)
 
 
@@ -295,7 +314,7 @@
         qkv.append(dot_nn(normed, wt[i]))
     q, k, v = qkv
     at = lambda a, i: a[i * n : (i + 1) * n]
-    pairs = [(i, j) for i in range(4) for j in range(i + 1)]
+    pairs = [(i, j) for i in range(1, 4) for j in range(i + 1)]
     lane = lax.broadcasted_iota(jnp.int32, (1024, 128), 0) // 64
     head = lax.broadcasted_iota(jnp.int32, (1024, 128), 1)
     gather_heads = (lane == head).astype(BF16)
@@ -306,7 +325,7 @@
     scores = dot_nn(prod.astype(BF16), gather_heads) * 0.125
     score = {pair: at(scores, number) for number, pair in enumerate(pairs)}
     weight = {}
-    for i in range(4):
+    for i in range(1, 4):
         top = functools.reduce(jnp.maximum, [score[i, j] for j in range(i + 1)])
         es = [jnp.exp(score[i, j] - top) for j in range(i + 1)]
         total = functools.reduce(jnp.add, es)
@@ -315,7 +334,7 @@
     spread = dot_nn(jnp.concatenate([weight[p] for p in pairs], 0).astype(BF16), spread_heads)
     wide = {pair: at(spread, number) for number, pair in enumerate(pairs)}
     mixed = jnp.concatenate(
-        [functools.reduce(jnp.add, [wide[i, j] * at(v, j) for j in range(i + 1)]) for i in range(4)], 0
+        [at(v, 0)] + [functools.reduce(jnp.add, [wide[i, j] * at(v, j) for j in range(i + 1)]) for i in range(1, 4)], 0
     ).astype(BF16)
     copies[3].wait()
     update = dot_nn(mixed, wt[3])
@@ -335,7 +354,7 @@
         hit = vocab == codes_ref[:, i : i + 1]
         picked = jnp.sum(jnp.where(hit, logits, 0.0), -1, keepdims=True)
         loss = loss + top + jnp.log(total) - picked
-        dlogits = (e / total - hit.astype(F32)).astype(BF16)
+        dlogits = (e * (1.0 / total) - hit.astype(F32)).astype(BF16)
         dfinal.append(dot_nn(dlogits, tab[i]) * scale)
     loss_ref[...] = jnp.broadcast_to(loss, (n, 128)).T[0:1, :]
     dfinal = jnp.concatenate(dfinal, 0)
@@ -345,16 +364,18 @@
     dweights = dot_nn(dprod.astype(BF16), gather_heads)
     dweight = {pair: at(dweights, number) for number, pair in enumerate(pairs)}
     dscore = []
-    for i in range(4):
+    for i in range(1, 4):
         mean = functools.reduce(jnp.add, [weight[i, j] * dweight[i, j] for j in range(i + 1)])
         for j in range(i + 1):
             dscore.append(weight[i, j] * (dweight[i, j] - mean) * 0.125)
     spread = dot_nn(jnp.concatenate(dscore, 0).astype(BF16), spread_heads)
     dwide = {pair: at(spread, number) for number, pair in enumerate(pairs)}
     add = lambda terms: functools.reduce(jnp.add, terms)
-    dq = jnp.concatenate([add([dwide[i, j] * at(k, j) for j in range(i + 1)]) for i in range(4)], 0)
-    dk = jnp.concatenate([add([dwide[i, j] * at(q, i) for i in range(j, 4)]) for j in range(4)], 0)
-    dv = jnp.concatenate([add([wide[i, j] * at(dmixed, i) for i in range(j, 4)]) for j in range(4)], 0)
+    dq = [add([dwide[i, j] * at(k, j) for j in range(i + 1)]) for i in range(1, 4)]
+    dq = jnp.concatenate([jnp.zeros((n, 1024), F32)] + dq, 0)
+    dk = jnp.concatenate([add([dwide[i, j] * at(q, i) for i in range(max(j, 1), 4)]) for j in range(4)], 0)
+    dv = [add([wide[i, j] * at(dmixed, i) for i in range(max(j, 1), 4)]) for j in range(4)]
+    dv = jnp.concatenate([dv[0] + at(dmixed, 0)] + dv[1:], 0)
     dnormed = dot_nt(dq.astype(BF16), wt[0]) + dot_nt(dk.astype(BF16), wt[1]) + dot_nt(dv.astype(BF16), wt[2])
     dstream = dout + r1 * (dnormed - stream * (r1 * r1) * jnp.mean(dnormed * stream, -1, keepdims=True))
     dctx_ref[...] = add([at(dstream, i) for i in range(4)]).astype(BF16)
@@ -421,17 +442,14 @@
     )
     h_recv = move(h_send, other_core)
     embedded = call(embed_body, shape(3, 64, 1024), [VM] * 2, codes, table, after=carry[1:2], flops=3 << 27, nbytes=8 << 20)
-    own, send, own_stat, send_stat = call(
-        last_blocks_body,
-        (shape(128, 1024, dtype=F32), shape(128, 1024), shape(8, 1024, dtype=F32), shape(8, 1024, dtype=F32)),
+    own, send, own_stat = call(
+        last_blocks_body, (shape(128, 1024, dtype=F32), shape(160, 1024), shape(8, 1024, dtype=F32)),
         [VM] * 7, q, q_o, up_hi, down_lo, *carry, after=(embedded, h_recv, *pieces[1:]),
         scratch=[pltpu.VMEM(s.shape, s.dtype) for s in stats], flops=3 << 30, nbytes=3 << 20,
     )
-    attended = call(
-        join_cores_body, shape(8, 128, 128), [VM] * 4,
-        own, move(send, other_core), own_stat, move(send_stat, other_core), nbytes=1 << 20,
-    )
-    merged = call(pack_body, shape(4, 512, 256), [VM] * 4, *pieces, after=(own_stat,), nbytes=2 << 20)
+    joined = move(send, other_core)
+    attended = call(join_cores_body, shape(8, 128, 128), [VM] * 3, own, joined, own_stat, nbytes=1 << 20)
+    merged = call(pack_body, shape(4, 512, 256), [VM] * 4, *pieces, after=(joined,), nbytes=2 << 20)
     merged_o = move(merged, other_core)
     attended = lax.all_to_all(attended, ("h", "z"), 0, 0, tiled=True)
 

time: 112 us -> 111 us (level)
    ppermute x22 -> x21, starting transfers between devices: 29.6 us -> 29.3 us  [move(): return lax.ppermute(array, AXES, pairs)]
    ppermute x22 -> x21, waiting for transfers between devices: 9.82 us -> 9.7 us  [move(): return lax.ppermute(array, AXES, pairs)]
  transfers between devices with their start and end apart: 23 -> 22, of which waited for: 8 -> 8; matrix products, arithmetic and copies ran while one was open for 1% -> 1% of each run, Pallas kernels for 13% -> 13%
where the time goes in v2:
time: 111 us
  Pallas kernels  40.6 us (37%)
  starting transfers between devices  36.9 us (33%)
  waiting for transfers between devices  12.6 us (11%)
  blocking collectives  10.7 us (10%)
  local copies, waits for them, and re-layouts  9.02 us (8%)
    pallas_call x16, Pallas kernels, call(): pl.pallas_call(run, out_shape=out_shape, in_specs=in_specs, out_specs=out...  40.6 us
    ppermute x21, starting transfers between devices, move(): return lax.ppermute(array, AXES, pairs)  29.3 us
    all_to_all x1, blocking collectives, per_device(): attended = lax.all_to_all(attended, ('h', 'z'), 0, 0, tiled=True)  10.7 us
    ppermute x21, waiting for transfers between devices, move(): return lax.ppermute(array, AXES, pairs)  9.7 us
    unnamed x27, local copies, waits for them, and re-layouts  8.24 us
    all_to_all x1, starting transfers between devices, per_device(): mine = lax.all_to_all(full, ('h', 'z'), 0, 0, tiled=True)  7.66 us
    all_to_all x1, waiting for transfers between devices, per_device(): mine = lax.all_to_all(full, ('h', 'z'), 0, 0, tiled=True)  2.89 us
  transfers between devices with their start and end apart: 22, of which 8 were waited for; matrix products, arithmetic and copies ran while one was open for 1% of the time, Pallas kernels for 13%

profile of v2, /device:TPU:7, one launch (start us, length us, event | category | flops | bytes accessed | tf_op | source)
XLA Modules:
  0.0 110.7 jit_solution(10018951779918656532)
XLA Ops:
  0.6 2.5 %shard_map.104 = (bf16[8,128,384]{2,1,0:T(8,128)(2,1)}, bf16[4,128,384]{2,1,0:T(8,128)(2,1)}, bf16[1024,256]{1,0:T(8,128)(2,1)}) custom-call(bf16[256,512]{1,0:T(8,128)(2,1)} %refs_0_.4, bf16[256,512]{1,0:T(8,128)(2,1)} %refs_1_.3, bf16[256,512]{1,0:T(8,128)(2,1)} %refs_2_.2, bf16[1024,1024]{1,0:T(8,128)(2,1)} %refs_3_.4), custom_call_target="tpu_custom_call" | custom-call | bytes 3145728 | tf_op jit(solution)/shard_map/pallas_call | solution.py:67
  3.1 0.8 collective-permute-start
  3.9 1.3 %collective-permute-start.2 = (bf16[1024,256]{1,0:T(8,128)(2,1)}, bf16[1024,256]{1,0:T(8,128)(2,1)S(1)}, u32[]{:S(2)}, u32[]{:S(2)}) collective-permute-start(bf16[1024,256]{1,0:T(8,128)(2,1)} %get-tuple-element.34.refs_1_), channel_id=1, source_target_pairs={{0,2},{1,3},{2,0},{3,1},{4,6},{5,7},{6,4},{7,5},{8,10},{9,11},{10,... | collective-permute-start | bytes 1572872 | tf_op jit(solution)/shard_map/ppermute | solution.py:34
  5.2 0.2 collective-permute-done
  5.5 0.8 constant_dynamic-update-slice_fusion
  6.2 7.7 %all-to-all-start = ((bf16[8,128,384]{2,1,0:T(8,128)(2,1)}), bf16[8,128,384]{2,1,0:T(8,128)(2,1)S(1)}, u32[]{:S(2)}, u32[]{:S(2)}) async-start(bf16[8,128,384]{2,1,0:T(8,128)(2,1)} %constant_dynamic-update-slice_fusion), calls=%async_computation | async-start | bytes 1572864 | tf_op jit(solution)/shard_map/all_to_all | solution.py:408
  13.9 0.7 collective-permute-start.1
  14.6 3.0 %collective-permute-done.2.refs_3_ = bf16[1024,256]{1,0:T(8,128)(2,1)S(1)} collective-permute-done((bf16[1024,256]{1,0:T(8,128)(2,1)}, bf16[1024,256]{1,0:T(8,128)(2,1)S(1)}, u32[]{:S(2)}, u32[]{:S(2)}) %collective-permute-start.2) | collective-permute-done | bytes 524320 | tf_op jit(solution)/shard_map/ppermute | solution.py:34
  17.6 1.3 %collective-permute-start.3 = (bf16[1024,256]{1,0:T(8,128)(2,1)S(1)}, bf16[1024,256]{1,0:T(8,128)(2,1)S(1)}, u32[]{:S(2)}, u32[]{:S(2)}) collective-permute-start(bf16[1024,256]{1,0:T(8,128)(2,1)S(1)} %collective-permute-done.2.refs_3_), channel_id=1, source_target_pairs={{0,1},{1,0},{2,3},{3,2},{4,5},{5,4},{6,7},{7,6},{8,9},{9,8},{10,11... | collective-permute-start | bytes 1572872 | tf_op jit(solution)/shard_map/ppermute | solution.py:34
  18.9 1.6 %copy-done = bf16[1024,1024]{1,0:T(8,128)(2,1)S(1)} copy-done((bf16[1024,1024]{1,0:T(8,128)(2,1)S(1)}, bf16[1024,1024]{1,0:T(8,128)(2,1)}, u32[]{:S(2)}) %copy-start) | copy-done | bytes 2097176
  20.5 1.0 copy-done.3
  21.6 0.9 shard_map.105
  22.5 2.2 %copy-done.2 = bf16[512,4096]{1,0:T(8,128)(2,1)S(1)} copy-done((bf16[512,4096]{1,0:T(8,128)(2,1)S(1)}, bf16[512,4096]{1,0:T(8,128)(2,1)}, u32[]{:S(2)}) %copy-start.2) | copy-done | bytes 4194328
  24.7 1.0 copy-done.4
  25.7 1.2 %shard_map.106.refs_2_.refs_4_ = bf16[512,256]{1,0:T(8,128)(2,1)S(1)} custom-call(bf16[512,4096]{1,0:T(8,128)(2,1)S(1)} %copy-done.2, bf16[1024,256]{1,0:T(8,128)(2,1)S(1)} %copy-done.4, bf16[1024,256]{1,0:T(8,128)(2,1)S(1)} %collective-permute-done.1.refs_2_, bf16[1024,256]{1,0:T(8,128)(2,1)S(1)} %collective-permute-done.2.refs_3_, ...), custom_call_target="tpu_custom_call" | custom-call | flops 1073741824 | bytes 6291456 | tf_op jit(solution)/shard_map/pallas_call | solution.py:67
  27.0 2.9 %all-to-all-done.refs_0_ = bf16[8,128,384]{2,1,0:T(8,128)(2,1)S(1)} async-done(((bf16[8,128,384]{2,1,0:T(8,128)(2,1)}), bf16[8,128,384]{2,1,0:T(8,128)(2,1)S(1)}, u32[]{:S(2)}, u32[]{:S(2)}) %all-to-all-start) | async-done | bytes 786464 | tf_op jit(solution)/shard_map/all_to_all | solution.py:408
  30.0 1.4 %collective-permute-start.4 = (bf16[8,128,128]{2,1,0:T(8,128)(2,1)S(1)}, bf16[8,128,128]{2,1,0:T(8,128)(2,1)S(1)}, u32[]{:S(2)}, u32[]{:S(2)}) collective-permute-start(bf16[8,128,128]{2,1,0:T(8,128)(2,1)S(1)} %get-tuple-element.35.refs_0_), channel_id=1, source_target_pairs={{0,1},{1,0},{2,3},{3,2},{4,5},{5,4},{6,7},{7,6},{8,9},{9,8},{10,11... | collective-permute-start | bytes 786440 | tf_op jit(solution)/shard_map/ppermute | solution.py:34
  31.6 0.3 collective-permute-start.5
  31.9 1.3 %collective-permute-start.6 = (bf16[4,128,256]{2,1,0:T(8,128)(2,1)S(1)}, bf16[4,128,256]{2,1,0:T(8,128)(2,1)S(1)}, u32[]{:S(2)}, u32[]{:S(2)}) collective-permute-start(bf16[4,128,256]{2,1,0:T(8,128)(2,1)S(1)} %get-tuple-element.37.refs_3_.refs_5_), channel_id=1, source_target_pairs={{0,48},{1,49},{2,50},{3,51},{4,52},{5,53},{6,54},{7,55},{8,56},{9,... | collective-permute-start | bytes 786440 | tf_op jit(solution)/shard_map/ppermute | solution.py:34
  33.1 2.8 %shard_map.108 = (f32[128,2048]{1,0:T(8,128)S(1)}, f32[1,2048]{1,0:T(1,128)S(1)}, f32[1,2048]{1,0:T(1,128)S(1)}, bf16[512,256]{1,0:T(8,128)(2,1)S(1)}) custom-call(bf16[8,128,128]{2,1,0:T(8,128)(2,1)S(1)} %get-tuple-element.35.refs_0_, bf16[8,128,128]{2,1,0:T(8,128)(2,1)S(1)} %collective-permute-done.4.refs_1_, ...), custom_call_target="tpu_custom_call" | custom-call | flops 4294967296 | bytes 2097152 | tf_op jit(solution)/shard_map/pallas_call | solution.py:67
  36.1 3.1 %collective-permute-start.13 = (bf16[512,256]{1,0:T(8,128)(2,1)S(1)}, bf16[512,256]{1,0:T(8,128)(2,1)S(1)}, u32[]{:S(2)}, u32[]{:S(2)}) collective-permute-start(bf16[512,256]{1,0:T(8,128)(2,1)S(1)} %get-tuple-element.52.refs_0_), channel_id=1, source_target_pairs={{0,8},{1,9},{2,10},{3,11},{4,12},{5,13},{6,14},{7,15},{8,0},{9,1},... | collective-permute-start | bytes 786440 | tf_op jit(solution)/shard_map/ppermute | solution.py:34
  39.2 1.1 collective-permute-done.6.refs_1_.refs_3_
  40.4 2.6 %collective-permute-start.9 = (bf16[4,128,256]{2,1,0:T(8,128)(2,1)S(1)}, bf16[4,128,256]{2,1,0:T(8,128)(2,1)S(1)}, u32[]{:S(2)}, u32[]{:S(2)}) collective-permute-start(bf16[4,128,256]{2,1,0:T(8,128)(2,1)S(1)} %get-tuple-element.41.refs_9_), channel_id=1, source_target_pairs={{0,16},{1,17},{2,18},{3,19},{4,20},{5,21},{6,22},{7,23},{8,24},{9,... | collective-permute-start | bytes 786440 | tf_op jit(solution)/shard_map/ppermute | solution.py:34
  43.0 4.0 %shard_map.110 = (f32[128,2048]{1,0:T(8,128)S(1)}, f32[1,2048]{1,0:T(1,128)S(1)}, f32[1,2048]{1,0:T(1,128)S(1)}, bf16[4,128,256]{2,1,0:T(8,128)(2,1)S(1)}, bf16[4,128,256]{2,1,0:T(8,128)(2,1)S(1)}) custom-call(bf16[8,128,128]{2,1,0:T(8,128)(2,1)S(1)} %get-tuple-element.35.refs_0_, ...), custom_call_target="tpu_custom_call", output_to_operand_aliasing={{0}: (6, {}), {1}: (7, {}), {2}: (8, {})} | custom-call | flops 3221225472 | bytes 4194304 | tf_op jit(solution)/shard_map/pallas_call | solution.py:67
  47.0 2.0 %collective-permute-start.14 = (bf16[512,256]{1,0:T(8,128)(2,1)S(1)}, bf16[512,256]{1,0:T(8,128)(2,1)S(1)}, u32[]{:S(2)}, u32[]{:S(2)}) collective-permute-start(bf16[512,256]{1,0:T(8,128)(2,1)S(1)} %get-tuple-element.52.refs_0_), channel_id=1, source_target_pairs={{0,12},{1,13},{2,14},{3,15},{4,0},{5,1},{6,2},{7,3},{8,4},{9,5},{1... | collective-permute-start | bytes 786440 | tf_op jit(solution)/shard_map/ppermute | solution.py:34
  49.0 1.4 %collective-permute-start.8 = (bf16[4,128,256]{2,1,0:T(8,128)(2,1)S(1)}, bf16[4,128,256]{2,1,0:T(8,128)(2,1)S(1)}, u32[]{:S(2)}, u32[]{:S(2)}) collective-permute-start(bf16[4,128,256]{2,1,0:T(8,128)(2,1)S(1)} %get-tuple-element.43), channel_id=1, source_target_pairs={{0,48},{1,49},{2,50},{3,51},{4,52},{5,53},{6,54},{7,55},{8,56},{9,... | collective-permute-start | bytes 786440 | tf_op jit(solution)/shard_map/ppermute | solution.py:34
  50.5 3.2 %shard_map.111 = (f32[128,2048]{1,0:T(8,128)S(1)}, f32[1,2048]{1,0:T(1,128)S(1)}, f32[1,2048]{1,0:T(1,128)S(1)}) custom-call(bf16[8,128,128]{2,1,0:T(8,128)(2,1)S(1)} %get-tuple-element.35.refs_0_, bf16[8,128,128]{2,1,0:T(8,128)(2,1)S(1)} %collective-permute-done.4.refs_1_, ...), custom_call_target="tpu_custom_call", output_to_operand_aliasing={{0}: (4, {}), {1}: (5, {}), {2}: (6, {})} | custom-call | flops 3221225472 | bytes 3145728 | tf_op jit(solution)/shard_map/pallas_call | solution.py:67
  53.7 1.3 %shard_map.112.refs_7_.refs_2_ = bf16[3,64,1024]{2,1,0:T(8,128)(2,1)S(1)} custom-call(s32[64,4]{1,0:T(8,128)S(1)} %copy.17.refs_0_.refs_3_, bf16[4,1024,1024]{2,1,0:T(8,128)(2,1)S(1)} %bitcast.2, f32[1,2048]{1,0:T(1,128)S(1)} %get-tuple-element.49.refs_2_.refs_5_), custom_call_target="tpu_custom_call" | custom-call | flops 402653184 | bytes 8388608 | tf_op jit(solution)/shard_map/pallas_call | solution.py:67
  55.0 0.5 collective-permute-done.8.refs_3_
  55.5 3.9 %shard_map.113 = (f32[128,1024]{1,0:T(8,128)S(1)}, bf16[160,1024]{1,0:T(8,128)(2,1)S(1)}, f32[8,1024]{1,0:T(8,128)S(1)}) custom-call(bf16[8,128,128]{2,1,0:T(8,128)(2,1)S(1)} %get-tuple-element.35.refs_0_, bf16[8,128,128]{2,1,0:T(8,128)(2,1)S(1)} %collective-permute-done.4.refs_1_, bf16[4,128,256]{2,1,0:T(8,128)(2,1)S(1)} %collective-permute-done.7.refs_2_, ...), custom_call_target="tpu_custom_call" | custom-call | flops 3221225472 | bytes 3145728 | tf_op jit(solution)/shard_map/pallas_call | solution.py:67
  59.4 3.6 %collective-permute-start.15 = (bf16[160,1024]{1,0:T(8,128)(2,1)S(1)}, bf16[160,1024]{1,0:T(8,128)(2,1)S(1)}, u32[]{:S(2)}, u32[]{:S(2)}) collective-permute-start(bf16[160,1024]{1,0:T(8,128)(2,1)S(1)} %get-tuple-element.54), channel_id=1, source_target_pairs={{0,1},{1,0},{2,3},{3,2},{4,5},{5,4},{6,7},{7,6},{8,9},{9,8},{10,11... | collective-permute-start | bytes 983048 | tf_op jit(solution)/shard_map/ppermute | solution.py:34
  63.1 1.3 %collective-permute-done.15.refs_1_.refs_4_ = bf16[160,1024]{1,0:T(8,128)(2,1)S(1)} collective-permute-done((bf16[160,1024]{1,0:T(8,128)(2,1)S(1)}, bf16[160,1024]{1,0:T(8,128)(2,1)S(1)}, u32[]{:S(2)}, u32[]{:S(2)}) %collective-permute-start.15) | collective-permute-done | bytes 327712 | tf_op jit(solution)/shard_map/ppermute | solution.py:34
  64.4 0.5 collective-permute-start.16
  64.8 0.2 shard_map.114
  65.0 10.7 %all_to_all.10.refs_0_ = bf16[8,128,128]{2,1,0:T(8,128)(2,1)S(1)} all-to-all(bf16[8,128,128]{2,1,0:T(8,128)(2,1)S(1)} %shard_map.114), channel_id=1, replica_groups=mesh['h'=2,'x'=4,'z'=4,'l'=2,'c'=2] {'h','z'}, dimensions={0} | all-to-all | bytes 524288 | tf_op jit(solution)/shard_map/all_to_all | solution.py:454
  75.7 0.6 shard_map.116
  76.3 0.7 copy-done.8
  77.0 0.4 collective-permute-start.17
  77.4 3.4 %collective-permute-done.17.refs_1_ = bf16[64,1024]{1,0:T(8,128)(2,1)S(1)} collective-permute-done((bf16[64,1024]{1,0:T(8,128)(2,1)S(1)}, bf16[64,1024]{1,0:T(8,128)(2,1)S(1)}, u32[]{:S(2)}, u32[]{:S(2)}) %collective-permute-start.17) | collective-permute-done | bytes 131104 | tf_op jit(solution)/shard_map/ppermute | solution.py:34
  80.8 0.6 copy-done.10
  81.5 17.4 %shard_map.117 = (f32[1,64]{1,0:T(1,128)}, bf16[64,1024]{1,0:T(8,128)(2,1)}) custom-call(f32[64,1024]{1,0:T(8,128)} %copy-done.8, bf16[64,1024]{1,0:T(8,128)(2,1)} %copy-done.10, bf16[3,64,1024]{2,1,0:T(8,128)(2,1)} %copy-done.5, s32[64,4]{1,0:T(8,128)} %copy-done.6, bf16[4,1024,1024]{2,1,0:T(8,128)(2,1)} %refs_4_.1, bf16[4,1024,1024]{2,1,0:T(8,128)(2,1)} %refs_5_.1), custom_call_target="tpu_custom_call" | custom-call | flops 12884901888 | bytes 17825792 | tf_op jit(solution)/shard_map/pallas_call | solution.py:67
  98.9 0.5 collective-permute-start.19
  99.4 3.5 %collective-permute-start.18 = (bf16[64,1024]{1,0:T(8,128)(2,1)}, bf16[64,1024]{1,0:T(8,128)(2,1)S(1)}, u32[]{:S(2)}, u32[]{:S(2)}) collective-permute-start(bf16[64,1024]{1,0:T(8,128)(2,1)} %get-tuple-element.59.refs_0_), channel_id=1, source_target_pairs={{0,1},{1,0},{2,3},{3,2},{4,5},{5,4},{6,7},{7,6},{8,9},{9,8},{10,11... | collective-permute-start | bytes 393224 | tf_op jit(solution)/shard_map/ppermute | solution.py:34
  102.9 0.2 collective-permute-done.19.refs_1_
  103.0 4.3 %collective-permute-start.20 = (bf16[64,1024]{1,0:T(8,128)(2,1)S(1)}, bf16[64,1024]{1,0:T(8,128)(2,1)S(1)}, u32[]{:S(2)}, u32[]{:S(2)}) collective-permute-start(bf16[64,1024]{1,0:T(8,128)(2,1)S(1)} %collective-permute-done.19.refs_1_), channel_id=1, source_target_pairs={{0,1},{1,0},{2,3},{3,2},{4,5},{5,4},{6,7},{7,6},{8,9},{9,8},{10,11... | collective-permute-start | bytes 393224 | tf_op jit(solution)/shard_map/ppermute | solution.py:34
  107.4 0.9 copy-done.7
  108.3 0.8 shard_map.118.refs_0_
  109.1 1.6 %shard_map.119 = bf16[256,1024]{1,0:T(8,128)(2,1)} custom-call(bf16[128,1024]{1,0:T(8,128)(2,1)S(1)} %shard_map.118.refs_0_, bf16[64,1024]{1,0:T(8,128)(2,1)S(1)} %collective-permute-done.19.refs_1_, bf16[64,1024]{1,0:T(8,128)(2,1)S(1)} %collective-permute-done.20.refs_2_, bf16[1024,1024]{1,0:T(8,128)(2,1)S(1)} %copy-done.1), custom_call_target="tpu_custom_call" | custom-call | flops 268435456 | bytes 3145728 | tf_op jit(solution)/shard_map/pallas_call | solution.py:67
  (42 shorter events, 0.7 us)
Async XLA Ops:
  0.6 30.9 %copy-start.9 = (s32[64,4]{0,1:T(4,128)S(1)}, s32[64,4]{0,1:T(4,128)}, u32[]{:S(2)}) copy-start(s32[64,4]{0,1:T(4,128)} %param.15) | copy-start | bytes 3076
  3.1 2.3 %collective-permute-start = (bf16[4,128,384]{2,1,0:T(8,128)(2,1)}, bf16[4,128,384]{2,1,0:T(8,128)(2,1)S(1)}, u32[]{:S(2)}, u32[]{:S(2)}) collective-permute-start(bf16[4,128,384]{2,1,0:T(8,128)(2,1)} %get-tuple-element.32), channel_id=1, source_target_pairs={{0,1},{1,0},{2,3},{3,2},{4,5},{5,4},{6,7},{7,6},{8,9},{9,8},{10,11... | collective-permute-start | bytes 1179656 | tf_op jit(solution)/shard_map/ppermute | solution.py:34
  3.9 13.7 %collective-permute-start.2 = (bf16[1024,256]{1,0:T(8,128)(2,1)}, bf16[1024,256]{1,0:T(8,128)(2,1)S(1)}, u32[]{:S(2)}, u32[]{:S(2)}) collective-permute-start(bf16[1024,256]{1,0:T(8,128)(2,1)} %get-tuple-element.34.refs_1_), channel_id=1, source_target_pairs={{0,2},{1,3},{2,0},{3,1},{4,6},{5,7},{6,4},{7,5},{8,10},{9,11},{10,... | collective-permute-start | bytes 1572872 | tf_op jit(solution)/shard_map/ppermute | solution.py:34
  6.2 23.6 %all-to-all-start = ((bf16[8,128,384]{2,1,0:T(8,128)(2,1)}), bf16[8,128,384]{2,1,0:T(8,128)(2,1)S(1)}, u32[]{:S(2)}, u32[]{:S(2)}) async-start(bf16[8,128,384]{2,1,0:T(8,128)(2,1)} %constant_dynamic-update-slice_fusion), calls=%async_computation | async-start | bytes 1572864 | tf_op jit(solution)/shard_map/all_to_all | solution.py:408
  13.9 8.5 %collective-permute-start.1 = (bf16[1024,256]{1,0:T(8,128)(2,1)}, bf16[1024,256]{1,0:T(8,128)(2,1)S(1)}, u32[]{:S(2)}, u32[]{:S(2)}) collective-permute-start(bf16[1024,256]{1,0:T(8,128)(2,1)} %get-tuple-element.34.refs_1_), channel_id=1, source_target_pairs={{0,1},{1,0},{2,3},{3,2},{4,5},{5,4},{6,7},{7,6},{8,9},{9,8},{10,11... | collective-permute-start | bytes 1572872 | tf_op jit(solution)/shard_map/ppermute | solution.py:34
  17.6 4.9 %collective-permute-start.3 = (bf16[1024,256]{1,0:T(8,128)(2,1)S(1)}, bf16[1024,256]{1,0:T(8,128)(2,1)S(1)}, u32[]{:S(2)}, u32[]{:S(2)}) collective-permute-start(bf16[1024,256]{1,0:T(8,128)(2,1)S(1)} %collective-permute-done.2.refs_3_), channel_id=1, source_target_pairs={{0,1},{1,0},{2,3},{3,2},{4,5},{5,4},{6,7},{7,6},{8,9},{9,8},{10,11... | collective-permute-start | bytes 1572872 | tf_op jit(solution)/shard_map/ppermute | solution.py:34
  18.9 1.6 %copy-start = (bf16[1024,1024]{1,0:T(8,128)(2,1)S(1)}, bf16[1024,1024]{1,0:T(8,128)(2,1)}, u32[]{:S(2)}) copy-start(bf16[1024,1024]{1,0:T(8,128)(2,1)} %refs_3_.4) | copy-start | bytes 6291460
  20.5 1.0 copy-start.3
  22.5 2.2 %copy-start.2 = (bf16[512,4096]{1,0:T(8,128)(2,1)S(1)}, bf16[512,4096]{1,0:T(8,128)(2,1)}, u32[]{:S(2)}) copy-start(bf16[512,4096]{1,0:T(8,128)(2,1)} %refs_0_.6) | copy-start | bytes 12582916
  24.7 1.0 copy-start.4
  30.0 3.2 %collective-permute-start.4 = (bf16[8,128,128]{2,1,0:T(8,128)(2,1)S(1)}, bf16[8,128,128]{2,1,0:T(8,128)(2,1)S(1)}, u32[]{:S(2)}, u32[]{:S(2)}) collective-permute-start(bf16[8,128,128]{2,1,0:T(8,128)(2,1)S(1)} %get-tuple-element.35.refs_0_), channel_id=1, source_target_pairs={{0,1},{1,0},{2,3},{3,2},{4,5},{5,4},{6,7},{7,6},{8,9},{9,8},{10,11... | collective-permute-start | bytes 786440 | tf_op jit(solution)/shard_map/ppermute | solution.py:34
  31.4 15.6 %collective-permute-start.11 = (bf16[128,1024]{1,0:T(8,128)(2,1)S(1)}, bf16[128,1024]{1,0:T(8,128)(2,1)S(1)}, u32[]{:S(2)}, u32[]{:S(2)}) collective-permute-start(bf16[128,1024]{1,0:T(8,128)(2,1)S(1)} %get-tuple-element.51), channel_id=1, source_target_pairs={{0,1},{1,0},{2,3},{3,2},{4,5},{5,4},{6,7},{7,6},{8,9},{9,8},{10,11... | collective-permute-start | bytes 786440 | tf_op jit(solution)/shard_map/ppermute | solution.py:34
  31.6 22.1 %copy-start.6 = (s32[64,4]{1,0:T(8,128)}, s32[64,4]{1,0:T(8,128)S(1)}, u32[]{:S(2)}) copy-start(s32[64,4]{1,0:T(8,128)S(1)} %copy.17.refs_0_.refs_3_) | copy-start | bytes 3076
  31.6 7.6 %collective-permute-start.5 = (bf16[4,128,256]{2,1,0:T(8,128)(2,1)S(1)}, bf16[4,128,256]{2,1,0:T(8,128)(2,1)S(1)}, u32[]{:S(2)}, u32[]{:S(2)}) collective-permute-start(bf16[4,128,256]{2,1,0:T(8,128)(2,1)S(1)} %get-tuple-element.36.refs_2_.refs_4_), channel_id=1, source_target_pairs={{0,16},{1,17},{2,18},{3,19},{4,20},{5,21},{6,22},{7,23},{8,24},{9,... | collective-permute-start | bytes 786440 | tf_op jit(solution)/shard_map/ppermute | solution.py:34
  31.9 8.4 %collective-permute-start.6 = (bf16[4,128,256]{2,1,0:T(8,128)(2,1)S(1)}, bf16[4,128,256]{2,1,0:T(8,128)(2,1)S(1)}, u32[]{:S(2)}, u32[]{:S(2)}) collective-permute-start(bf16[4,128,256]{2,1,0:T(8,128)(2,1)S(1)} %get-tuple-element.37.refs_3_.refs_5_), channel_id=1, source_target_pairs={{0,48},{1,49},{2,50},{3,51},{4,52},{5,53},{6,54},{7,55},{8,56},{9,... | collective-permute-start | bytes 786440 | tf_op jit(solution)/shard_map/ppermute | solution.py:34
  36.0 19.6 %collective-permute-start.12 = (bf16[512,256]{1,0:T(8,128)(2,1)S(1)}, bf16[512,256]{1,0:T(8,128)(2,1)S(1)}, u32[]{:S(2)}, u32[]{:S(2)}) collective-permute-start(bf16[512,256]{1,0:T(8,128)(2,1)S(1)} %get-tuple-element.52.refs_0_), channel_id=1, source_target_pairs={{0,4},{1,5},{2,6},{3,7},{4,8},{5,9},{6,10},{7,11},{8,12},{9,13},{1... | collective-permute-start | bytes 786440 | tf_op jit(solution)/shard_map/ppermute | solution.py:34
  36.1 19.5 %collective-permute-start.13 = (bf16[512,256]{1,0:T(8,128)(2,1)S(1)}, bf16[512,256]{1,0:T(8,128)(2,1)S(1)}, u32[]{:S(2)}, u32[]{:S(2)}) collective-permute-start(bf16[512,256]{1,0:T(8,128)(2,1)S(1)} %get-tuple-element.52.refs_0_), channel_id=1, source_target_pairs={{0,8},{1,9},{2,10},{3,11},{4,12},{5,13},{6,14},{7,15},{8,0},{9,1},... | collective-permute-start | bytes 786440 | tf_op jit(solution)/shard_map/ppermute | solution.py:34
  40.3 8.7 %collective-permute-start.10 = (bf16[4,128,256]{2,1,0:T(8,128)(2,1)S(1)}, bf16[4,128,256]{2,1,0:T(8,128)(2,1)S(1)}, u32[]{:S(2)}, u32[]{:S(2)}) collective-permute-start(bf16[4,128,256]{2,1,0:T(8,128)(2,1)S(1)} %get-tuple-element.44), channel_id=1, source_target_pairs={{0,48},{1,49},{2,50},{3,51},{4,52},{5,53},{6,54},{7,55},{8,56},{9,... | collective-permute-start | bytes 786440 | tf_op jit(solution)/shard_map/ppermute | solution.py:34
  40.4 8.6 %collective-permute-start.9 = (bf16[4,128,256]{2,1,0:T(8,128)(2,1)S(1)}, bf16[4,128,256]{2,1,0:T(8,128)(2,1)S(1)}, u32[]{:S(2)}, u32[]{:S(2)}) collective-permute-start(bf16[4,128,256]{2,1,0:T(8,128)(2,1)S(1)} %get-tuple-element.41.refs_9_), channel_id=1, source_target_pairs={{0,16},{1,17},{2,18},{3,19},{4,20},{5,21},{6,22},{7,23},{8,24},{9,... | collective-permute-start | bytes 786440 | tf_op jit(solution)/shard_map/ppermute | solution.py:34
  43.0 10.7 %slice-start = ((s8[8388608]{0:T(1024)(128)(4,1)}), s8[4194304]{0:T(1024)(128)(4,1)S(1)}, s32[]{:S(2)}) async-start(s8[8388608]{0:T(1024)(128)(4,1)} %bitcast.1), calls=%async_computation.2 | async-start | bytes 8388608
  47.0 8.5 %collective-permute-start.14 = (bf16[512,256]{1,0:T(8,128)(2,1)S(1)}, bf16[512,256]{1,0:T(8,128)(2,1)S(1)}, u32[]{:S(2)}, u32[]{:S(2)}) collective-permute-start(bf16[512,256]{1,0:T(8,128)(2,1)S(1)} %get-tuple-element.52.refs_0_), channel_id=1, source_target_pairs={{0,12},{1,13},{2,14},{3,15},{4,0},{5,1},{6,2},{7,3},{8,4},{9,5},{1... | collective-permute-start | bytes 786440 | tf_op jit(solution)/shard_map/ppermute | solution.py:34
  49.0 6.0 %collective-permute-start.7 = (bf16[4,128,256]{2,1,0:T(8,128)(2,1)S(1)}, bf16[4,128,256]{2,1,0:T(8,128)(2,1)S(1)}, u32[]{:S(2)}, u32[]{:S(2)}) collective-permute-start(bf16[4,128,256]{2,1,0:T(8,128)(2,1)S(1)} %get-tuple-element.42), channel_id=1, source_target_pairs={{0,16},{1,17},{2,18},{3,19},{4,20},{5,21},{6,22},{7,23},{8,24},{9,... | collective-permute-start | bytes 786440 | tf_op jit(solution)/shard_map/ppermute | solution.py:34
  49.0 4.7 %slice-start.1 = ((s8[8388608]{0:T(1024)(128)(4,1)}), s8[4194304]{0:T(1024)(128)(4,1)S(1)}, s32[]{:S(2)}) async-start(s8[8388608]{0:T(1024)(128)(4,1)} %bitcast.1), calls=%async_computation.3 | async-start | bytes 8388608
  49.0 6.5 %collective-permute-start.8 = (bf16[4,128,256]{2,1,0:T(8,128)(2,1)S(1)}, bf16[4,128,256]{2,1,0:T(8,128)(2,1)S(1)}, u32[]{:S(2)}, u32[]{:S(2)}) collective-permute-start(bf16[4,128,256]{2,1,0:T(8,128)(2,1)S(1)} %get-tuple-element.43), channel_id=1, source_target_pairs={{0,48},{1,49},{2,50},{3,51},{4,52},{5,53},{6,54},{7,55},{8,56},{9,... | collective-permute-start | bytes 786440 | tf_op jit(solution)/shard_map/ppermute | solution.py:34
  55.0 21.3 %copy-start.5 = (bf16[3,64,1024]{2,1,0:T(8,128)(2,1)}, bf16[3,64,1024]{2,1,0:T(8,128)(2,1)S(1)}, u32[]{:S(2)}) copy-start(bf16[3,64,1024]{2,1,0:T(8,128)(2,1)S(1)} %shard_map.112.refs_7_.refs_2_) | copy-start | bytes 1179652
  59.4 4.9 %collective-permute-start.15 = (bf16[160,1024]{1,0:T(8,128)(2,1)S(1)}, bf16[160,1024]{1,0:T(8,128)(2,1)S(1)}, u32[]{:S(2)}, u32[]{:S(2)}) collective-permute-start(bf16[160,1024]{1,0:T(8,128)(2,1)S(1)} %get-tuple-element.54), channel_id=1, source_target_pairs={{0,1},{1,0},{2,3},{3,2},{4,5},{5,4},{6,7},{7,6},{8,9},{9,8},{10,11... | collective-permute-start | bytes 983048 | tf_op jit(solution)/shard_map/ppermute | solution.py:34
  64.4 11.3 %collective-permute-start.16 = (bf16[4,512,256]{2,1,0:T(8,128)(2,1)S(1)}, bf16[4,512,256]{2,1,0:T(8,128)(2,1)S(1)}, u32[]{:S(2)}, u32[]{:S(2)}) collective-permute-start(bf16[4,512,256]{2,1,0:T(8,128)(2,1)S(1)} %shard_map.115.refs_1_), channel_id=1, source_target_pairs={{0,1},{1,0},{2,3},{3,2},{4,5},{5,4},{6,7},{7,6},{8,9},{9,8},{10,11... | collective-permute-start | bytes 3145736 | tf_op jit(solution)/shard_map/ppermute | solution.py:34
  76.3 0.7 copy-start.8
  77.0 3.8 %collective-permute-start.17 = (bf16[64,1024]{1,0:T(8,128)(2,1)S(1)}, bf16[64,1024]{1,0:T(8,128)(2,1)S(1)}, u32[]{:S(2)}, u32[]{:S(2)}) collective-permute-start(bf16[64,1024]{1,0:T(8,128)(2,1)S(1)} %get-tuple-element.57), channel_id=1, source_target_pairs={{0,2},{1,3},{2,0},{3,1},{4,6},{5,7},{6,4},{7,5},{8,10},{9,11},{10,... | collective-permute-start | bytes 393224 | tf_op jit(solution)/shard_map/ppermute | solution.py:34
  80.8 0.6 copy-start.10
  81.5 25.9 %copy-start.1 = (bf16[1024,1024]{1,0:T(8,128)(2,1)S(1)}, bf16[1024,1024]{1,0:T(8,128)(2,1)}, u32[]{:S(2)}) copy-start(bf16[1024,1024]{1,0:T(8,128)(2,1)} %refs_3_.4) | copy-start | bytes 6291460
  98.9 4.1 %collective-permute-start.19 = (bf16[64,1024]{1,0:T(8,128)(2,1)}, bf16[64,1024]{1,0:T(8,128)(2,1)S(1)}, u32[]{:S(2)}, u32[]{:S(2)}) collective-permute-start(bf16[64,1024]{1,0:T(8,128)(2,1)} %get-tuple-element.59.refs_0_), channel_id=1, source_target_pairs={{0,2},{1,3},{2,0},{3,1},{4,6},{5,7},{6,4},{7,5},{8,10},{9,11},{10,... | collective-permute-start | bytes 393224 | tf_op jit(solution)/shard_map/ppermute | solution.py:34
  99.4 8.0 %collective-permute-start.18 = (bf16[64,1024]{1,0:T(8,128)(2,1)}, bf16[64,1024]{1,0:T(8,128)(2,1)S(1)}, u32[]{:S(2)}, u32[]{:S(2)}) collective-permute-start(bf16[64,1024]{1,0:T(8,128)(2,1)} %get-tuple-element.59.refs_0_), channel_id=1, source_target_pairs={{0,1},{1,0},{2,3},{3,2},{4,5},{5,4},{6,7},{7,6},{8,9},{9,8},{10,11... | collective-permute-start | bytes 393224 | tf_op jit(solution)/shard_map/ppermute | solution.py:34
  103.0 6.1 %collective-permute-start.20 = (bf16[64,1024]{1,0:T(8,128)(2,1)S(1)}, bf16[64,1024]{1,0:T(8,128)(2,1)S(1)}, u32[]{:S(2)}, u32[]{:S(2)}) collective-permute-start(bf16[64,1024]{1,0:T(8,128)(2,1)S(1)} %collective-permute-done.19.refs_1_), channel_id=1, source_target_pairs={{0,1},{1,0},{2,3},{3,2},{4,5},{5,4},{6,7},{7,6},{8,9},{9,8},{10,11... | collective-permute-start | bytes 393224 | tf_op jit(solution)/shard_map/ppermute | solution.py:34
  107.4 0.9 copy-start.7

commit v3 on v2

--- a/solution.py
+++ b/solution.py
@@ -341,22 +341,24 @@
     out = stream + update
     r2 = rms(out)
     final = (out * r2).astype(BF16)
-    loss = jnp.zeros((n, 1), F32)
-    dfinal = []
     scale = 3.0 / 1024**0.5
-    vocab = lax.broadcasted_iota(jnp.int32, (n, 1024), 1)
+    logits = []
     for i in range(4):
         copies[4 + i].wait()
-        logits = dot_nt(at(final, i), tab[i]) * scale
-        top = jnp.max(logits, -1, keepdims=True)
-        e = jnp.exp(logits - top)
-        total = jnp.sum(e, -1, keepdims=True)
-        hit = vocab == codes_ref[:, i : i + 1]
-        picked = jnp.sum(jnp.where(hit, logits, 0.0), -1, keepdims=True)
-        loss = loss + top + jnp.log(total) - picked
-        dlogits = (e * (1.0 / total) - hit.astype(F32)).astype(BF16)
-        dfinal.append(dot_nn(dlogits, tab[i]) * scale)
+    for i in range(4):
+        logits.append(dot_nt(at(final, i), tab[i]))
+    logits = jnp.concatenate(logits, 0) * scale
+    top = jnp.max(logits, -1, keepdims=True)
+    e = jnp.exp(logits - top)
+    total = jnp.sum(e, -1, keepdims=True)
+    vocab = lax.broadcasted_iota(jnp.int32, (4 * n, 1024), 1)
+    hit = vocab == jnp.concatenate([codes_ref[:, i : i + 1] for i in range(4)], 0)
+    picked = jnp.sum(jnp.where(hit, logits, 0.0), -1, keepdims=True)
+    losses = top + jnp.log(total) - picked
+    loss = functools.reduce(jnp.add, [at(losses, i) for i in range(4)])
     loss_ref[...] = jnp.broadcast_to(loss, (n, 128)).T[0:1, :]
+    dlogits = (e * (1.0 / total) - hit.astype(F32)).astype(BF16)
+    dfinal = [dot_nn(at(dlogits, i), tab[i]) * scale for i in range(4)]
     dfinal = jnp.concatenate(dfinal, 0)
     dout = r2 * (dfinal - out * (r2 * r2) * jnp.mean(dfinal * out, -1, keepdims=True))
     dmixed = dot_nt(dout.astype(BF16), wt[3])

time: 111 us -> 110 us (level)
  Pallas kernels: 40.6 us -> 39.2 us
    pallas_call x16, Pallas kernels: 40.6 us -> 39.2 us  [call(): pl.pallas_call(run, out_shape=out_shape, in_specs=in_specs, out_specs=out...]
where the time goes in v3:
time: 110 us; the launch traced here: 109 us
  Pallas kernels  39.2 us (36%)
  starting transfers between devices  36.9 us (34%)
  waiting for transfers between devices  12.6 us (11%)
  blocking collectives  10.7 us (10%)
  local copies, waits for them, and re-layouts  9.02 us (8%)
    pallas_call x16, Pallas kernels, call(): pl.pallas_call(run, out_shape=out_shape, in_specs=in_specs, out_specs=out...  39.2 us
    ppermute x21, starting transfers between devices, move(): return lax.ppermute(array, AXES, pairs)  29.3 us
    all_to_all x1, blocking collectives, per_device(): attended = lax.all_to_all(attended, ('h', 'z'), 0, 0, tiled=True)  10.7 us
    ppermute x21, waiting for transfers between devices, move(): return lax.ppermute(array, AXES, pairs)  9.71 us
    unnamed x27, local copies, waits for them, and re-layouts  8.24 us
    all_to_all x1, starting transfers between devices, per_device(): mine = lax.all_to_all(full, ('h', 'z'), 0, 0, tiled=True)  7.66 us
    all_to_all x1, waiting for transfers between devices, per_device(): mine = lax.all_to_all(full, ('h', 'z'), 0, 0, tiled=True)  2.89 us
  transfers between devices with their start and end apart: 22, of which 8 were waited for; matrix products, arithmetic and copies ran while one was open for 1% of the time, Pallas kernels for 13%

profile of v3, /device:TPU:7, one launch (start us, length us, event | category | flops | bytes accessed | tf_op | source)
XLA Modules:
  0.0 109.4 jit_solution(1723447892685875547)
XLA Ops:
  0.6 2.5 %shard_map.104 = (bf16[8,128,384]{2,1,0:T(8,128)(2,1)}, bf16[4,128,384]{2,1,0:T(8,128)(2,1)}, bf16[1024,256]{1,0:T(8,128)(2,1)}) custom-call(bf16[256,512]{1,0:T(8,128)(2,1)} %refs_0_.4, bf16[256,512]{1,0:T(8,128)(2,1)} %refs_1_.3, bf16[256,512]{1,0:T(8,128)(2,1)} %refs_2_.2, bf16[1024,1024]{1,0:T(8,128)(2,1)} %refs_3_.4), custom_call_target="tpu_custom_call" | custom-call | bytes 3145728 | tf_op jit(solution)/shard_map/pallas_call | solution.py:67
  3.1 0.8 collective-permute-start
  3.9 1.3 %collective-permute-start.2 = (bf16[1024,256]{1,0:T(8,128)(2,1)}, bf16[1024,256]{1,0:T(8,128)(2,1)S(1)}, u32[]{:S(2)}, u32[]{:S(2)}) collective-permute-start(bf16[1024,256]{1,0:T(8,128)(2,1)} %get-tuple-element.34.refs_1_), channel_id=1, source_target_pairs={{0,2},{1,3},{2,0},{3,1},{4,6},{5,7},{6,4},{7,5},{8,10},{9,11},{10,... | collective-permute-start | bytes 1572872 | tf_op jit(solution)/shard_map/ppermute | solution.py:34
  5.2 0.2 collective-permute-done
  5.5 0.8 constant_dynamic-update-slice_fusion
  6.2 7.7 %all-to-all-start = ((bf16[8,128,384]{2,1,0:T(8,128)(2,1)}), bf16[8,128,384]{2,1,0:T(8,128)(2,1)S(1)}, u32[]{:S(2)}, u32[]{:S(2)}) async-start(bf16[8,128,384]{2,1,0:T(8,128)(2,1)} %constant_dynamic-update-slice_fusion), calls=%async_computation | async-start | bytes 1572864 | tf_op jit(solution)/shard_map/all_to_all | solution.py:410
  13.9 0.7 collective-permute-start.1
  14.6 3.0 %collective-permute-done.2.refs_3_ = bf16[1024,256]{1,0:T(8,128)(2,1)S(1)} collective-permute-done((bf16[1024,256]{1,0:T(8,128)(2,1)}, bf16[1024,256]{1,0:T(8,128)(2,1)S(1)}, u32[]{:S(2)}, u32[]{:S(2)}) %collective-permute-start.2) | collective-permute-done | bytes 524320 | tf_op jit(solution)/shard_map/ppermute | solution.py:34
  17.6 1.3 %collective-permute-start.3 = (bf16[1024,256]{1,0:T(8,128)(2,1)S(1)}, bf16[1024,256]{1,0:T(8,128)(2,1)S(1)}, u32[]{:S(2)}, u32[]{:S(2)}) collective-permute-start(bf16[1024,256]{1,0:T(8,128)(2,1)S(1)} %collective-permute-done.2.refs_3_), channel_id=1, source_target_pairs={{0,1},{1,0},{2,3},{3,2},{4,5},{5,4},{6,7},{7,6},{8,9},{9,8},{10,11... | collective-permute-start | bytes 1572872 | tf_op jit(solution)/shard_map/ppermute | solution.py:34
  18.9 1.6 %copy-done = bf16[1024,1024]{1,0:T(8,128)(2,1)S(1)} copy-done((bf16[1024,1024]{1,0:T(8,128)(2,1)S(1)}, bf16[1024,1024]{1,0:T(8,128)(2,1)}, u32[]{:S(2)}) %copy-start) | copy-done | bytes 2097176
  20.5 1.0 copy-done.3
  21.6 0.9 shard_map.105
  22.5 2.2 %copy-done.2 = bf16[512,4096]{1,0:T(8,128)(2,1)S(1)} copy-done((bf16[512,4096]{1,0:T(8,128)(2,1)S(1)}, bf16[512,4096]{1,0:T(8,128)(2,1)}, u32[]{:S(2)}) %copy-start.2) | copy-done | bytes 4194328
  24.7 1.0 copy-done.4
  25.7 1.2 %shard_map.106.refs_2_.refs_4_ = bf16[512,256]{1,0:T(8,128)(2,1)S(1)} custom-call(bf16[512,4096]{1,0:T(8,128)(2,1)S(1)} %copy-done.2, bf16[1024,256]{1,0:T(8,128)(2,1)S(1)} %copy-done.4, bf16[1024,256]{1,0:T(8,128)(2,1)S(1)} %collective-permute-done.1.refs_2_, bf16[1024,256]{1,0:T(8,128)(2,1)S(1)} %collective-permute-done.2.refs_3_, ...), custom_call_target="tpu_custom_call" | custom-call | flops 1073741824 | bytes 6291456 | tf_op jit(solution)/shard_map/pallas_call | solution.py:67
  27.0 2.9 %all-to-all-done.refs_0_ = bf16[8,128,384]{2,1,0:T(8,128)(2,1)S(1)} async-done(((bf16[8,128,384]{2,1,0:T(8,128)(2,1)}), bf16[8,128,384]{2,1,0:T(8,128)(2,1)S(1)}, u32[]{:S(2)}, u32[]{:S(2)}) %all-to-all-start) | async-done | bytes 786464 | tf_op jit(solution)/shard_map/all_to_all | solution.py:410
  30.0 1.4 %collective-permute-start.4 = (bf16[8,128,128]{2,1,0:T(8,128)(2,1)S(1)}, bf16[8,128,128]{2,1,0:T(8,128)(2,1)S(1)}, u32[]{:S(2)}, u32[]{:S(2)}) collective-permute-start(bf16[8,128,128]{2,1,0:T(8,128)(2,1)S(1)} %get-tuple-element.35.refs_0_), channel_id=1, source_target_pairs={{0,1},{1,0},{2,3},{3,2},{4,5},{5,4},{6,7},{7,6},{8,9},{9,8},{10,11... | collective-permute-start | bytes 786440 | tf_op jit(solution)/shard_map/ppermute | solution.py:34
  31.6 0.3 collective-permute-start.5
  31.9 1.3 %collective-permute-start.6 = (bf16[4,128,256]{2,1,0:T(8,128)(2,1)S(1)}, bf16[4,128,256]{2,1,0:T(8,128)(2,1)S(1)}, u32[]{:S(2)}, u32[]{:S(2)}) collective-permute-start(bf16[4,128,256]{2,1,0:T(8,128)(2,1)S(1)} %get-tuple-element.37.refs_3_.refs_5_), channel_id=1, source_target_pairs={{0,48},{1,49},{2,50},{3,51},{4,52},{5,53},{6,54},{7,55},{8,56},{9,... | collective-permute-start | bytes 786440 | tf_op jit(solution)/shard_map/ppermute | solution.py:34
  33.1 2.8 %shard_map.108 = (f32[128,2048]{1,0:T(8,128)S(1)}, f32[1,2048]{1,0:T(1,128)S(1)}, f32[1,2048]{1,0:T(1,128)S(1)}, bf16[512,256]{1,0:T(8,128)(2,1)S(1)}) custom-call(bf16[8,128,128]{2,1,0:T(8,128)(2,1)S(1)} %get-tuple-element.35.refs_0_, bf16[8,128,128]{2,1,0:T(8,128)(2,1)S(1)} %collective-permute-done.4.refs_1_, ...), custom_call_target="tpu_custom_call" | custom-call | flops 4294967296 | bytes 2097152 | tf_op jit(solution)/shard_map/pallas_call | solution.py:67
  36.1 3.1 %collective-permute-start.13 = (bf16[512,256]{1,0:T(8,128)(2,1)S(1)}, bf16[512,256]{1,0:T(8,128)(2,1)S(1)}, u32[]{:S(2)}, u32[]{:S(2)}) collective-permute-start(bf16[512,256]{1,0:T(8,128)(2,1)S(1)} %get-tuple-element.52.refs_0_), channel_id=1, source_target_pairs={{0,8},{1,9},{2,10},{3,11},{4,12},{5,13},{6,14},{7,15},{8,0},{9,1},... | collective-permute-start | bytes 786440 | tf_op jit(solution)/shard_map/ppermute | solution.py:34
  39.2 1.1 collective-permute-done.6.refs_1_.refs_3_
  40.4 2.6 %collective-permute-start.9 = (bf16[4,128,256]{2,1,0:T(8,128)(2,1)S(1)}, bf16[4,128,256]{2,1,0:T(8,128)(2,1)S(1)}, u32[]{:S(2)}, u32[]{:S(2)}) collective-permute-start(bf16[4,128,256]{2,1,0:T(8,128)(2,1)S(1)} %get-tuple-element.41.refs_9_), channel_id=1, source_target_pairs={{0,16},{1,17},{2,18},{3,19},{4,20},{5,21},{6,22},{7,23},{8,24},{9,... | collective-permute-start | bytes 786440 | tf_op jit(solution)/shard_map/ppermute | solution.py:34
  43.0 4.0 %shard_map.110 = (f32[128,2048]{1,0:T(8,128)S(1)}, f32[1,2048]{1,0:T(1,128)S(1)}, f32[1,2048]{1,0:T(1,128)S(1)}, bf16[4,128,256]{2,1,0:T(8,128)(2,1)S(1)}, bf16[4,128,256]{2,1,0:T(8,128)(2,1)S(1)}) custom-call(bf16[8,128,128]{2,1,0:T(8,128)(2,1)S(1)} %get-tuple-element.35.refs_0_, ...), custom_call_target="tpu_custom_call", output_to_operand_aliasing={{0}: (6, {}), {1}: (7, {}), {2}: (8, {})} | custom-call | flops 3221225472 | bytes 4194304 | tf_op jit(solution)/shard_map/pallas_call | solution.py:67
  47.0 2.0 %collective-permute-start.14 = (bf16[512,256]{1,0:T(8,128)(2,1)S(1)}, bf16[512,256]{1,0:T(8,128)(2,1)S(1)}, u32[]{:S(2)}, u32[]{:S(2)}) collective-permute-start(bf16[512,256]{1,0:T(8,128)(2,1)S(1)} %get-tuple-element.52.refs_0_), channel_id=1, source_target_pairs={{0,12},{1,13},{2,14},{3,15},{4,0},{5,1},{6,2},{7,3},{8,4},{9,5},{1... | collective-permute-start | bytes 786440 | tf_op jit(solution)/shard_map/ppermute | solution.py:34
  49.0 1.4 %collective-permute-start.8 = (bf16[4,128,256]{2,1,0:T(8,128)(2,1)S(1)}, bf16[4,128,256]{2,1,0:T(8,128)(2,1)S(1)}, u32[]{:S(2)}, u32[]{:S(2)}) collective-permute-start(bf16[4,128,256]{2,1,0:T(8,128)(2,1)S(1)} %get-tuple-element.43), channel_id=1, source_target_pairs={{0,48},{1,49},{2,50},{3,51},{4,52},{5,53},{6,54},{7,55},{8,56},{9,... | collective-permute-start | bytes 786440 | tf_op jit(solution)/shard_map/ppermute | solution.py:34
  50.5 3.2 %shard_map.111 = (f32[128,2048]{1,0:T(8,128)S(1)}, f32[1,2048]{1,0:T(1,128)S(1)}, f32[1,2048]{1,0:T(1,128)S(1)}) custom-call(bf16[8,128,128]{2,1,0:T(8,128)(2,1)S(1)} %get-tuple-element.35.refs_0_, bf16[8,128,128]{2,1,0:T(8,128)(2,1)S(1)} %collective-permute-done.4.refs_1_, ...), custom_call_target="tpu_custom_call", output_to_operand_aliasing={{0}: (4, {}), {1}: (5, {}), {2}: (6, {})} | custom-call | flops 3221225472 | bytes 3145728 | tf_op jit(solution)/shard_map/pallas_call | solution.py:67
  53.7 1.3 %shard_map.112.refs_7_.refs_2_ = bf16[3,64,1024]{2,1,0:T(8,128)(2,1)S(1)} custom-call(s32[64,4]{1,0:T(8,128)S(1)} %copy.17.refs_0_.refs_3_, bf16[4,1024,1024]{2,1,0:T(8,128)(2,1)S(1)} %bitcast.2, f32[1,2048]{1,0:T(1,128)S(1)} %get-tuple-element.49.refs_2_.refs_5_), custom_call_target="tpu_custom_call" | custom-call | flops 402653184 | bytes 8388608 | tf_op jit(solution)/shard_map/pallas_call | solution.py:67
  55.0 0.5 collective-permute-done.8.refs_3_
  55.5 3.9 %shard_map.113 = (f32[128,1024]{1,0:T(8,128)S(1)}, bf16[160,1024]{1,0:T(8,128)(2,1)S(1)}, f32[8,1024]{1,0:T(8,128)S(1)}) custom-call(bf16[8,128,128]{2,1,0:T(8,128)(2,1)S(1)} %get-tuple-element.35.refs_0_, bf16[8,128,128]{2,1,0:T(8,128)(2,1)S(1)} %collective-permute-done.4.refs_1_, bf16[4,128,256]{2,1,0:T(8,128)(2,1)S(1)} %collective-permute-done.7.refs_2_, ...), custom_call_target="tpu_custom_call" | custom-call | flops 3221225472 | bytes 3145728 | tf_op jit(solution)/shard_map/pallas_call | solution.py:67
  59.4 3.6 %collective-permute-start.15 = (bf16[160,1024]{1,0:T(8,128)(2,1)S(1)}, bf16[160,1024]{1,0:T(8,128)(2,1)S(1)}, u32[]{:S(2)}, u32[]{:S(2)}) collective-permute-start(bf16[160,1024]{1,0:T(8,128)(2,1)S(1)} %get-tuple-element.54), channel_id=1, source_target_pairs={{0,1},{1,0},{2,3},{3,2},{4,5},{5,4},{6,7},{7,6},{8,9},{9,8},{10,11... | collective-permute-start | bytes 983048 | tf_op jit(solution)/shard_map/ppermute | solution.py:34
  63.1 1.3 %collective-permute-done.15.refs_1_.refs_4_ = bf16[160,1024]{1,0:T(8,128)(2,1)S(1)} collective-permute-done((bf16[160,1024]{1,0:T(8,128)(2,1)S(1)}, bf16[160,1024]{1,0:T(8,128)(2,1)S(1)}, u32[]{:S(2)}, u32[]{:S(2)}) %collective-permute-start.15) | collective-permute-done | bytes 327712 | tf_op jit(solution)/shard_map/ppermute | solution.py:34
  64.4 0.5 collective-permute-start.16
  64.8 0.2 shard_map.114
  65.0 10.7 %all_to_all.10.refs_0_ = bf16[8,128,128]{2,1,0:T(8,128)(2,1)S(1)} all-to-all(bf16[8,128,128]{2,1,0:T(8,128)(2,1)S(1)} %shard_map.114), channel_id=1, replica_groups=mesh['h'=2,'x'=4,'z'=4,'l'=2,'c'=2] {'h','z'}, dimensions={0} | all-to-all | bytes 524288 | tf_op jit(solution)/shard_map/all_to_all | solution.py:456
  75.7 0.6 shard_map.116
  76.3 0.7 copy-done.8
  77.0 0.4 collective-permute-start.17
  77.4 3.4 %collective-permute-done.17.refs_1_ = bf16[64,1024]{1,0:T(8,128)(2,1)S(1)} collective-permute-done((bf16[64,1024]{1,0:T(8,128)(2,1)S(1)}, bf16[64,1024]{1,0:T(8,128)(2,1)S(1)}, u32[]{:S(2)}, u32[]{:S(2)}) %collective-permute-start.17) | collective-permute-done | bytes 131104 | tf_op jit(solution)/shard_map/ppermute | solution.py:34
  80.8 0.6 copy-done.10
  81.5 16.1 %shard_map.117 = (f32[1,64]{1,0:T(1,128)}, bf16[64,1024]{1,0:T(8,128)(2,1)}) custom-call(f32[64,1024]{1,0:T(8,128)} %copy-done.8, bf16[64,1024]{1,0:T(8,128)(2,1)} %copy-done.10, bf16[3,64,1024]{2,1,0:T(8,128)(2,1)} %copy-done.5, s32[64,4]{1,0:T(8,128)} %copy-done.6, bf16[4,1024,1024]{2,1,0:T(8,128)(2,1)} %refs_4_.1, bf16[4,1024,1024]{2,1,0:T(8,128)(2,1)} %refs_5_.1), custom_call_target="tpu_custom_call" | custom-call | flops 12884901888 | bytes 17825792 | tf_op jit(solution)/shard_map/pallas_call | solution.py:67
  97.6 0.5 collective-permute-start.19
  98.0 3.5 %collective-permute-start.18 = (bf16[64,1024]{1,0:T(8,128)(2,1)}, bf16[64,1024]{1,0:T(8,128)(2,1)S(1)}, u32[]{:S(2)}, u32[]{:S(2)}) collective-permute-start(bf16[64,1024]{1,0:T(8,128)(2,1)} %get-tuple-element.59.refs_0_), channel_id=1, source_target_pairs={{0,1},{1,0},{2,3},{3,2},{4,5},{5,4},{6,7},{7,6},{8,9},{9,8},{10,11... | collective-permute-start | bytes 393224 | tf_op jit(solution)/shard_map/ppermute | solution.py:34
  101.5 0.2 collective-permute-done.19.refs_1_
  101.7 4.3 %collective-permute-start.20 = (bf16[64,1024]{1,0:T(8,128)(2,1)S(1)}, bf16[64,1024]{1,0:T(8,128)(2,1)S(1)}, u32[]{:S(2)}, u32[]{:S(2)}) collective-permute-start(bf16[64,1024]{1,0:T(8,128)(2,1)S(1)} %collective-permute-done.19.refs_1_), channel_id=1, source_target_pairs={{0,1},{1,0},{2,3},{3,2},{4,5},{5,4},{6,7},{7,6},{8,9},{9,8},{10,11... | collective-permute-start | bytes 393224 | tf_op jit(solution)/shard_map/ppermute | solution.py:34
  106.0 0.9 copy-done.7
  106.9 0.8 shard_map.118.refs_0_
  107.7 1.6 %shard_map.119 = bf16[256,1024]{1,0:T(8,128)(2,1)} custom-call(bf16[128,1024]{1,0:T(8,128)(2,1)S(1)} %shard_map.118.refs_0_, bf16[64,1024]{1,0:T(8,128)(2,1)S(1)} %collective-permute-done.19.refs_1_, bf16[64,1024]{1,0:T(8,128)(2,1)S(1)} %collective-permute-done.20.refs_2_, bf16[1024,1024]{1,0:T(8,128)(2,1)S(1)} %copy-done.1), custom_call_target="tpu_custom_call" | custom-call | flops 268435456 | bytes 3145728 | tf_op jit(solution)/shard_map/pallas_call | solution.py:67
  (42 shorter events, 0.7 us)
Async XLA Ops:
  0.6 30.9 %copy-start.9 = (s32[64,4]{0,1:T(4,128)S(1)}, s32[64,4]{0,1:T(4,128)}, u32[]{:S(2)}) copy-start(s32[64,4]{0,1:T(4,128)} %param.15) | copy-start | bytes 3076
  3.1 2.3 %collective-permute-start = (bf16[4,128,384]{2,1,0:T(8,128)(2,1)}, bf16[4,128,384]{2,1,0:T(8,128)(2,1)S(1)}, u32[]{:S(2)}, u32[]{:S(2)}) collective-permute-start(bf16[4,128,384]{2,1,0:T(8,128)(2,1)} %get-tuple-element.32), channel_id=1, source_target_pairs={{0,1},{1,0},{2,3},{3,2},{4,5},{5,4},{6,7},{7,6},{8,9},{9,8},{10,11... | collective-permute-start | bytes 1179656 | tf_op jit(solution)/shard_map/ppermute | solution.py:34
  3.9 13.7 %collective-permute-start.2 = (bf16[1024,256]{1,0:T(8,128)(2,1)}, bf16[1024,256]{1,0:T(8,128)(2,1)S(1)}, u32[]{:S(2)}, u32[]{:S(2)}) collective-permute-start(bf16[1024,256]{1,0:T(8,128)(2,1)} %get-tuple-element.34.refs_1_), channel_id=1, source_target_pairs={{0,2},{1,3},{2,0},{3,1},{4,6},{5,7},{6,4},{7,5},{8,10},{9,11},{10,... | collective-permute-start | bytes 1572872 | tf_op jit(solution)/shard_map/ppermute | solution.py:34
  6.2 23.6 %all-to-all-start = ((bf16[8,128,384]{2,1,0:T(8,128)(2,1)}), bf16[8,128,384]{2,1,0:T(8,128)(2,1)S(1)}, u32[]{:S(2)}, u32[]{:S(2)}) async-start(bf16[8,128,384]{2,1,0:T(8,128)(2,1)} %constant_dynamic-update-slice_fusion), calls=%async_computation | async-start | bytes 1572864 | tf_op jit(solution)/shard_map/all_to_all | solution.py:410
  13.9 8.5 %collective-permute-start.1 = (bf16[1024,256]{1,0:T(8,128)(2,1)}, bf16[1024,256]{1,0:T(8,128)(2,1)S(1)}, u32[]{:S(2)}, u32[]{:S(2)}) collective-permute-start(bf16[1024,256]{1,0:T(8,128)(2,1)} %get-tuple-element.34.refs_1_), channel_id=1, source_target_pairs={{0,1},{1,0},{2,3},{3,2},{4,5},{5,4},{6,7},{7,6},{8,9},{9,8},{10,11... | collective-permute-start | bytes 1572872 | tf_op jit(solution)/shard_map/ppermute | solution.py:34
  17.6 4.9 %collective-permute-start.3 = (bf16[1024,256]{1,0:T(8,128)(2,1)S(1)}, bf16[1024,256]{1,0:T(8,128)(2,1)S(1)}, u32[]{:S(2)}, u32[]{:S(2)}) collective-permute-start(bf16[1024,256]{1,0:T(8,128)(2,1)S(1)} %collective-permute-done.2.refs_3_), channel_id=1, source_target_pairs={{0,1},{1,0},{2,3},{3,2},{4,5},{5,4},{6,7},{7,6},{8,9},{9,8},{10,11... | collective-permute-start | bytes 1572872 | tf_op jit(solution)/shard_map/ppermute | solution.py:34
  18.9 1.6 %copy-start = (bf16[1024,1024]{1,0:T(8,128)(2,1)S(1)}, bf16[1024,1024]{1,0:T(8,128)(2,1)}, u32[]{:S(2)}) copy-start(bf16[1024,1024]{1,0:T(8,128)(2,1)} %refs_3_.4) | copy-start | bytes 6291460
  20.5 1.0 copy-start.3
  22.5 2.2 %copy-start.2 = (bf16[512,4096]{1,0:T(8,128)(2,1)S(1)}, bf16[512,4096]{1,0:T(8,128)(2,1)}, u32[]{:S(2)}) copy-start(bf16[512,4096]{1,0:T(8,128)(2,1)} %refs_0_.6) | copy-start | bytes 12582916
  24.7 1.0 copy-start.4
  30.0 3.2 %collective-permute-start.4 = (bf16[8,128,128]{2,1,0:T(8,128)(2,1)S(1)}, bf16[8,128,128]{2,1,0:T(8,128)(2,1)S(1)}, u32[]{:S(2)}, u32[]{:S(2)}) collective-permute-start(bf16[8,128,128]{2,1,0:T(8,128)(2,1)S(1)} %get-tuple-element.35.refs_0_), channel_id=1, source_target_pairs={{0,1},{1,0},{2,3},{3,2},{4,5},{5,4},{6,7},{7,6},{8,9},{9,8},{10,11... | collective-permute-start | bytes 786440 | tf_op jit(solution)/shard_map/ppermute | solution.py:34
  31.4 15.6 %collective-permute-start.11 = (bf16[128,1024]{1,0:T(8,128)(2,1)S(1)}, bf16[128,1024]{1,0:T(8,128)(2,1)S(1)}, u32[]{:S(2)}, u32[]{:S(2)}) collective-permute-start(bf16[128,1024]{1,0:T(8,128)(2,1)S(1)} %get-tuple-element.51), channel_id=1, source_target_pairs={{0,1},{1,0},{2,3},{3,2},{4,5},{5,4},{6,7},{7,6},{8,9},{9,8},{10,11... | collective-permute-start | bytes 786440 | tf_op jit(solution)/shard_map/ppermute | solution.py:34
  31.6 22.1 %copy-start.6 = (s32[64,4]{1,0:T(8,128)}, s32[64,4]{1,0:T(8,128)S(1)}, u32[]{:S(2)}) copy-start(s32[64,4]{1,0:T(8,128)S(1)} %copy.17.refs_0_.refs_3_) | copy-start | bytes 3076
  31.6 7.6 %collective-permute-start.5 = (bf16[4,128,256]{2,1,0:T(8,128)(2,1)S(1)}, bf16[4,128,256]{2,1,0:T(8,128)(2,1)S(1)}, u32[]{:S(2)}, u32[]{:S(2)}) collective-permute-start(bf16[4,128,256]{2,1,0:T(8,128)(2,1)S(1)} %get-tuple-element.36.refs_2_.refs_4_), channel_id=1, source_target_pairs={{0,16},{1,17},{2,18},{3,19},{4,20},{5,21},{6,22},{7,23},{8,24},{9,... | collective-permute-start | bytes 786440 | tf_op jit(solution)/shard_map/ppermute | solution.py:34
  31.9 8.4 %collective-permute-start.6 = (bf16[4,128,256]{2,1,0:T(8,128)(2,1)S(1)}, bf16[4,128,256]{2,1,0:T(8,128)(2,1)S(1)}, u32[]{:S(2)}, u32[]{:S(2)}) collective-permute-start(bf16[4,128,256]{2,1,0:T(8,128)(2,1)S(1)} %get-tuple-element.37.refs_3_.refs_5_), channel_id=1, source_target_pairs={{0,48},{1,49},{2,50},{3,51},{4,52},{5,53},{6,54},{7,55},{8,56},{9,... | collective-permute-start | bytes 786440 | tf_op jit(solution)/shard_map/ppermute | solution.py:34
  36.0 19.6 %collective-permute-start.12 = (bf16[512,256]{1,0:T(8,128)(2,1)S(1)}, bf16[512,256]{1,0:T(8,128)(2,1)S(1)}, u32[]{:S(2)}, u32[]{:S(2)}) collective-permute-start(bf16[512,256]{1,0:T(8,128)(2,1)S(1)} %get-tuple-element.52.refs_0_), channel_id=1, source_target_pairs={{0,4},{1,5},{2,6},{3,7},{4,8},{5,9},{6,10},{7,11},{8,12},{9,13},{1... | collective-permute-start | bytes 786440 | tf_op jit(solution)/shard_map/ppermute | solution.py:34
  36.1 19.5 %collective-permute-start.13 = (bf16[512,256]{1,0:T(8,128)(2,1)S(1)}, bf16[512,256]{1,0:T(8,128)(2,1)S(1)}, u32[]{:S(2)}, u32[]{:S(2)}) collective-permute-start(bf16[512,256]{1,0:T(8,128)(2,1)S(1)} %get-tuple-element.52.refs_0_), channel_id=1, source_target_pairs={{0,8},{1,9},{2,10},{3,11},{4,12},{5,13},{6,14},{7,15},{8,0},{9,1},... | collective-permute-start | bytes 786440 | tf_op jit(solution)/shard_map/ppermute | solution.py:34
  40.3 8.7 %collective-permute-start.10 = (bf16[4,128,256]{2,1,0:T(8,128)(2,1)S(1)}, bf16[4,128,256]{2,1,0:T(8,128)(2,1)S(1)}, u32[]{:S(2)}, u32[]{:S(2)}) collective-permute-start(bf16[4,128,256]{2,1,0:T(8,128)(2,1)S(1)} %get-tuple-element.44), channel_id=1, source_target_pairs={{0,48},{1,49},{2,50},{3,51},{4,52},{5,53},{6,54},{7,55},{8,56},{9,... | collective-permute-start | bytes 786440 | tf_op jit(solution)/shard_map/ppermute | solution.py:34
  40.4 8.6 %collective-permute-start.9 = (bf16[4,128,256]{2,1,0:T(8,128)(2,1)S(1)}, bf16[4,128,256]{2,1,0:T(8,128)(2,1)S(1)}, u32[]{:S(2)}, u32[]{:S(2)}) collective-permute-start(bf16[4,128,256]{2,1,0:T(8,128)(2,1)S(1)} %get-tuple-element.41.refs_9_), channel_id=1, source_target_pairs={{0,16},{1,17},{2,18},{3,19},{4,20},{5,21},{6,22},{7,23},{8,24},{9,... | collective-permute-start | bytes 786440 | tf_op jit(solution)/shard_map/ppermute | solution.py:34
  43.0 10.7 %slice-start = ((s8[8388608]{0:T(1024)(128)(4,1)}), s8[4194304]{0:T(1024)(128)(4,1)S(1)}, s32[]{:S(2)}) async-start(s8[8388608]{0:T(1024)(128)(4,1)} %bitcast.1), calls=%async_computation.2 | async-start | bytes 8388608
  47.0 8.5 %collective-permute-start.14 = (bf16[512,256]{1,0:T(8,128)(2,1)S(1)}, bf16[512,256]{1,0:T(8,128)(2,1)S(1)}, u32[]{:S(2)}, u32[]{:S(2)}) collective-permute-start(bf16[512,256]{1,0:T(8,128)(2,1)S(1)} %get-tuple-element.52.refs_0_), channel_id=1, source_target_pairs={{0,12},{1,13},{2,14},{3,15},{4,0},{5,1},{6,2},{7,3},{8,4},{9,5},{1... | collective-permute-start | bytes 786440 | tf_op jit(solution)/shard_map/ppermute | solution.py:34
  49.0 6.0 %collective-permute-start.7 = (bf16[4,128,256]{2,1,0:T(8,128)(2,1)S(1)}, bf16[4,128,256]{2,1,0:T(8,128)(2,1)S(1)}, u32[]{:S(2)}, u32[]{:S(2)}) collective-permute-start(bf16[4,128,256]{2,1,0:T(8,128)(2,1)S(1)} %get-tuple-element.42), channel_id=1, source_target_pairs={{0,16},{1,17},{2,18},{3,19},{4,20},{5,21},{6,22},{7,23},{8,24},{9,... | collective-permute-start | bytes 786440 | tf_op jit(solution)/shard_map/ppermute | solution.py:34
  49.0 4.7 %slice-start.1 = ((s8[8388608]{0:T(1024)(128)(4,1)}), s8[4194304]{0:T(1024)(128)(4,1)S(1)}, s32[]{:S(2)}) async-start(s8[8388608]{0:T(1024)(128)(4,1)} %bitcast.1), calls=%async_computation.3 | async-start | bytes 8388608
  49.0 6.5 %collective-permute-start.8 = (bf16[4,128,256]{2,1,0:T(8,128)(2,1)S(1)}, bf16[4,128,256]{2,1,0:T(8,128)(2,1)S(1)}, u32[]{:S(2)}, u32[]{:S(2)}) collective-permute-start(bf16[4,128,256]{2,1,0:T(8,128)(2,1)S(1)} %get-tuple-element.43), channel_id=1, source_target_pairs={{0,48},{1,49},{2,50},{3,51},{4,52},{5,53},{6,54},{7,55},{8,56},{9,... | collective-permute-start | bytes 786440 | tf_op jit(solution)/shard_map/ppermute | solution.py:34
  55.0 21.3 %copy-start.5 = (bf16[3,64,1024]{2,1,0:T(8,128)(2,1)}, bf16[3,64,1024]{2,1,0:T(8,128)(2,1)S(1)}, u32[]{:S(2)}) copy-start(bf16[3,64,1024]{2,1,0:T(8,128)(2,1)S(1)} %shard_map.112.refs_7_.refs_2_) | copy-start | bytes 1179652
  59.4 4.9 %collective-permute-start.15 = (bf16[160,1024]{1,0:T(8,128)(2,1)S(1)}, bf16[160,1024]{1,0:T(8,128)(2,1)S(1)}, u32[]{:S(2)}, u32[]{:S(2)}) collective-permute-start(bf16[160,1024]{1,0:T(8,128)(2,1)S(1)} %get-tuple-element.54), channel_id=1, source_target_pairs={{0,1},{1,0},{2,3},{3,2},{4,5},{5,4},{6,7},{7,6},{8,9},{9,8},{10,11... | collective-permute-start | bytes 983048 | tf_op jit(solution)/shard_map/ppermute | solution.py:34
  64.4 11.3 %collective-permute-start.16 = (bf16[4,512,256]{2,1,0:T(8,128)(2,1)S(1)}, bf16[4,512,256]{2,1,0:T(8,128)(2,1)S(1)}, u32[]{:S(2)}, u32[]{:S(2)}) collective-permute-start(bf16[4,512,256]{2,1,0:T(8,128)(2,1)S(1)} %shard_map.115.refs_1_), channel_id=1, source_target_pairs={{0,1},{1,0},{2,3},{3,2},{4,5},{5,4},{6,7},{7,6},{8,9},{9,8},{10,11... | collective-permute-start | bytes 3145736 | tf_op jit(solution)/shard_map/ppermute | solution.py:34
  76.3 0.7 copy-start.8
  77.0 3.8 %collective-permute-start.17 = (bf16[64,1024]{1,0:T(8,128)(2,1)S(1)}, bf16[64,1024]{1,0:T(8,128)(2,1)S(1)}, u32[]{:S(2)}, u32[]{:S(2)}) collective-permute-start(bf16[64,1024]{1,0:T(8,128)(2,1)S(1)} %get-tuple-element.57), channel_id=1, source_target_pairs={{0,2},{1,3},{2,0},{3,1},{4,6},{5,7},{6,4},{7,5},{8,10},{9,11},{10,... | collective-permute-start | bytes 393224 | tf_op jit(solution)/shard_map/ppermute | solution.py:34
  80.8 0.6 copy-start.10
  81.5 24.5 %copy-start.1 = (bf16[1024,1024]{1,0:T(8,128)(2,1)S(1)}, bf16[1024,1024]{1,0:T(8,128)(2,1)}, u32[]{:S(2)}) copy-start(bf16[1024,1024]{1,0:T(8,128)(2,1)} %refs_3_.4) | copy-start | bytes 6291460
  97.6 4.1 %collective-permute-start.19 = (bf16[64,1024]{1,0:T(8,128)(2,1)}, bf16[64,1024]{1,0:T(8,128)(2,1)S(1)}, u32[]{:S(2)}, u32[]{:S(2)}) collective-permute-start(bf16[64,1024]{1,0:T(8,128)(2,1)} %get-tuple-element.59.refs_0_), channel_id=1, source_target_pairs={{0,2},{1,3},{2,0},{3,1},{4,6},{5,7},{6,4},{7,5},{8,10},{9,11},{10,... | collective-permute-start | bytes 393224 | tf_op jit(solution)/shard_map/ppermute | solution.py:34
  98.0 8.0 %collective-permute-start.18 = (bf16[64,1024]{1,0:T(8,128)(2,1)}, bf16[64,1024]{1,0:T(8,128)(2,1)S(1)}, u32[]{:S(2)}, u32[]{:S(2)}) collective-permute-start(bf16[64,1024]{1,0:T(8,128)(2,1)} %get-tuple-element.59.refs_0_), channel_id=1, source_target_pairs={{0,1},{1,0},{2,3},{3,2},{4,5},{5,4},{6,7},{7,6},{8,9},{9,8},{10,11... | collective-permute-start | bytes 393224 | tf_op jit(solution)/shard_map/ppermute | solution.py:34
  101.7 6.1 %collective-permute-start.20 = (bf16[64,1024]{1,0:T(8,128)(2,1)S(1)}, bf16[64,1024]{1,0:T(8,128)(2,1)S(1)}, u32[]{:S(2)}, u32[]{:S(2)}) collective-permute-start(bf16[64,1024]{1,0:T(8,128)(2,1)S(1)} %collective-permute-done.19.refs_1_), channel_id=1, source_target_pairs={{0,1},{1,0},{2,3},{3,2},{4,5},{5,4},{6,7},{7,6},{8,9},{9,8},{10,11... | collective-permute-start | bytes 393224 | tf_op jit(solution)/shard_map/ppermute | solution.py:34
  106.0 0.9 copy-start.7

commit v4 on v3

--- a/solution.py
+++ b/solution.py
@@ -383,19 +383,8 @@
     dctx_ref[...] = add([at(dstream, i) for i in range(4)]).astype(BF16)
 
 
-def grad_chip_body(own_ref, other_ref, cw_ref, out_ref, rows):
-    c = lax.axis_index("c")
-    rows[pl.ds(pl.multiple_of(c * 64, 64), 64), :] = own_ref[...]
-    rows[pl.ds(pl.multiple_of((1 - c) * 64, 64), 64), :] = other_ref[...]
-    out_ref[...] = dot_nt(rows[...], cw_ref[...]).astype(BF16)
-
-
-def grad_body(chip_ref, l_ref, lc_ref, cw_ref, out_ref, rows):
-    l, c = lax.axis_index("l"), lax.axis_index("c")
-    rows[pl.ds(pl.multiple_of(c * 64, 64), 64), :] = l_ref[...]
-    rows[pl.ds(pl.multiple_of((1 - c) * 64, 64), 64), :] = lc_ref[...]
-    out_ref[pl.ds(pl.multiple_of(l * 128, 128), 128), :] = chip_ref[...]
-    out_ref[pl.ds(pl.multiple_of((1 - l) * 128, 128), 128), :] = dot_nt(rows[...], cw_ref[...]).astype(BF16)
+def grad_body(rows_ref, cw_ref, out_ref):
+    out_ref[...] = dot_nt(rows_ref[...], cw_ref[...]).astype(BF16)
 
 
 def per_device(hidden_in, queries, keys, values, out_weight, context_weight, codes, table, depth_weights):
@@ -467,16 +456,8 @@
         scratch=[pltpu.VMEM((4, 1024, 1024), BF16), pltpu.VMEM((4, 1024, 1024), BF16), pltpu.SemaphoreType.DMA((8,))],
         limit=60, flops=12 << 30, nbytes=17 << 20,
     )
-    d_l = move(dcontext, l_swap)
-    rows = [pltpu.VMEM((128, 1024), BF16)]
-    grad_chip = call(
-        grad_chip_body, shape(128, 1024), [VM] * 3, dcontext, move(dcontext, other_core), context_weight,
-        scratch=rows, flops=1 << 28, nbytes=3 << 20,
-    )
-    grad = call(
-        grad_body, shape(256, 1024), [VM] * 4, grad_chip, d_l, move(d_l, other_core), context_weight,
-        scratch=rows, flops=1 << 28, nbytes=3 << 20,
-    )
+    rows = lax.all_gather(dcontext, ("l", "c"), axis=0, tiled=True)
+    grad = call(grad_body, shape(256, 1024), [VM] * 2, rows, context_weight, flops=1 << 29, nbytes=3 << 20)
     return losses.reshape(64), grad
 
 

time: 110 us -> 109 us (level)
  blocking collectives: 10.7 us -> 20.4 us
  starting transfers between devices: 36.9 us -> 28.6 us
    all_gather x0 -> x1, blocking collectives: none -> 9.74 us  [per_device(): rows = lax.all_gather(dcontext, ('l', 'c'), axis=0, tiled=True)]
    ppermute x21 -> x18, starting transfers between devices: 29.3 us -> 21 us  [move(): return lax.ppermute(array, AXES, pairs)]
    unnamed x27 -> x25, local copies, waits for them, and re-layouts: 8.24 us -> 7.33 us
    pallas_call x16 -> x15, Pallas kernels: 39.2 us -> 38.3 us  [call(): pl.pallas_call(run, out_shape=out_shape, in_specs=in_specs, out_specs=out...]
    ppermute x21 -> x18, waiting for transfers between devices: 9.71 us -> 9.56 us  [move(): return lax.ppermute(array, AXES, pairs)]
  transfers between devices with their start and end apart: 22 -> 19, of which waited for: 8 -> 7; matrix products, arithmetic and copies ran while one was open for 1% -> 1% of each run, Pallas kernels for 13% -> 13%
where the time goes in v4:
time: 109 us
  Pallas kernels  38.3 us (35%)
  starting transfers between devices  28.6 us (26%)
  blocking collectives  20.4 us (19%)
  waiting for transfers between devices  12.4 us (11%)
  local copies, waits for them, and re-layouts  8.1 us (7%)
    pallas_call x15, Pallas kernels, call(): pl.pallas_call(run, out_shape=out_shape, in_specs=in_specs, out_specs=out...  38.3 us
    ppermute x18, starting transfers between devices, move(): return lax.ppermute(array, AXES, pairs)  21 us
    all_to_all x1, blocking collectives, per_device(): attended = lax.all_to_all(attended, ('h', 'z'), 0, 0, tiled=True)  10.7 us
    all_gather x1, blocking collectives, per_device(): rows = lax.all_gather(dcontext, ('l', 'c'), axis=0, tiled=True)  9.74 us
    ppermute x18, waiting for transfers between devices, move(): return lax.ppermute(array, AXES, pairs)  9.56 us
    all_to_all x1, starting transfers between devices, per_device(): mine = lax.all_to_all(full, ('h', 'z'), 0, 0, tiled=True)  7.66 us
    unnamed x25, local copies, waits for them, and re-layouts  7.33 us
    all_to_all x1, waiting for transfers between devices, per_device(): mine = lax.all_to_all(full, ('h', 'z'), 0, 0, tiled=True)  2.89 us
  transfers between devices with their start and end apart: 19, of which 7 were waited for; matrix products, arithmetic and copies ran while one was open for 1% of the time, Pallas kernels for 13%

profile of v4, /device:TPU:7, one launch (start us, length us, event | category | flops | bytes accessed | tf_op | source)
XLA Modules:
  0.0 108.8 jit_solution(14122122561771881815)
XLA Ops:
  0.6 2.5 %shard_map.104 = (bf16[8,128,384]{2,1,0:T(8,128)(2,1)}, bf16[4,128,384]{2,1,0:T(8,128)(2,1)}, bf16[1024,256]{1,0:T(8,128)(2,1)}) custom-call(bf16[256,512]{1,0:T(8,128)(2,1)} %refs_0_.4, bf16[256,512]{1,0:T(8,128)(2,1)} %refs_1_.4, bf16[256,512]{1,0:T(8,128)(2,1)} %refs_2_.1, bf16[1024,1024]{1,0:T(8,128)(2,1)} %refs_1_.7), custom_call_target="tpu_custom_call" | custom-call | bytes 3145728 | tf_op jit(solution)/shard_map/pallas_call | solution.py:67
  3.1 0.8 collective-permute-start
  3.9 1.3 %collective-permute-start.2 = (bf16[1024,256]{1,0:T(8,128)(2,1)}, bf16[1024,256]{1,0:T(8,128)(2,1)S(1)}, u32[]{:S(2)}, u32[]{:S(2)}) collective-permute-start(bf16[1024,256]{1,0:T(8,128)(2,1)} %get-tuple-element.34.refs_1_), channel_id=1, source_target_pairs={{0,2},{1,3},{2,0},{3,1},{4,6},{5,7},{6,4},{7,5},{8,10},{9,11},{10,... | collective-permute-start | bytes 1572872 | tf_op jit(solution)/shard_map/ppermute | solution.py:34
  5.2 0.2 collective-permute-done
  5.5 0.8 constant_dynamic-update-slice_fusion
  6.2 7.7 %all-to-all-start = ((bf16[8,128,384]{2,1,0:T(8,128)(2,1)}), bf16[8,128,384]{2,1,0:T(8,128)(2,1)S(1)}, u32[]{:S(2)}, u32[]{:S(2)}) async-start(bf16[8,128,384]{2,1,0:T(8,128)(2,1)} %constant_dynamic-update-slice_fusion), calls=%async_computation | async-start | bytes 1572864 | tf_op jit(solution)/shard_map/all_to_all | solution.py:399
  13.9 0.7 collective-permute-start.1
  14.6 3.0 %collective-permute-done.2.refs_3_ = bf16[1024,256]{1,0:T(8,128)(2,1)S(1)} collective-permute-done((bf16[1024,256]{1,0:T(8,128)(2,1)}, bf16[1024,256]{1,0:T(8,128)(2,1)S(1)}, u32[]{:S(2)}, u32[]{:S(2)}) %collective-permute-start.2) | collective-permute-done | bytes 524320 | tf_op jit(solution)/shard_map/ppermute | solution.py:34
  17.6 1.3 %collective-permute-start.3 = (bf16[1024,256]{1,0:T(8,128)(2,1)S(1)}, bf16[1024,256]{1,0:T(8,128)(2,1)S(1)}, u32[]{:S(2)}, u32[]{:S(2)}) collective-permute-start(bf16[1024,256]{1,0:T(8,128)(2,1)S(1)} %collective-permute-done.2.refs_3_), channel_id=1, source_target_pairs={{0,1},{1,0},{2,3},{3,2},{4,5},{5,4},{6,7},{7,6},{8,9},{9,8},{10,11... | collective-permute-start | bytes 1572872 | tf_op jit(solution)/shard_map/ppermute | solution.py:34
  18.9 1.6 %copy-done = bf16[1024,1024]{1,0:T(8,128)(2,1)S(1)} copy-done((bf16[1024,1024]{1,0:T(8,128)(2,1)S(1)}, bf16[1024,1024]{1,0:T(8,128)(2,1)}, u32[]{:S(2)}) %copy-start) | copy-done | bytes 2097176
  20.5 1.0 copy-done.3
  21.6 0.9 shard_map.105
  22.5 2.2 %copy-done.2 = bf16[512,4096]{1,0:T(8,128)(2,1)S(1)} copy-done((bf16[512,4096]{1,0:T(8,128)(2,1)S(1)}, bf16[512,4096]{1,0:T(8,128)(2,1)}, u32[]{:S(2)}) %copy-start.2) | copy-done | bytes 4194328
  24.7 1.0 copy-done.4
  25.7 1.2 %shard_map.106.refs_2_.refs_4_ = bf16[512,256]{1,0:T(8,128)(2,1)S(1)} custom-call(bf16[512,4096]{1,0:T(8,128)(2,1)S(1)} %copy-done.2, bf16[1024,256]{1,0:T(8,128)(2,1)S(1)} %copy-done.4, bf16[1024,256]{1,0:T(8,128)(2,1)S(1)} %collective-permute-done.1.refs_2_, bf16[1024,256]{1,0:T(8,128)(2,1)S(1)} %collective-permute-done.2.refs_3_, ...), custom_call_target="tpu_custom_call" | custom-call | flops 1073741824 | bytes 6291456 | tf_op jit(solution)/shard_map/pallas_call | solution.py:67
  27.0 2.9 %all-to-all-done.refs_0_ = bf16[8,128,384]{2,1,0:T(8,128)(2,1)S(1)} async-done(((bf16[8,128,384]{2,1,0:T(8,128)(2,1)}), bf16[8,128,384]{2,1,0:T(8,128)(2,1)S(1)}, u32[]{:S(2)}, u32[]{:S(2)}) %all-to-all-start) | async-done | bytes 786464 | tf_op jit(solution)/shard_map/all_to_all | solution.py:399
  29.8 0.1 shard_map.107
  30.0 1.4 %collective-permute-start.4 = (bf16[8,128,128]{2,1,0:T(8,128)(2,1)S(1)}, bf16[8,128,128]{2,1,0:T(8,128)(2,1)S(1)}, u32[]{:S(2)}, u32[]{:S(2)}) collective-permute-start(bf16[8,128,128]{2,1,0:T(8,128)(2,1)S(1)} %get-tuple-element.35.refs_0_), channel_id=1, source_target_pairs={{0,1},{1,0},{2,3},{3,2},{4,5},{5,4},{6,7},{7,6},{8,9},{9,8},{10,11... | collective-permute-start | bytes 786440 | tf_op jit(solution)/shard_map/ppermute | solution.py:34
  31.4 0.1 collective-permute-start.11
  31.5 0.1 copy.17.refs_0_.refs_3_
  31.6 0.3 collective-permute-start.5
  31.9 1.3 %collective-permute-start.6 = (bf16[4,128,256]{2,1,0:T(8,128)(2,1)S(1)}, bf16[4,128,256]{2,1,0:T(8,128)(2,1)S(1)}, u32[]{:S(2)}, u32[]{:S(2)}) collective-permute-start(bf16[4,128,256]{2,1,0:T(8,128)(2,1)S(1)} %get-tuple-element.37.refs_3_.refs_5_), channel_id=1, source_target_pairs={{0,48},{1,49},{2,50},{3,51},{4,52},{5,53},{6,54},{7,55},{8,56},{9,... | collective-permute-start | bytes 786440 | tf_op jit(solution)/shard_map/ppermute | solution.py:34
  33.1 2.8 %shard_map.108 = (f32[128,2048]{1,0:T(8,128)S(1)}, f32[1,2048]{1,0:T(1,128)S(1)}, f32[1,2048]{1,0:T(1,128)S(1)}, bf16[512,256]{1,0:T(8,128)(2,1)S(1)}) custom-call(bf16[8,128,128]{2,1,0:T(8,128)(2,1)S(1)} %get-tuple-element.35.refs_0_, bf16[8,128,128]{2,1,0:T(8,128)(2,1)S(1)} %collective-permute-done.4.refs_1_, ...), custom_call_target="tpu_custom_call" | custom-call | flops 4294967296 | bytes 2097152 | tf_op jit(solution)/shard_map/pallas_call | solution.py:67
  36.0 0.1 collective-permute-start.12
  36.1 3.1 %collective-permute-start.13 = (bf16[512,256]{1,0:T(8,128)(2,1)S(1)}, bf16[512,256]{1,0:T(8,128)(2,1)S(1)}, u32[]{:S(2)}, u32[]{:S(2)}) collective-permute-start(bf16[512,256]{1,0:T(8,128)(2,1)S(1)} %get-tuple-element.52.refs_0_), channel_id=1, source_target_pairs={{0,8},{1,9},{2,10},{3,11},{4,12},{5,13},{6,14},{7,15},{8,0},{9,1},... | collective-permute-start | bytes 786440 | tf_op jit(solution)/shard_map/ppermute | solution.py:34
  39.2 1.1 collective-permute-done.6.refs_1_.refs_3_
  40.3 0.1 collective-permute-start.10
  40.4 2.6 %collective-permute-start.9 = (bf16[4,128,256]{2,1,0:T(8,128)(2,1)S(1)}, bf16[4,128,256]{2,1,0:T(8,128)(2,1)S(1)}, u32[]{:S(2)}, u32[]{:S(2)}) collective-permute-start(bf16[4,128,256]{2,1,0:T(8,128)(2,1)S(1)} %get-tuple-element.41.refs_9_), channel_id=1, source_target_pairs={{0,16},{1,17},{2,18},{3,19},{4,20},{5,21},{6,22},{7,23},{8,24},{9,... | collective-permute-start | bytes 786440 | tf_op jit(solution)/shard_map/ppermute | solution.py:34
  43.0 4.0 %shard_map.110 = (f32[128,2048]{1,0:T(8,128)S(1)}, f32[1,2048]{1,0:T(1,128)S(1)}, f32[1,2048]{1,0:T(1,128)S(1)}, bf16[4,128,256]{2,1,0:T(8,128)(2,1)S(1)}, bf16[4,128,256]{2,1,0:T(8,128)(2,1)S(1)}) custom-call(bf16[8,128,128]{2,1,0:T(8,128)(2,1)S(1)} %get-tuple-element.35.refs_0_, ...), custom_call_target="tpu_custom_call", output_to_operand_aliasing={{0}: (6, {}), {1}: (7, {}), {2}: (8, {})} | custom-call | flops 3221225472 | bytes 4194304 | tf_op jit(solution)/shard_map/pallas_call | solution.py:67
  47.0 2.0 %collective-permute-start.14 = (bf16[512,256]{1,0:T(8,128)(2,1)S(1)}, bf16[512,256]{1,0:T(8,128)(2,1)S(1)}, u32[]{:S(2)}, u32[]{:S(2)}) collective-permute-start(bf16[512,256]{1,0:T(8,128)(2,1)S(1)} %get-tuple-element.52.refs_0_), channel_id=1, source_target_pairs={{0,12},{1,13},{2,14},{3,15},{4,0},{5,1},{6,2},{7,3},{8,4},{9,5},{1... | collective-permute-start | bytes 786440 | tf_op jit(solution)/shard_map/ppermute | solution.py:34
  49.0 1.4 %collective-permute-start.8 = (bf16[4,128,256]{2,1,0:T(8,128)(2,1)S(1)}, bf16[4,128,256]{2,1,0:T(8,128)(2,1)S(1)}, u32[]{:S(2)}, u32[]{:S(2)}) collective-permute-start(bf16[4,128,256]{2,1,0:T(8,128)(2,1)S(1)} %get-tuple-element.43), channel_id=1, source_target_pairs={{0,48},{1,49},{2,50},{3,51},{4,52},{5,53},{6,54},{7,55},{8,56},{9,... | collective-permute-start | bytes 786440 | tf_op jit(solution)/shard_map/ppermute | solution.py:34
  50.5 3.2 %shard_map.111 = (f32[128,2048]{1,0:T(8,128)S(1)}, f32[1,2048]{1,0:T(1,128)S(1)}, f32[1,2048]{1,0:T(1,128)S(1)}) custom-call(bf16[8,128,128]{2,1,0:T(8,128)(2,1)S(1)} %get-tuple-element.35.refs_0_, bf16[8,128,128]{2,1,0:T(8,128)(2,1)S(1)} %collective-permute-done.4.refs_1_, ...), custom_call_target="tpu_custom_call", output_to_operand_aliasing={{0}: (4, {}), {1}: (5, {}), {2}: (6, {})} | custom-call | flops 3221225472 | bytes 3145728 | tf_op jit(solution)/shard_map/pallas_call | solution.py:67
  53.7 1.3 %shard_map.112.refs_7_.refs_2_ = bf16[3,64,1024]{2,1,0:T(8,128)(2,1)S(1)} custom-call(s32[64,4]{1,0:T(8,128)S(1)} %copy.17.refs_0_.refs_3_, bf16[4,1024,1024]{2,1,0:T(8,128)(2,1)S(1)} %bitcast.2, f32[1,2048]{1,0:T(1,128)S(1)} %get-tuple-element.49.refs_2_.refs_5_), custom_call_target="tpu_custom_call" | custom-call | flops 402653184 | bytes 8388608 | tf_op jit(solution)/shard_map/pallas_call | solution.py:67
  55.0 0.5 collective-permute-done.8.refs_3_
  55.5 3.9 %shard_map.113 = (f32[128,1024]{1,0:T(8,128)S(1)}, bf16[160,1024]{1,0:T(8,128)(2,1)S(1)}, f32[8,1024]{1,0:T(8,128)S(1)}) custom-call(bf16[8,128,128]{2,1,0:T(8,128)(2,1)S(1)} %get-tuple-element.35.refs_0_, bf16[8,128,128]{2,1,0:T(8,128)(2,1)S(1)} %collective-permute-done.4.refs_1_, bf16[4,128,256]{2,1,0:T(8,128)(2,1)S(1)} %collective-permute-done.7.refs_2_, ...), custom_call_target="tpu_custom_call" | custom-call | flops 3221225472 | bytes 3145728 | tf_op jit(solution)/shard_map/pallas_call | solution.py:67
  59.4 3.6 %collective-permute-start.15 = (bf16[160,1024]{1,0:T(8,128)(2,1)S(1)}, bf16[160,1024]{1,0:T(8,128)(2,1)S(1)}, u32[]{:S(2)}, u32[]{:S(2)}) collective-permute-start(bf16[160,1024]{1,0:T(8,128)(2,1)S(1)} %get-tuple-element.54), channel_id=1, source_target_pairs={{0,1},{1,0},{2,3},{3,2},{4,5},{5,4},{6,7},{7,6},{8,9},{9,8},{10,11... | collective-permute-start | bytes 983048 | tf_op jit(solution)/shard_map/ppermute | solution.py:34
  63.1 1.3 %collective-permute-done.15.refs_1_.refs_4_ = bf16[160,1024]{1,0:T(8,128)(2,1)S(1)} collective-permute-done((bf16[160,1024]{1,0:T(8,128)(2,1)S(1)}, bf16[160,1024]{1,0:T(8,128)(2,1)S(1)}, u32[]{:S(2)}, u32[]{:S(2)}) %collective-permute-start.15) | collective-permute-done | bytes 327712 | tf_op jit(solution)/shard_map/ppermute | solution.py:34
  64.4 0.5 collective-permute-start.16
  64.8 0.2 shard_map.114
  65.0 10.7 %all_to_all.10.refs_0_ = bf16[8,128,128]{2,1,0:T(8,128)(2,1)S(1)} all-to-all(bf16[8,128,128]{2,1,0:T(8,128)(2,1)S(1)} %shard_map.114), channel_id=1, replica_groups=mesh['h'=2,'x'=4,'z'=4,'l'=2,'c'=2] {'h','z'}, dimensions={0} | all-to-all | bytes 524288 | tf_op jit(solution)/shard_map/all_to_all | solution.py:445
  75.7 0.6 shard_map.116
  76.3 0.7 copy-done.7
  77.0 0.4 collective-permute-start.17
  77.4 3.4 %collective-permute-done.17.refs_1_ = bf16[64,1024]{1,0:T(8,128)(2,1)S(1)} collective-permute-done((bf16[64,1024]{1,0:T(8,128)(2,1)S(1)}, bf16[64,1024]{1,0:T(8,128)(2,1)S(1)}, u32[]{:S(2)}, u32[]{:S(2)}) %collective-permute-start.17) | collective-permute-done | bytes 131104 | tf_op jit(solution)/shard_map/ppermute | solution.py:34
  80.8 0.7 copy-done.9
  81.5 16.0 %shard_map.117 = (f32[1,64]{1,0:T(1,128)}, bf16[64,1024]{1,0:T(8,128)(2,1)}) custom-call(f32[64,1024]{1,0:T(8,128)} %copy-done.7, bf16[64,1024]{1,0:T(8,128)(2,1)} %copy-done.9, bf16[3,64,1024]{2,1,0:T(8,128)(2,1)} %copy-done.5, s32[64,4]{1,0:T(8,128)} %copy-done.6, bf16[4,1024,1024]{2,1,0:T(8,128)(2,1)} %refs_4_.1, bf16[4,1024,1024]{2,1,0:T(8,128)(2,1)} %refs_5_.1), custom_call_target="tpu_custom_call" | custom-call | flops 12884901888 | bytes 17825792 | tf_op jit(solution)/shard_map/pallas_call | solution.py:67
  97.5 9.7 %all_gather.3.refs_0_ = bf16[256,1024]{1,0:T(8,128)(2,1)S(1)} all-gather(bf16[64,1024]{1,0:T(8,128)(2,1)} %get-tuple-element.59), channel_id=1, replica_groups=mesh['h'=2,'x'=4,'z'=4,'l'=2,'c'=2] {'l','c'}, dimensions={0}, use_global_device_ids=true | all-gather | bytes 655360 | tf_op jit(solution)/shard_map/all_gather | solution.py:459
  107.3 1.5 %shard_map.118 = bf16[256,1024]{1,0:T(8,128)(2,1)} custom-call(bf16[256,1024]{1,0:T(8,128)(2,1)S(1)} %all_gather.3.refs_0_, bf16[1024,1024]{1,0:T(8,128)(2,1)S(1)} %copy-done.1), custom_call_target="tpu_custom_call" | custom-call | flops 536870912 | bytes 3145728 | tf_op jit(solution)/shard_map/pallas_call | solution.py:67
  (34 shorter events, 0.2 us)
Async XLA Ops:
  0.6 30.9 %copy-start.8 = (s32[64,4]{0,1:T(4,128)S(1)}, s32[64,4]{0,1:T(4,128)}, u32[]{:S(2)}) copy-start(s32[64,4]{0,1:T(4,128)} %param.15) | copy-start | bytes 3076
  3.1 2.3 %collective-permute-start = (bf16[4,128,384]{2,1,0:T(8,128)(2,1)}, bf16[4,128,384]{2,1,0:T(8,128)(2,1)S(1)}, u32[]{:S(2)}, u32[]{:S(2)}) collective-permute-start(bf16[4,128,384]{2,1,0:T(8,128)(2,1)} %get-tuple-element.32), channel_id=1, source_target_pairs={{0,1},{1,0},{2,3},{3,2},{4,5},{5,4},{6,7},{7,6},{8,9},{9,8},{10,11... | collective-permute-start | bytes 1179656 | tf_op jit(solution)/shard_map/ppermute | solution.py:34
  3.9 13.7 %collective-permute-start.2 = (bf16[1024,256]{1,0:T(8,128)(2,1)}, bf16[1024,256]{1,0:T(8,128)(2,1)S(1)}, u32[]{:S(2)}, u32[]{:S(2)}) collective-permute-start(bf16[1024,256]{1,0:T(8,128)(2,1)} %get-tuple-element.34.refs_1_), channel_id=1, source_target_pairs={{0,2},{1,3},{2,0},{3,1},{4,6},{5,7},{6,4},{7,5},{8,10},{9,11},{10,... | collective-permute-start | bytes 1572872 | tf_op jit(solution)/shard_map/ppermute | solution.py:34
  6.2 23.6 %all-to-all-start = ((bf16[8,128,384]{2,1,0:T(8,128)(2,1)}), bf16[8,128,384]{2,1,0:T(8,128)(2,1)S(1)}, u32[]{:S(2)}, u32[]{:S(2)}) async-start(bf16[8,128,384]{2,1,0:T(8,128)(2,1)} %constant_dynamic-update-slice_fusion), calls=%async_computation | async-start | bytes 1572864 | tf_op jit(solution)/shard_map/all_to_all | solution.py:399
  13.9 8.5 %collective-permute-start.1 = (bf16[1024,256]{1,0:T(8,128)(2,1)}, bf16[1024,256]{1,0:T(8,128)(2,1)S(1)}, u32[]{:S(2)}, u32[]{:S(2)}) collective-permute-start(bf16[1024,256]{1,0:T(8,128)(2,1)} %get-tuple-element.34.refs_1_), channel_id=1, source_target_pairs={{0,1},{1,0},{2,3},{3,2},{4,5},{5,4},{6,7},{7,6},{8,9},{9,8},{10,11... | collective-permute-start | bytes 1572872 | tf_op jit(solution)/shard_map/ppermute | solution.py:34
  17.6 4.9 %collective-permute-start.3 = (bf16[1024,256]{1,0:T(8,128)(2,1)S(1)}, bf16[1024,256]{1,0:T(8,128)(2,1)S(1)}, u32[]{:S(2)}, u32[]{:S(2)}) collective-permute-start(bf16[1024,256]{1,0:T(8,128)(2,1)S(1)} %collective-permute-done.2.refs_3_), channel_id=1, source_target_pairs={{0,1},{1,0},{2,3},{3,2},{4,5},{5,4},{6,7},{7,6},{8,9},{9,8},{10,11... | collective-permute-start | bytes 1572872 | tf_op jit(solution)/shard_map/ppermute | solution.py:34
  18.9 1.6 %copy-start = (bf16[1024,1024]{1,0:T(8,128)(2,1)S(1)}, bf16[1024,1024]{1,0:T(8,128)(2,1)}, u32[]{:S(2)}) copy-start(bf16[1024,1024]{1,0:T(8,128)(2,1)} %refs_1_.7) | copy-start | bytes 6291460
  20.5 1.0 copy-start.3
  22.5 2.2 %copy-start.2 = (bf16[512,4096]{1,0:T(8,128)(2,1)S(1)}, bf16[512,4096]{1,0:T(8,128)(2,1)}, u32[]{:S(2)}) copy-start(bf16[512,4096]{1,0:T(8,128)(2,1)} %refs_0_.6) | copy-start | bytes 12582916
  24.7 1.0 copy-start.4
  30.0 3.2 %collective-permute-start.4 = (bf16[8,128,128]{2,1,0:T(8,128)(2,1)S(1)}, bf16[8,128,128]{2,1,0:T(8,128)(2,1)S(1)}, u32[]{:S(2)}, u32[]{:S(2)}) collective-permute-start(bf16[8,128,128]{2,1,0:T(8,128)(2,1)S(1)} %get-tuple-element.35.refs_0_), channel_id=1, source_target_pairs={{0,1},{1,0},{2,3},{3,2},{4,5},{5,4},{6,7},{7,6},{8,9},{9,8},{10,11... | collective-permute-start | bytes 786440 | tf_op jit(solution)/shard_map/ppermute | solution.py:34
  31.4 15.6 %collective-permute-start.11 = (bf16[128,1024]{1,0:T(8,128)(2,1)S(1)}, bf16[128,1024]{1,0:T(8,128)(2,1)S(1)}, u32[]{:S(2)}, u32[]{:S(2)}) collective-permute-start(bf16[128,1024]{1,0:T(8,128)(2,1)S(1)} %get-tuple-element.51), channel_id=1, source_target_pairs={{0,1},{1,0},{2,3},{3,2},{4,5},{5,4},{6,7},{7,6},{8,9},{9,8},{10,11... | collective-permute-start | bytes 786440 | tf_op jit(solution)/shard_map/ppermute | solution.py:34
  31.6 22.1 %copy-start.6 = (s32[64,4]{1,0:T(8,128)}, s32[64,4]{1,0:T(8,128)S(1)}, u32[]{:S(2)}) copy-start(s32[64,4]{1,0:T(8,128)S(1)} %copy.17.refs_0_.refs_3_) | copy-start | bytes 3076
  31.6 7.6 %collective-permute-start.5 = (bf16[4,128,256]{2,1,0:T(8,128)(2,1)S(1)}, bf16[4,128,256]{2,1,0:T(8,128)(2,1)S(1)}, u32[]{:S(2)}, u32[]{:S(2)}) collective-permute-start(bf16[4,128,256]{2,1,0:T(8,128)(2,1)S(1)} %get-tuple-element.36.refs_2_.refs_4_), channel_id=1, source_target_pairs={{0,16},{1,17},{2,18},{3,19},{4,20},{5,21},{6,22},{7,23},{8,24},{9,... | collective-permute-start | bytes 786440 | tf_op jit(solution)/shard_map/ppermute | solution.py:34
  31.9 8.4 %collective-permute-start.6 = (bf16[4,128,256]{2,1,0:T(8,128)(2,1)S(1)}, bf16[4,128,256]{2,1,0:T(8,128)(2,1)S(1)}, u32[]{:S(2)}, u32[]{:S(2)}) collective-permute-start(bf16[4,128,256]{2,1,0:T(8,128)(2,1)S(1)} %get-tuple-element.37.refs_3_.refs_5_), channel_id=1, source_target_pairs={{0,48},{1,49},{2,50},{3,51},{4,52},{5,53},{6,54},{7,55},{8,56},{9,... | collective-permute-start | bytes 786440 | tf_op jit(solution)/shard_map/ppermute | solution.py:34
  36.0 19.6 %collective-permute-start.12 = (bf16[512,256]{1,0:T(8,128)(2,1)S(1)}, bf16[512,256]{1,0:T(8,128)(2,1)S(1)}, u32[]{:S(2)}, u32[]{:S(2)}) collective-permute-start(bf16[512,256]{1,0:T(8,128)(2,1)S(1)} %get-tuple-element.52.refs_0_), channel_id=1, source_target_pairs={{0,4},{1,5},{2,6},{3,7},{4,8},{5,9},{6,10},{7,11},{8,12},{9,13},{1... | collective-permute-start | bytes 786440 | tf_op jit(solution)/shard_map/ppermute | solution.py:34
  36.1 19.5 %collective-permute-start.13 = (bf16[512,256]{1,0:T(8,128)(2,1)S(1)}, bf16[512,256]{1,0:T(8,128)(2,1)S(1)}, u32[]{:S(2)}, u32[]{:S(2)}) collective-permute-start(bf16[512,256]{1,0:T(8,128)(2,1)S(1)} %get-tuple-element.52.refs_0_), channel_id=1, source_target_pairs={{0,8},{1,9},{2,10},{3,11},{4,12},{5,13},{6,14},{7,15},{8,0},{9,1},... | collective-permute-start | bytes 786440 | tf_op jit(solution)/shard_map/ppermute | solution.py:34
  40.3 8.7 %collective-permute-start.10 = (bf16[4,128,256]{2,1,0:T(8,128)(2,1)S(1)}, bf16[4,128,256]{2,1,0:T(8,128)(2,1)S(1)}, u32[]{:S(2)}, u32[]{:S(2)}) collective-permute-start(bf16[4,128,256]{2,1,0:T(8,128)(2,1)S(1)} %get-tuple-element.44), channel_id=1, source_target_pairs={{0,48},{1,49},{2,50},{3,51},{4,52},{5,53},{6,54},{7,55},{8,56},{9,... | collective-permute-start | bytes 786440 | tf_op jit(solution)/shard_map/ppermute | solution.py:34
  40.4 8.6 %collective-permute-start.9 = (bf16[4,128,256]{2,1,0:T(8,128)(2,1)S(1)}, bf16[4,128,256]{2,1,0:T(8,128)(2,1)S(1)}, u32[]{:S(2)}, u32[]{:S(2)}) collective-permute-start(bf16[4,128,256]{2,1,0:T(8,128)(2,1)S(1)} %get-tuple-element.41.refs_9_), channel_id=1, source_target_pairs={{0,16},{1,17},{2,18},{3,19},{4,20},{5,21},{6,22},{7,23},{8,24},{9,... | collective-permute-start | bytes 786440 | tf_op jit(solution)/shard_map/ppermute | solution.py:34
  43.0 10.7 %slice-start = ((s8[8388608]{0:T(1024)(128)(4,1)}), s8[4194304]{0:T(1024)(128)(4,1)S(1)}, s32[]{:S(2)}) async-start(s8[8388608]{0:T(1024)(128)(4,1)} %bitcast.1), calls=%async_computation.2 | async-start | bytes 8388608
  47.0 8.5 %collective-permute-start.14 = (bf16[512,256]{1,0:T(8,128)(2,1)S(1)}, bf16[512,256]{1,0:T(8,128)(2,1)S(1)}, u32[]{:S(2)}, u32[]{:S(2)}) collective-permute-start(bf16[512,256]{1,0:T(8,128)(2,1)S(1)} %get-tuple-element.52.refs_0_), channel_id=1, source_target_pairs={{0,12},{1,13},{2,14},{3,15},{4,0},{5,1},{6,2},{7,3},{8,4},{9,5},{1... | collective-permute-start | bytes 786440 | tf_op jit(solution)/shard_map/ppermute | solution.py:34
  49.0 6.0 %collective-permute-start.7 = (bf16[4,128,256]{2,1,0:T(8,128)(2,1)S(1)}, bf16[4,128,256]{2,1,0:T(8,128)(2,1)S(1)}, u32[]{:S(2)}, u32[]{:S(2)}) collective-permute-start(bf16[4,128,256]{2,1,0:T(8,128)(2,1)S(1)} %get-tuple-element.42), channel_id=1, source_target_pairs={{0,16},{1,17},{2,18},{3,19},{4,20},{5,21},{6,22},{7,23},{8,24},{9,... | collective-permute-start | bytes 786440 | tf_op jit(solution)/shard_map/ppermute | solution.py:34
  49.0 4.7 %slice-start.1 = ((s8[8388608]{0:T(1024)(128)(4,1)}), s8[4194304]{0:T(1024)(128)(4,1)S(1)}, s32[]{:S(2)}) async-start(s8[8388608]{0:T(1024)(128)(4,1)} %bitcast.1), calls=%async_computation.3 | async-start | bytes 8388608
  49.0 6.5 %collective-permute-start.8 = (bf16[4,128,256]{2,1,0:T(8,128)(2,1)S(1)}, bf16[4,128,256]{2,1,0:T(8,128)(2,1)S(1)}, u32[]{:S(2)}, u32[]{:S(2)}) collective-permute-start(bf16[4,128,256]{2,1,0:T(8,128)(2,1)S(1)} %get-tuple-element.43), channel_id=1, source_target_pairs={{0,48},{1,49},{2,50},{3,51},{4,52},{5,53},{6,54},{7,55},{8,56},{9,... | collective-permute-start | bytes 786440 | tf_op jit(solution)/shard_map/ppermute | solution.py:34
  55.0 21.3 %copy-start.5 = (bf16[3,64,1024]{2,1,0:T(8,128)(2,1)}, bf16[3,64,1024]{2,1,0:T(8,128)(2,1)S(1)}, u32[]{:S(2)}) copy-start(bf16[3,64,1024]{2,1,0:T(8,128)(2,1)S(1)} %shard_map.112.refs_7_.refs_2_) | copy-start | bytes 1179652
  59.4 4.9 %collective-permute-start.15 = (bf16[160,1024]{1,0:T(8,128)(2,1)S(1)}, bf16[160,1024]{1,0:T(8,128)(2,1)S(1)}, u32[]{:S(2)}, u32[]{:S(2)}) collective-permute-start(bf16[160,1024]{1,0:T(8,128)(2,1)S(1)} %get-tuple-element.54), channel_id=1, source_target_pairs={{0,1},{1,0},{2,3},{3,2},{4,5},{5,4},{6,7},{7,6},{8,9},{9,8},{10,11... | collective-permute-start | bytes 983048 | tf_op jit(solution)/shard_map/ppermute | solution.py:34
  64.4 11.3 %collective-permute-start.16 = (bf16[4,512,256]{2,1,0:T(8,128)(2,1)S(1)}, bf16[4,512,256]{2,1,0:T(8,128)(2,1)S(1)}, u32[]{:S(2)}, u32[]{:S(2)}) collective-permute-start(bf16[4,512,256]{2,1,0:T(8,128)(2,1)S(1)} %shard_map.115.refs_1_), channel_id=1, source_target_pairs={{0,1},{1,0},{2,3},{3,2},{4,5},{5,4},{6,7},{7,6},{8,9},{9,8},{10,11... | collective-permute-start | bytes 3145736 | tf_op jit(solution)/shard_map/ppermute | solution.py:34
  76.3 0.7 copy-start.7
  77.0 3.8 %collective-permute-start.17 = (bf16[64,1024]{1,0:T(8,128)(2,1)S(1)}, bf16[64,1024]{1,0:T(8,128)(2,1)S(1)}, u32[]{:S(2)}, u32[]{:S(2)}) collective-permute-start(bf16[64,1024]{1,0:T(8,128)(2,1)S(1)} %get-tuple-element.57), channel_id=1, source_target_pairs={{0,2},{1,3},{2,0},{3,1},{4,6},{5,7},{6,4},{7,5},{8,10},{9,11},{10,... | collective-permute-start | bytes 393224 | tf_op jit(solution)/shard_map/ppermute | solution.py:34
  80.8 0.7 copy-start.9
  81.5 25.8 %copy-start.1 = (bf16[1024,1024]{1,0:T(8,128)(2,1)S(1)}, bf16[1024,1024]{1,0:T(8,128)(2,1)}, u32[]{:S(2)}) copy-start(bf16[1024,1024]{1,0:T(8,128)(2,1)} %refs_1_.7) | copy-start | bytes 6291460
